TPU v7x, 256 devices: a whole 4x4x8 slice. The times are simulated.
256 devices in a mesh: inst: 32 (over z, x), tp: 8 (over y, core).
Axes of the slice: x: 4, y: 4, z: 8, core: 2. Of those that a mesh axis runs over, the one named last changes fastest.
Arguments:
- queries: bfloat16 [256, 2, 64, 128], P('inst', None, 'tp'), may hold values from -100 to 100
- new_keys: bfloat16 [256, 2, 8, 128], P('inst', None, 'tp'), may hold values from -8 to 8
- new_values: bfloat16 [256, 2, 8, 128], P('inst', None, 'tp'), may hold values from -6 to 6
- key_pool: bfloat16 [2048, 8, 128, 128], P('inst', 'tp'), may hold values from -8 to 8
- value_pool: bfloat16 [2048, 8, 128, 128], P('inst', 'tp'), may hold values from -6 to 6
- block_table: int32 [256, 8], P('inst'), may hold values from 0 to 63
- lengths: int32 [256], P('inst'), may hold values from 1 to 1024, 131072 in all
- lend_entry: int32 [1024], P('inst'), may hold values from 0 to 63, as said below
- lend_target: int32 [1024, 1], P('inst'), may hold values from 0 to 31; in each aligned block of 32 rows (0 to 31, 32 to 63, ...) at most 2 rows name the same one
- out_weight: bfloat16 [8192, 4096], P('tp'), may hold values from -0.0625 to 0.0625
Outputs:
- projected: bfloat16 [256, 2, 4096], P('inst', None, 'tp')
Inputs may be any that keep to these rules, and one draw needn't show every extreme that they name: `lend_entry`: each of an instance's 32 entries is distinct. `lend_target`: among the 32 rows of one instance no creditor is named more than 2 times, and some instance names one creditor exactly 2 times; a creditor may be the instance itself. `block_table`: slots may be shared by several entries. The lengths sum to 131072 and the largest is exactly 1024.
All inputs are finite; a program needn't handle non-finite values. No bound on the sum of `lengths` on one device may be relied on, other than what follows from the above.
Results may differ from a plain program's by a relative error of at most 0.019.
Values may be sent and summed in bfloat16 or wider, within the bound.
No kernel may reach another device: no remote copies, remote signals or barrier semaphores. Data moves between devices by JAX's collectives and lax.ppermute only.
A program may use at most 64 MiB of HBM per device.

v0:
```python
import jax
import jax.numpy as jnp
from jax import lax
from jax.sharding import PartitionSpec as P

MASKED_SCORE = -1e30


def block_state(query_rows, key_blocks, value_blocks, live_mask, scale_factor):
    scores = (
        jnp.einsum("nhgd,nbhtd->nhgbt", query_rows, key_blocks, preferred_element_type=jnp.float32)
        * scale_factor
    )
    live_full = live_mask[:, None, None, :, :]
    masked = jnp.where(live_full, scores, MASKED_SCORE)
    peak_score = jnp.max(masked, axis=(3, 4))
    weights = jnp.where(live_full, jnp.exp(masked - peak_score[..., None, None]), 0.0)
    weight_sum = jnp.sum(weights, axis=(3, 4))
    value_sum = jnp.einsum(
        "nhgbt,nbhtd->nhgd",
        weights,
        value_blocks,
        preferred_element_type=jnp.float32,
        precision=lax.Precision.HIGHEST,
    )
    return (peak_score, weight_sum, value_sum)


def combine_states(first_state, second_state):
    peak_score = jnp.maximum(first_state[0], second_state[0])
    first_scale = jnp.exp(first_state[0] - peak_score)
    second_scale = jnp.exp(second_state[0] - peak_score)
    weight_sum = first_state[1] * first_scale + second_state[1] * second_scale
    value_sum = first_state[2] * first_scale[..., None] + second_state[2] * second_scale[..., None]
    return (peak_score, weight_sum, value_sum)


def on_device(
    queries,
    new_keys,
    new_values,
    key_pool,
    value_pool,
    block_table,
    lengths,
    lend_entry,
    lend_target,
    out_weight,
):
    req_count, step_count, head_count, head_size = queries.shape
    local_kv = new_keys.shape[2]
    group_size = head_count // local_kv
    block_len = key_pool.shape[2]
    block_shape = key_pool.shape[1:]
    max_blocks = block_table.shape[1]
    lend_count = lend_entry.shape[0]
    instances = lax.axis_size("inst")
    capacity = max(2, 2 * lend_count // instances)
    scale_factor = head_size ** (-0.5)
    targets = lend_target[:, 0]
    order_index = jnp.arange(lend_count)
    before = order_index[:, None] > order_index[None, :]
    same_target = targets[:, None] == targets[None, :]
    rank_within = jnp.sum(jnp.logical_and(before, same_target), axis=1)
    slot_index = targets * capacity + rank_within
    lent_request = lend_entry // max_blocks
    lent_block = lend_entry % max_blocks
    lent_slot = block_table[lent_request, lent_block]
    positions = jnp.arange(max_blocks * block_len, dtype=jnp.int32).reshape(max_blocks, block_len)
    live_cached = positions[None] < lengths[:, None, None]
    home_keys = key_pool[block_table]
    home_values = value_pool[block_table]
    fresh_keys = jnp.transpose(new_keys, (0, 2, 1, 3))[:, None]
    fresh_values = jnp.transpose(new_values, (0, 2, 1, 3))[:, None]
    query_rows = queries.reshape(req_count, step_count, local_kv, group_size, head_size)
    step_range = jnp.arange(step_count)
    outputs = []
    wanted = (
        jnp.zeros((instances * capacity,), jnp.int32)
        .at[slot_index]
        .set(lent_slot)
        .reshape(instances, capacity)
    )
    served = lax.all_to_all(wanted, "inst", split_axis=0, concat_axis=0, tiled=True).reshape(-1)
    pulled = (
        lax.all_to_all(
            key_pool[served].reshape((instances, capacity) + block_shape),
            "inst",
            split_axis=0,
            concat_axis=0,
            tiled=True,
        ),
        lax.all_to_all(
            value_pool[served].reshape((instances, capacity) + block_shape),
            "inst",
            split_axis=0,
            concat_axis=0,
            tiled=True,
        ),
    )
    pulled_keys = pulled[0].reshape((instances * capacity,) + block_shape)[slot_index]
    pulled_values = pulled[1].reshape((instances * capacity,) + block_shape)[slot_index]
    all_keys = (
        home_keys.reshape((req_count * max_blocks,) + block_shape)
        .at[lend_entry]
        .set(pulled_keys)
        .reshape(home_keys.shape)
    )
    all_values = (
        home_values.reshape((req_count * max_blocks,) + block_shape)
        .at[lend_entry]
        .set(pulled_values)
        .reshape(home_values.shape)
    )
    for step_index in range(step_count):
        fresh_mask = jnp.broadcast_to(
            (step_range <= step_index)[None, None, :], (req_count, 1, step_count)
        )
        state = combine_states(
            block_state(query_rows[:, step_index], all_keys, all_values, live_cached, scale_factor),
            block_state(
                query_rows[:, step_index], fresh_keys, fresh_values, fresh_mask, scale_factor
            ),
        )
        attention = state[2] / state[1][..., None]
        outputs.append(attention.reshape(req_count, head_count * head_size).astype(jnp.bfloat16))
    stacked = jnp.stack(outputs, axis=1)
    partial_out = jnp.einsum("rsf,fo->rso", stacked, out_weight, preferred_element_type=jnp.float32)
    return lax.psum_scatter(partial_out.astype(jnp.bfloat16), "tp", scatter_dimension=2, tiled=True)


def solution(mesh):
    placed = (
        P("inst", None, "tp", None),
        P("inst", None, "tp", None),
        P("inst", None, "tp", None),
        P("inst", "tp", None, None),
        P("inst", "tp", None, None),
        P("inst", None),
        P("inst"),
        P("inst"),
        P("inst", None),
        P("tp", None),
    )
    return jax.shard_map(
        on_device, mesh=mesh, in_specs=placed, out_specs=P("inst", None, "tp"), check_vma=False
    )
```

profile of v0, /device:TPU:1, one launch (start us, length us, event | category | flops | bytes accessed | tf_op | source)
XLA Modules:
  0.0 200.4 jit_solution(12710370678166811333)
XLA Ops:
  6.5 0.8 fusion.50
  7.4 0.9 convert_reduce_fusion
  8.3 0.7 fusion.47
  8.9 1.4 gather_fusion.1
  10.4 0.7 scatter_custom_fusion
  11.1 20.2 %all_to_all.19 = s32[32,1,2]{2,1,0:T(1,128)S(1)} all-to-all(s32[32,1,2]{2,1,0:T(1,128)S(1)} %bitcast.98), channel_id=1, replica_groups=mesh['inst'=32,'tp'=8] {'inst'}, dimensions={0} | all-to-all | bytes 512 | tf_op jit(solution)/shard_map/all_to_all | solution.py:84
  31.4 0.5 broadcast.229
  31.9 0.7 reduce.19
  32.7 2.1 %gather_fusion.2 = bf16[64,128,128]{2,1,0:T(8,128)(2,1)} fusion(bf16[64,128,128]{2,1,0:T(8,128)(2,1)S(1)} %bitcast.85, s32[1024]{0:T(1024)S(1)} %pad_clamp_fusion.1), kind=kCustom, calls=%fused_computation.2 | custom fusion | bytes 4194560 | tf_op jit(solution)/shard_map/gather | solution.py:87
  34.8 4.8 %all-to-all-start.1 = ((bf16[32,2,1,128,128]{4,3,1,2,0:T(8,128)(2,1)}), bf16[32,2,1,128,128]{4,3,1,2,0:T(8,128)(2,1)}, u32[]{:S(2)}, u32[]{:S(2)}) async-start(bf16[32,2,1,128,128]{4,3,1,2,0:T(8,128)(2,1)} %bitcast.93), calls=%async_computation.1 | async-start | bytes 4194304 | tf_op jit(solution)/shard_map/all_to_all | solution.py:86
  39.6 3.8 %gather_fusion.5 = bf16[64,128,128]{2,1,0:T(8,128)(2,1)} fusion(bf16[64,128,128]{2,1,0:T(8,128)(2,1)} %bitcast.90, s32[1024]{0:T(1024)S(1)} %pad_clamp_fusion.1), kind=kCustom, calls=%fused_computation.5 | custom fusion | bytes 4194560 | tf_op jit(solution)/shard_map/gather | solution.py:94
  43.4 43.1 %all-to-all-done.1 = bf16[32,2,1,128,128]{4,3,1,2,0:T(8,128)(2,1)} async-done(((bf16[32,2,1,128,128]{4,3,1,2,0:T(8,128)(2,1)}), bf16[32,2,1,128,128]{4,3,1,2,0:T(8,128)(2,1)}, u32[]{:S(2)}, u32[]{:S(2)}) %all-to-all-start.1) | async-done | bytes 2097184 | tf_op jit(solution)/shard_map/all_to_all | solution.py:86
  86.5 7.6 %all-to-all-start.2 = ((bf16[32,2,1,128,128]{4,3,1,2,0:T(8,128)(2,1)}), bf16[32,2,1,128,128]{4,3,1,2,0:T(8,128)(2,1)}, u32[]{:S(2)}, u32[]{:S(2)}) async-start(bf16[32,2,1,128,128]{4,3,1,2,0:T(8,128)(2,1)} %bitcast.92), calls=%async_computation.2 | async-start | bytes 4194304 | tf_op jit(solution)/shard_map/all_to_all | solution.py:93
  94.2 2.2 %gather_fusion = bf16[64,128,128]{2,1,0:T(8,128)(2,1)} fusion(bf16[64,128,128]{2,1,0:T(8,128)(2,1)S(1)} %bitcast.84, s32[1024]{0:T(1024)S(1)} %pad_clamp_fusion.2), kind=kCustom, calls=%fused_computation | custom fusion | bytes 4194560 | tf_op jit(solution)/shard_map/gather | solution.py:71
  96.4 3.7 %gather_fusion.4 = bf16[64,128,128]{2,1,0:T(8,128)(2,1)} fusion(bf16[64,128,128]{2,1,0:T(8,128)(2,1)} %bitcast.91, s32[1024]{0:T(1024)S(1)} %pad_clamp_fusion.2), kind=kCustom, calls=%fused_computation.4 | custom fusion | bytes 4194560 | tf_op jit(solution)/shard_map/gather | solution.py:72
  100.2 0.1 fusion.66
  100.4 0.1 fusion.68
  100.7 2.3 %gather_fusion.3 = bf16[32,128,128]{2,1,0:T(8,128)(2,1)S(1)} fusion(bf16[64,128,128]{2,1,0:T(8,128)(2,1)} %bitcast.7, s32[1024]{0:T(1024)S(1)} %pad_clamp_fusion), kind=kCustom, calls=%fused_computation.3 | custom fusion | bytes 2097280 | tf_op jit(solution)/shard_map/gather | solution.py:101
  103.1 4.6 %scatter_fusion = bf16[64,128,128]{2,1,0:T(8,128)(2,1)} fusion(bf16[64,128,128]{2,1,0:T(8,128)(2,1)} %gather_fusion, s32[32]{0:T(128)S(1)} %get-tuple-element.14, bf16[32,128,128]{2,1,0:T(8,128)(2,1)S(1)} %gather_fusion.3), kind=kCustom, calls=%fused_computation.8 | custom fusion | bytes 3145856 | tf_op jit(solution)/shard_map/scatter | solution.py:106
  107.7 2.5 %fusion.65 = (f32[8,8]{1,0:T(8,128)S(1)}, f32[8,8,8,128]{3,1,2,0:T(8,128)S(1)}) fusion(bf16[8,8,128,128]{3,2,1,0:T(8,128)(2,1)} %bitcast.88, bf16[8,2,1,8,128]{4,3,0,2,1:T(8,128)(2,1)S(1)} %bitcast.96, pred[8,8,128]{2,1,0:T(8,128)(4,1)S(1)} %broadcast_compare_fusion), kind=kOutput, calls=%fused_computation.109 | convolution fusion | flops 16973760 | bytes 2384128 | tf_op jit(solution)/shard_map/nhgd,nbhtd->nhgbt/dot_general | solution.py:11
  110.2 1.4 fusion.67
  111.5 28.3 %all-to-all-done.2 = bf16[32,2,1,128,128]{4,3,1,2,0:T(8,128)(2,1)} async-done(((bf16[32,2,1,128,128]{4,3,1,2,0:T(8,128)(2,1)}), bf16[32,2,1,128,128]{4,3,1,2,0:T(8,128)(2,1)}, u32[]{:S(2)}, u32[]{:S(2)}) %all-to-all-start.2) | async-done | bytes 2097184 | tf_op jit(solution)/shard_map/all_to_all | solution.py:93
  139.9 2.3 %gather_fusion.6 = bf16[32,128,128]{2,1,0:T(8,128)(2,1)S(1)} fusion(bf16[64,128,128]{2,1,0:T(8,128)(2,1)} %bitcast.16, s32[1024]{0:T(1024)S(1)} %pad_clamp_fusion), kind=kCustom, calls=%fused_computation.6 | custom fusion | bytes 2097280 | tf_op jit(solution)/shard_map/gather | solution.py:102
  142.2 1.2 fusion.19
  143.5 4.6 %scatter_fusion.1 = bf16[64,128,128]{2,1,0:T(8,128)(2,1)} fusion(bf16[64,128,128]{2,1,0:T(8,128)(2,1)} %gather_fusion.4, s32[32]{0:T(128)S(1)} %get-tuple-element.14, bf16[32,128,128]{2,1,0:T(8,128)(2,1)S(1)} %gather_fusion.6), kind=kCustom, calls=%fused_computation.9 | custom fusion | bytes 3145856 | tf_op jit(solution)/shard_map/scatter | solution.py:112
  148.1 2.7 %fusion.14 = f32[8,8,128]{2,1,0:T(8,128)S(1)} fusion(bf16[8,8,128,128]{3,2,1,0:T(8,128)(2,1)} %bitcast.86, f32[8,8,8,128]{3,1,2,0:T(8,128)} %get-tuple-element.20, f32[8,8]{1,0:T(8,128)S(1)} %get-tuple-element.19, pred[8,8,128]{2,1,0:T(8,128)(4,1)S(1)} %broadcast_compare_fusion, f32[8,8]{1,0:T(8,128)S(1)} %get-tuple-element.9), kind=kOutput, calls=%fused_computation.28 | convolution fusion | flops 100802560 | bytes 2400768 | tf_op jit(solution)/shard_map/nhgbt,nbhtd->nhgd/dot_general | solution.py:19
  150.8 0.3 fusion.15
  151.1 2.6 %fusion.13 = f32[8,8,128]{2,1,0:T(8,128)S(1)} fusion(bf16[8,8,128,128]{3,2,1,0:T(8,128)(2,1)} %bitcast.87, f32[8,8,8,128]{3,1,2,0:T(8,128)S(1)} %get-tuple-element.16, f32[8,8]{1,0:T(8,128)S(1)} %get-tuple-element.15, pred[8,8,128]{2,1,0:T(8,128)(4,1)S(1)} %broadcast_compare_fusion, f32[8,8]{1,0:T(8,128)S(1)} %get-tuple-element.12), kind=kOutput, calls=%fused_computation.26 | convolution fusion | flops 100802560 | bytes 2400768 | tf_op jit(solution)/shard_map/nhgbt,nbhtd->nhgd/dot_general | solution.py:19
  153.7 0.3 fusion.16
  154.0 5.2 %fusion.2 = bf16[8,2,4096]{2,0,1:T(8,128)(2,1)} fusion(bf16[1024,4096]{1,0:T(8,128)(2,1)} %param.19, bf16[8,1,1024]{2,0,1:T(8,128)(2,1)S(1)} %convert_element_type.36, bf16[8,1,1024]{2,0,1:T(8,128)(2,1)S(1)} %convert_element_type.34), kind=kOutput, calls=%fused_computation.12 | convolution fusion | flops 134299648 | bytes 8552448 | tf_op jit(solution)/shard_map/rsf,fo->rso/dot_general | solution.py:128
  159.3 32.9 %reduce-scatter.2.cloned.1.call-done = bf16[8,2,512]{2,0,1:T(8,128)(2,1)} async-done(((bf16[8,2,4096]{2,0,1:T(8,128)(2,1)}), bf16[8,2,512]{2,0,1:T(8,128)(2,1)}) %reduce-scatter.2.cloned.1.call-update) | async-done | bytes 16400 | tf_op jit(solution)/shard_map/reduce_scatter | solution.py:129
  192.2 1.3 copy.20
  (34 shorter events, 0.6 us)
Async XLA Ops:
  6.5 26.2 %copy-start = (bf16[64,1,128,128]{3,2,1,0:T(8,128)(2,1)S(1)}, bf16[64,1,128,128]{3,2,1,0:T(8,128)(2,1)}, u32[]{:S(2)}) copy-start(bf16[64,1,128,128]{3,2,1,0:T(8,128)(2,1)} %param.13) | copy-start | bytes 6291460
  34.8 51.6 %all-to-all-start.1 = ((bf16[32,2,1,128,128]{4,3,1,2,0:T(8,128)(2,1)}), bf16[32,2,1,128,128]{4,3,1,2,0:T(8,128)(2,1)}, u32[]{:S(2)}, u32[]{:S(2)}) async-start(bf16[32,2,1,128,128]{4,3,1,2,0:T(8,128)(2,1)} %bitcast.93), calls=%async_computation.1 | async-start | bytes 4194304 | tf_op jit(solution)/shard_map/all_to_all | solution.py:86
  86.5 7.7 %copy-start.1 = (s32[8,8]{1,0:T(8,128)S(1)}, s32[8,8]{1,0:T(8,128)}, u32[]{:S(2)}) copy-start(s32[8,8]{1,0:T(8,128)} %param.15) | copy-start | bytes 772
  86.5 53.4 %all-to-all-start.2 = ((bf16[32,2,1,128,128]{4,3,1,2,0:T(8,128)(2,1)}), bf16[32,2,1,128,128]{4,3,1,2,0:T(8,128)(2,1)}, u32[]{:S(2)}, u32[]{:S(2)}) async-start(bf16[32,2,1,128,128]{4,3,1,2,0:T(8,128)(2,1)} %bitcast.92), calls=%async_computation.2 | async-start | bytes 4194304 | tf_op jit(solution)/shard_map/all_to_all | solution.py:93
  94.1 98.1 %reduce-scatter.2.cloned.1.call-start = ((), (), s32[]{:S(2)}) async-start(), calls=%async_computation.4 | async-start | bytes 147456 | tf_op jit(solution)/shard_map/reduce_scatter | solution.py:129
  96.4 3.8 %copy-start.3 = (bf16[8,2,8,128]{3,2,1,0:T(8,128)(2,1)S(1)}, bf16[8,2,8,128]{3,2,1,0:T(8,128)(2,1)}, u32[]{:S(2)}) copy-start(bf16[8,2,8,128]{3,2,1,0:T(8,128)(2,1)} %param.10) | copy-start | bytes 98308
  96.4 3.8 %copy-start.5 = (bf16[8,2,1,128]{3,1,2,0:T(2,128)(2,1)S(1)}, bf16[8,2,1,128]{3,1,2,0:T(2,128)(2,1)}, u32[]{:S(2)}) copy-start(bf16[8,2,1,128]{3,1,2,0:T(2,128)(2,1)} %param.11) | copy-start | bytes 12292
  96.4 4.2 %copy-start.4 = (s32[8]{0:T(128)S(1)}, s32[8]{0:T(128)}, u32[]{:S(2)}) copy-start(s32[8]{0:T(128)} %param.16) | copy-start | bytes 100
  107.7 2.5 %copy-start.2 = (bf16[64,128,128]{2,1,0:T(8,128)(2,1)S(1)}, bf16[64,128,128]{2,1,0:T(8,128)(2,1)}, u32[]{:S(2)}) copy-start(bf16[64,128,128]{2,1,0:T(8,128)(2,1)} %scatter_fusion) | copy-start | bytes 6291460
  143.5 7.3 %copy-start.6 = (bf16[8,2,1,128]{3,1,2,0:T(2,128)(2,1)S(1)}, bf16[8,2,1,128]{3,1,2,0:T(2,128)(2,1)}, u32[]{:S(2)}) copy-start(bf16[8,2,1,128]{3,1,2,0:T(2,128)(2,1)} %param.12) | copy-start | bytes 12292
Sparse Core Ops, SparseCore 0:
  159.4 32.7 reduce-scatter.1
where the time goes:
time: 203 us; the launch traced here: 200 us
  waiting for transfers between devices  104 us (51%)
  local copies, waits for them, and re-layouts  30 us (15%)
  blocking collectives  20.2 us (10%)
  matrix products  15.2 us (7%)
  between operations  13.6 us (7%)
  starting transfers between devices  12.4 us (6%)
  other arithmetic  4.53 us (2%)
    all_to_all x1, waiting for transfers between devices, on_device(): lax.all_to_all(key_pool[served].reshape((instances, capacity) + block_sha...  43.1 us
    reduce_scatter x1, waiting for transfers between devices, on_device(): lax.psum_scatter(partial_out.astype(jnp.bfloat16), 'tp', scatter_dimensio...  32.9 us
    all_to_all x1, waiting for transfers between devices, on_device(): lax.all_to_all(value_pool[served].reshape((instances, capacity) + block_s...  28.3 us
    all_to_all x1, blocking collectives, on_device(): lax.all_to_all(wanted, 'inst', split_axis=0, concat_axis=0, tiled=True)  20.2 us
    all_to_all x1, starting transfers between devices, on_device(): lax.all_to_all(value_pool[served].reshape((instances, capacity) + block_s...  7.59 us
    dot_general x4, matrix products, block_state(): jnp.einsum('nhgbt,nbhtd->nhgd', weights, value_blocks, preferred_element_...  5.86 us
    dot_general x1, matrix products, on_device(): jnp.einsum('rsf,fo->rso', stacked, out_weight, preferred_element_type=jnp...  5.22 us
    all_to_all x1, starting transfers between devices, on_device(): lax.all_to_all(key_pool[served].reshape((instances, capacity) + block_sha...  4.76 us
  transfers between devices with their start and end apart: 3, of which 3 were waited for; matrix products, arithmetic and copies ran while one was open for 11% of the time, Pallas kernels for 0%

commit v1 on v0

v1 whole, which is shorter than its diff:
```python
import functools

import jax
import jax.numpy as jnp
from jax import lax
from jax.experimental import pallas as pl
from jax.experimental.pallas import tpu as pltpu
from jax.sharding import PartitionSpec as P

DEAD = -1e30
CAP = 2
GROUP = 8
ROWS = 16
SLAB = 48
BF = jnp.bfloat16
F32 = jnp.float32
VM = pl.BlockSpec(memory_space=pltpu.VMEM)
SM = pl.BlockSpec(memory_space=pltpu.SMEM)


def lane_iota():
    return lax.broadcasted_iota(jnp.int32, (ROWS, 128), 1)


def pack_kernel(entry, target, table, lengths, q, send, count, slots, lives):
    peers = send.shape[0]
    blocks = table.shape[1]

    def clear(i, _):
        count[i] = 0
        for c in range(CAP):
            slots[i * CAP + c] = 0
            lives[i * CAP + c] = 0
        return 0

    lax.fori_loop(0, peers, clear, 0)

    def place(j, _):
        e = entry[j]
        t = target[j, 0]
        r = e // blocks
        b = e % blocks
        rank = count[t]
        count[t] = rank + 1
        live = jnp.clip(lengths[r] - b * 128, 0, 128)
        slots[t * CAP + rank] = table[r, b]
        lives[t * CAP + rank] = live
        send[t, pl.ds(pl.multiple_of(rank * ROWS, ROWS), ROWS), :] = q[r]
        return 0

    lax.fori_loop(0, entry.shape[0], place, 0)
    lane = lane_iota()

    def side(i, _):
        v = jnp.where(lane == 0, slots[i * CAP], 0)
        v = jnp.where(lane == 1, lives[i * CAP], v)
        v = jnp.where(lane == 2, slots[i * CAP + 1], v)
        v = jnp.where(lane == 3, lives[i * CAP + 1], v)
        send[i, CAP * ROWS :, :] = v.astype(F32).astype(BF)
        return 0

    lax.fori_loop(0, peers, side, 0)


def block_partial(q, k, v, live, scale):
    s = lax.dot_general(q, k, (((1,), (1,)), ((), ())), preferred_element_type=F32) * scale
    s = jnp.where(lane_iota() < live, s, DEAD)
    m = jnp.max(s, axis=1, keepdims=True)
    p = jnp.exp(s - m)
    l = jnp.sum(p, axis=1, keepdims=True)
    o = jnp.dot(p.astype(BF), v, preferred_element_type=F32) / l
    return o, m + jnp.log(l)


def serve_kernel(recv, kp, vp, back, side_f, side_i, side_s, ids, lse, sem):
    peers = recv.shape[0]
    scale = 128**-0.5
    side_f[...] = recv[:, CAP * ROWS :, :].astype(F32).reshape(peers * ROWS, 128)
    side_i[...] = side_f[pl.ds(0, peers, stride=ROWS), :].astype(jnp.int32)
    copy = pltpu.make_async_copy(side_i, side_s, sem)
    copy.start()
    back[...] = jnp.zeros(back.shape, BF)
    lse[...] = jnp.full(lse.shape, DEAD, F32)
    copy.wait()

    def listing(i, n):
        for c in range(CAP):
            ids[n] = i * CAP + c
            n = n + jnp.where(side_s[i, 2 * c + 1] > 0, 1, 0)
        return n

    n = lax.fori_loop(0, peers, listing, 0)
    last = jnp.maximum(n - 1, 0)

    def work(g, _):
        todo = []
        for i in range(GROUP):
            item = ids[jnp.minimum(g * GROUP + i, last)]
            peer = item // CAP
            c = item % CAP
            slot = side_s[peer, 2 * c]
            live = side_s[peer, 2 * c + 1]
            q = recv[peer, pl.ds(pl.multiple_of(c * ROWS, ROWS), ROWS), :]
            todo.append((item, peer, c, block_partial(q, kp[slot], vp[slot], live, scale)))
        for item, peer, c, (o, z) in todo:
            back[peer, pl.ds(pl.multiple_of(c * ROWS, ROWS), ROWS), :] = o.astype(BF)
            lse[item] = jnp.broadcast_to(z, (ROWS, 128))
        return 0

    lax.fori_loop(0, (n + GROUP - 1) // GROUP, work, 0)
    lane = lane_iota()

    def side(i, _):
        out = jnp.zeros((ROWS, 128), F32)
        for c in range(CAP):
            rest = lse[i * CAP + c]
            for piece in range(3):
                part = rest.astype(BF).astype(F32)
                rest = rest - part
                out = jnp.where(lane == 3 * c + piece, part, out)
        back[i, CAP * ROWS :, :] = out.astype(BF)
        return 0

    lax.fori_loop(0, peers, side, 0, unroll=4)


def home_kernel(entry, table, lengths, q, nk, nv, kp, vp, o_out, z_out, lent, ids):
    requests, blocks = table.shape
    scale = 128**-0.5
    entries = requests * blocks
    z_out[...] = jnp.full(z_out.shape, DEAD, F32)
    o_out[...] = jnp.zeros(o_out.shape, BF)

    def clear(i, _):
        lent[i] = 0
        return 0

    lax.fori_loop(0, entries, clear, 0, unroll=8)

    def mark(j, _):
        lent[entry[j]] = 1
        return 0

    lax.fori_loop(0, entry.shape[0], mark, 0, unroll=8)

    def listing(e, n):
        ids[n] = e
        alive = lengths[e // blocks] > (e % blocks) * 128
        return n + jnp.where(jnp.logical_and(alive, lent[e] == 0), 1, 0)

    n = lax.fori_loop(0, entries, listing, 0, unroll=4)
    last = jnp.maximum(n - 1, 0)

    def work(g, _):
        todo = []
        for i in range(GROUP):
            e = ids[jnp.minimum(g * GROUP + i, last)]
            r = e // blocks
            b = e % blocks
            slot = table[r, b]
            todo.append((e, block_partial(q[r], kp[slot], vp[slot], lengths[r] - b * 128, scale)))
        for e, (o, z) in todo:
            o_out[e] = o.astype(BF)
            z_out[e] = jnp.broadcast_to(z, (ROWS, 128))
        return 0

    lax.fori_loop(0, (n + GROUP - 1) // GROUP, work, 0)
    second = lax.broadcasted_iota(jnp.int32, (ROWS, 1), 0) >= ROWS // 2
    for r in range(requests):
        qr = q[r].astype(F32)
        k = nk[r].astype(F32)
        v = nv[r].astype(F32)
        s0 = jnp.sum(qr * k[0:1], axis=1, keepdims=True) * scale
        s1 = jnp.sum(qr * k[1:2], axis=1, keepdims=True) * scale
        s1 = jnp.where(second, s1, DEAD)
        m = jnp.maximum(s0, s1)
        p0 = jnp.exp(s0 - m)
        p1 = jnp.where(second, jnp.exp(s1 - m), 0.0)
        l = p0 + p1
        o = (p0 * v[0:1] + p1 * v[1:2]) / l
        o_out[entries + r] = o.astype(BF)
        z_out[entries + r] = jnp.broadcast_to(m + jnp.log(l), (ROWS, 128))


def merge_kernel(entry, target, back, o_home, z_home, w, out, o_all, z_all, att, count):
    requests = o_home.shape[0] // 9
    entries = requests * 8
    peers = back.shape[0]
    o_all[...] = o_home[...].astype(F32)
    z_all[...] = z_home[...]

    def clear(i, _):
        count[i] = 0
        return 0

    lax.fori_loop(0, peers, clear, 0, unroll=8)

    def fetch(j, _):
        e = entry[j]
        t = target[j, 0]
        rank = count[t]
        count[t] = rank + 1
        o_all[e] = back[t, pl.ds(pl.multiple_of(rank * ROWS, ROWS), ROWS), :].astype(F32)
        side = back[t, CAP * ROWS :, :].astype(F32)
        z = jnp.where(
            rank == 0,
            side[:, 0:1] + side[:, 1:2] + side[:, 2:3],
            side[:, 3:4] + side[:, 4:5] + side[:, 5:6],
        )
        z_all[e] = jnp.broadcast_to(z, (ROWS, 128))
        return 0

    lax.fori_loop(0, entry.shape[0], fetch, 0, unroll=4)
    for r in range(requests):
        z = [z_all[r * 8 + b] for b in range(8)] + [z_all[entries + r]]
        o = [o_all[r * 8 + b] for b in range(8)] + [o_all[entries + r]]
        m = functools.reduce(jnp.maximum, z)
        f = [jnp.exp(x - m) for x in z]
        top = functools.reduce(jnp.add, [a * b for a, b in zip(f, o)])
        att[r * ROWS : (r + 1) * ROWS, :] = top / functools.reduce(jnp.add, f)
    heads = ROWS // 2
    a = jnp.concatenate(
        [att[pl.ds(g, 2 * requests, stride=heads), :].astype(BF) for g in range(heads)], axis=1
    )
    width = out.shape[2]

    def project(p, _):
        cols = pl.ds(pl.multiple_of(p * width, width), width)
        out[p] = jnp.dot(a, w[:, cols], preferred_element_type=F32).astype(BF)
        return 0

    lax.fori_loop(0, out.shape[0], project, 0)


def sum_kernel(parts, out):
    total = parts[0].astype(F32)
    for i in range(1, parts.shape[0]):
        total = total + parts[i].astype(F32)
    out[...] = total.astype(BF)


def params(limit):
    return pltpu.CompilerParams(vmem_limit_bytes=limit * 1024 * 1024)


def on_device(
    queries,
    new_keys,
    new_values,
    key_pool,
    value_pool,
    block_table,
    lengths,
    lend_entry,
    lend_target,
    out_weight,
):
    requests, steps, heads, size = queries.shape
    peers = lax.axis_size("inst")
    parts = lax.axis_size("tp")
    pool = key_pool.shape[0]
    entries = requests * block_table.shape[1]
    q = queries.reshape(requests, steps * heads, size)
    nk = new_keys.reshape(requests, steps, size)
    nv = new_values.reshape(requests, steps, size)
    kp = key_pool.reshape(pool, 128, size)
    vp = value_pool.reshape(pool, 128, size)
    smem = lambda n: pltpu.SMEM((n,), jnp.int32)

    send = pl.pallas_call(
        pack_kernel,
        out_shape=jax.ShapeDtypeStruct((peers, SLAB, size), BF),
        in_specs=[SM, SM, SM, SM, VM],
        out_specs=VM,
        scratch_shapes=[smem(peers), smem(peers * CAP), smem(peers * CAP)],
        compiler_params=params(8),
    )(lend_entry, lend_target, block_table, lengths, q)

    recv = lax.all_to_all(send, "inst", split_axis=0, concat_axis=0, tiled=True)

    o_home, z_home = pl.pallas_call(
        home_kernel,
        out_shape=(
            jax.ShapeDtypeStruct((entries + requests, ROWS, size), BF),
            jax.ShapeDtypeStruct((entries + requests, ROWS, size), F32),
        ),
        in_specs=[SM, SM, SM, VM, VM, VM, VM, VM],
        out_specs=(VM, VM),
        scratch_shapes=[smem(entries), smem(entries + 1)],
        compiler_params=params(16),
    )(lend_entry, block_table, lengths, q, nk, nv, kp, vp)

    back = pl.pallas_call(
        serve_kernel,
        out_shape=jax.ShapeDtypeStruct((peers, SLAB, size), BF),
        in_specs=[VM, VM, VM],
        out_specs=VM,
        scratch_shapes=[
            pltpu.VMEM((peers * ROWS, 128), F32),
            pltpu.VMEM((peers, 128), jnp.int32),
            pltpu.SMEM((peers, 128), jnp.int32),
            smem(peers * CAP + 1),
            pltpu.VMEM((peers * CAP, ROWS, 128), F32),
            pltpu.SemaphoreType.DMA,
        ],
        compiler_params=params(16),
    )(recv, kp, vp)

    mine = lax.all_to_all(back, "inst", split_axis=0, concat_axis=0, tiled=True)

    partial = pl.pallas_call(
        merge_kernel,
        out_shape=jax.ShapeDtypeStruct((parts, requests * steps, out_weight.shape[1] // parts), BF),
        in_specs=[SM, SM, VM, VM, VM, VM],
        out_specs=VM,
        scratch_shapes=[
            pltpu.VMEM((entries + requests, ROWS, size), F32),
            pltpu.VMEM((entries + requests, ROWS, size), F32),
            pltpu.VMEM((requests * ROWS, size), F32),
            smem(peers),
        ],
        compiler_params=params(24),
    )(lend_entry, lend_target, mine, o_home, z_home, out_weight)

    shares = lax.all_to_all(partial, "tp", split_axis=0, concat_axis=0, tiled=True)

    total = pl.pallas_call(
        sum_kernel,
        out_shape=jax.ShapeDtypeStruct(shares.shape[1:], BF),
        in_specs=[VM],
        out_specs=VM,
    )(shares)
    return total.reshape(requests, steps, total.shape[1])


def solution(mesh):
    placed = (
        P("inst", None, "tp", None),
        P("inst", None, "tp", None),
        P("inst", None, "tp", None),
        P("inst", "tp", None, None),
        P("inst", "tp", None, None),
        P("inst", None),
        P("inst"),
        P("inst"),
        P("inst", None),
        P("tp", None),
    )
    return jax.shard_map(
        on_device, mesh=mesh, in_specs=placed, out_specs=P("inst", None, "tp"), check_vma=False
    )
```

time: 203 us -> 88.7 us (0.44); the launches traced: 200 us -> 89.4 us
  waiting for transfers between devices: 104 us -> 3.69 us
  Pallas kernels: 0 us -> 22.1 us
  blocking collectives: 20.2 us -> 38.4 us
  local copies, waits for them, and re-layouts: 30 us -> 13 us
  matrix products: 15.2 us -> 0 us
  between operations: 13.6 us -> 0.14 us
  other arithmetic: 4.53 us -> 0 us
    all_to_all x2 -> x1, waiting for transfers between devices: 71.4 us -> 3.69 us  [on_device(): mine = lax.all_to_all(back, 'inst', split_axis=0, concat_axis=0, tiled=True)]
    reduce_scatter x1 -> x0, waiting for transfers between devices: 32.9 us -> none  [on_device(): lax.psum_scatter(partial_out.astype(jnp.bfloat16), 'tp', scatter_dimensio...]
    pallas_call x0 -> x5, Pallas kernels: none -> 22.1 us  [the longest x1 7.53 us: on_device(): pl.pallas_call(home_kernel, out_shape=(jax.ShapeDtypeStruct((entries + re...]
    all_to_all x1 -> x2, blocking collectives: 20.2 us -> 38.4 us  [the longest x1 25.5 us: on_device(): recv = lax.all_to_all(send, 'inst', split_axis=0, concat_axis=0, tiled=True)]
    gather x7 -> x0, local copies, waits for them, and re-layouts: 17.9 us -> none  [the longest x1 3.76 us: on_device(): value_pool[served].reshape((instances, capacity) + block_shape)]
    dot_general x9 -> x0, matrix products: 15.2 us -> none  [the longest x4 5.86 us: block_state(): jnp.einsum('nhgbt,nbhtd->nhgd', weights, value_blocks, preferred_element_...]
    unnamed x15 -> x31, local copies, waits for them, and re-layouts: 0.03 us -> 11.7 us
    scatter x3 -> x0, local copies, waits for them, and re-layouts: 9.95 us -> none  [the longest x1 4.64 us: on_device(): all_keys = home_keys.reshape((req_count * max_blocks,) + block_shape).at[...]
  transfers between devices with their start and end apart: 3 -> 1, of which waited for: 3 -> 1; matrix products, arithmetic and copies ran while one was open for 11% -> 0% of each run, Pallas kernels for 0% -> 8%
where the time goes in v1:
time: 88.7 us; the launch traced here: 89.4 us
  blocking collectives  38.4 us (43%)
  Pallas kernels  22.1 us (25%)
  local copies, waits for them, and re-layouts  13 us (15%)
  starting transfers between devices  12.1 us (14%)
  waiting for transfers between devices  3.69 us (4%)
    all_to_all x1, blocking collectives, on_device(): recv = lax.all_to_all(send, 'inst', split_axis=0, concat_axis=0, tiled=True)  25.5 us
    all_to_all x1, blocking collectives, on_device(): lax.all_to_all(partial, 'tp', split_axis=0, concat_axis=0, tiled=True)  13 us
    all_to_all x1, starting transfers between devices, on_device(): mine = lax.all_to_all(back, 'inst', split_axis=0, concat_axis=0, tiled=True)  12.1 us
    unnamed x31, local copies, waits for them, and re-layouts  11.7 us
    pallas_call x1, Pallas kernels, on_device(): pl.pallas_call(home_kernel, out_shape=(jax.ShapeDtypeStruct((entries + re...  7.53 us
    pallas_call x1, Pallas kernels, on_device(): pl.pallas_call(serve_kernel, out_shape=jax.ShapeDtypeStruct((peers, SLAB,...  6.13 us
    pallas_call x1, Pallas kernels, on_device(): pl.pallas_call(merge_kernel, out_shape=jax.ShapeDtypeStruct((parts, reque...  4.82 us
    all_to_all x1, waiting for transfers between devices, on_device(): mine = lax.all_to_all(back, 'inst', split_axis=0, concat_axis=0, tiled=True)  3.69 us
  transfers between devices with their start and end apart: 1, of which 1 were waited for; matrix products, arithmetic and copies ran while one was open for 0% of the time, Pallas kernels for 8%

profile of v1, /device:TPU:1, one launch (start us, length us, event | category | flops | bytes accessed | tf_op | source)
XLA Modules:
  0.0 89.4 jit_solution(6549395796984296518)
XLA Ops:
  0.0 0.7 copy.12.target
  0.7 0.8 copy-done.5
  1.5 0.0 copy-start.7
  1.5 0.7 copy-done.7
  2.2 0.0 copy-start.9
  2.2 0.7 copy-done.9
  2.8 0.7 copy-done.13
  3.5 2.0 %shard_map.100 = bf16[32,48,128]{2,1,0:T(8,128)(2,1)S(1)} custom-call(s32[32]{0:T(128)S(1)} %copy-done.9, s32[32,1]{1,0:T(8,128)S(1)} %copy.12.target, s32[8,8]{1,0:T(8,128)S(1)} %copy-done.7, s32[8]{0:T(128)S(1)} %copy-done.13, bf16[8,16,128]{2,1,0:T(8,128)(2,1)S(1)} %bitcast.9), custom_call_target="tpu_custom_call" | custom-call | tf_op jit(solution)/shard_map/pallas_call | solution.py:270
  5.5 25.5 %all_to_all.15.recv = bf16[32,48,128]{2,1,0:T(8,128)(2,1)S(1)} all-to-all(bf16[32,48,128]{2,1,0:T(8,128)(2,1)S(1)} %shard_map.100), channel_id=1, replica_groups=mesh['inst'=32,'tp'=8] {'inst'}, dimensions={0} | all-to-all | bytes 786432 | tf_op jit(solution)/shard_map/all_to_all | solution.py:279
  31.0 1.6 %copy-done.1 = bf16[64,1,128,128]{3,2,1,0:T(8,128)(2,1)S(1)} copy-done((bf16[64,1,128,128]{3,2,1,0:T(8,128)(2,1)S(1)}, bf16[64,1,128,128]{3,2,1,0:T(8,128)(2,1)}, u32[]{:S(2)}) %copy-start.1) | copy-done | bytes 2097176
  32.6 1.6 %copy-done.3 = bf16[64,1,128,128]{3,2,1,0:T(8,128)(2,1)S(1)} copy-done((bf16[64,1,128,128]{3,2,1,0:T(8,128)(2,1)S(1)}, bf16[64,1,128,128]{3,2,1,0:T(8,128)(2,1)}, u32[]{:S(2)}) %copy-start.3) | copy-done | bytes 2097176
  34.2 0.0 copy-start.11
  34.2 0.0 copy-start.12
  34.2 0.0 copy-start.14
  34.2 6.1 %shard_map.101 = bf16[32,48,128]{2,1,0:T(8,128)(2,1)} custom-call(bf16[32,48,128]{2,1,0:T(8,128)(2,1)S(1)} %all_to_all.15.recv, bf16[64,128,128]{2,1,0:T(8,128)(2,1)S(1)} %bitcast.5, bf16[64,128,128]{2,1,0:T(8,128)(2,1)S(1)} %bitcast.7), custom_call_target="tpu_custom_call" | custom-call | tf_op jit(solution)/shard_map/pallas_call | solution.py:293
  40.4 12.1 %all-to-all-start.1 = ((bf16[32,48,128]{2,1,0:T(8,128)(2,1)}), bf16[32,48,128]{2,1,0:T(8,128)(2,1)S(1)}, u32[]{:S(2)}, u32[]{:S(2)}) async-start(bf16[32,48,128]{2,1,0:T(8,128)(2,1)} %shard_map.101), calls=%async_computation.1 | async-start | bytes 786432 | tf_op jit(solution)/shard_map/all_to_all | solution.py:309
  52.5 0.0 copy-done.2
  52.5 0.0 copy-done.6
  52.5 0.0 copy-done.8
  52.5 0.0 copy-done.10
  52.5 0.0 copy-done.11
  52.5 0.0 copy-done.12
  52.5 0.0 copy-done.14
  52.5 0.0 copy-start.4
  52.5 1.6 %copy-done.4 = bf16[64,1,128,128]{3,2,1,0:T(8,128)(2,1)S(1)} copy-done((bf16[64,1,128,128]{3,2,1,0:T(8,128)(2,1)S(1)}, bf16[64,1,128,128]{3,2,1,0:T(8,128)(2,1)}, u32[]{:S(2)}) %copy-start.4) | copy-done | bytes 2097176
  54.1 7.5 %shard_map.102 = (bf16[72,16,128]{2,1,0:T(8,128)(2,1)S(1)}, f32[72,16,128]{2,1,0:T(8,128)S(1)}) custom-call(s32[32]{0:T(128)S(1)} %copy-done.10, s32[8,8]{1,0:T(8,128)S(1)} %copy-done.8, s32[8]{0:T(128)S(1)} %copy-done.14, bf16[8,16,128]{2,1,0:T(8,128)(2,1)S(1)} %bitcast.10, bf16[8,2,128]{2,1,0:T(2,128)(2,1)S(1)} %bitcast.11, ...), custom_call_target="tpu_custom_call" | custom-call | tf_op jit(solution)/shard_map/pallas_call | solution.py:281
  61.7 3.7 %all-to-all-done.1.back = bf16[32,48,128]{2,1,0:T(8,128)(2,1)S(1)} async-done(((bf16[32,48,128]{2,1,0:T(8,128)(2,1)}), bf16[32,48,128]{2,1,0:T(8,128)(2,1)S(1)}, u32[]{:S(2)}, u32[]{:S(2)}) %all-to-all-start.1) | async-done | bytes 393248 | tf_op jit(solution)/shard_map/all_to_all | solution.py:309
  65.4 3.4 %copy-done = bf16[1024,4096]{1,0:T(8,128)(2,1)S(1)} copy-done((bf16[1024,4096]{1,0:T(8,128)(2,1)S(1)}, bf16[1024,4096]{1,0:T(8,128)(2,1)}, u32[]{:S(2)}) %copy-start) | copy-done | bytes 8388632
  68.7 4.8 %shard_map.103 = bf16[8,16,512]{2,1,0:T(8,128)(2,1)S(1)} custom-call(s32[32]{0:T(128)S(1)} %copy-done.10, s32[32,1]{1,0:T(8,128)S(1)} %copy.12.target, bf16[32,48,128]{2,1,0:T(8,128)(2,1)S(1)} %all-to-all-done.1.back, bf16[72,16,128]{2,1,0:T(8,128)(2,1)S(1)} %get-tuple-element.7.o_home, f32[72,16,128]{2,1,0:T(8,128)S(1)} %get-tuple-element.8.z_home, ...), custom_call_target="tpu_custom_call" | custom-call | tf_op jit(solution)/shard_map/pallas_call | solution.py:311
  73.6 13.0 %all_to_all.16.parts = bf16[8,16,512]{2,1,0:T(8,128)(2,1)} all-to-all(bf16[8,16,512]{2,1,0:T(8,128)(2,1)S(1)} %shard_map.103), channel_id=1, replica_groups=mesh['inst'=32,'tp'=8] {'tp'}, dimensions={0} | all-to-all | bytes 262144 | tf_op jit(solution)/shard_map/all_to_all | solution.py:325
  86.5 1.5 %shard_map.104 = bf16[16,512]{1,0:T(8,128)(2,1)} custom-call(bf16[8,16,512]{2,1,0:T(8,128)(2,1)} %all_to_all.16.parts), custom_call_target="tpu_custom_call" | custom-call | tf_op jit(solution)/shard_map/pallas_call | solution.py:327
  88.1 1.3 %reshape.23 = bf16[8,2,512]{2,1,0:T(2,128)(2,1)} reshape(bf16[16,512]{1,0:T(8,128)(2,1)} %shard_map.104) | data formatting | bytes 32768 | tf_op jit(solution)/shard_map/reshape | solution.py:333
  (9 shorter events, 0.0 us)
Async XLA Ops:
  0.7 0.8 copy-start.5
  1.5 0.7 copy-start.7
  2.2 0.7 copy-start.9
  2.8 0.7 copy-start.13
  31.0 1.6 %copy-start.1 = (bf16[64,1,128,128]{3,2,1,0:T(8,128)(2,1)S(1)}, bf16[64,1,128,128]{3,2,1,0:T(8,128)(2,1)}, u32[]{:S(2)}) copy-start(bf16[64,1,128,128]{3,2,1,0:T(8,128)(2,1)} %param.13) | copy-start | bytes 6291460
  32.6 1.6 %copy-start.3 = (bf16[64,1,128,128]{3,2,1,0:T(8,128)(2,1)S(1)}, bf16[64,1,128,128]{3,2,1,0:T(8,128)(2,1)}, u32[]{:S(2)}) copy-start(bf16[64,1,128,128]{3,2,1,0:T(8,128)(2,1)} %param.14) | copy-start | bytes 6291460
  34.2 18.3 %copy-start.2 = (bf16[64,1,128,128]{3,2,1,0:T(8,128)(2,1)S(1)}, bf16[64,1,128,128]{3,2,1,0:T(8,128)(2,1)}, u32[]{:S(2)}) copy-start(bf16[64,1,128,128]{3,2,1,0:T(8,128)(2,1)} %param.13) | copy-start | bytes 6291460
  34.2 18.3 %copy-start.6 = (bf16[8,2,8,128]{3,2,1,0:T(8,128)(2,1)S(1)}, bf16[8,2,8,128]{3,2,1,0:T(8,128)(2,1)}, u32[]{:S(2)}) copy-start(bf16[8,2,8,128]{3,2,1,0:T(8,128)(2,1)} %param.10) | copy-start | bytes 98308
  34.2 18.3 %copy-start.8 = (s32[8,8]{1,0:T(8,128)S(1)}, s32[8,8]{1,0:T(8,128)}, u32[]{:S(2)}) copy-start(s32[8,8]{1,0:T(8,128)} %table.3) | copy-start | bytes 772
  34.2 18.3 %copy-start.10 = (s32[32]{0:T(128)S(1)}, s32[32]{0:T(128)}, u32[]{:S(2)}) copy-start(s32[32]{0:T(128)} %entry.5) | copy-start | bytes 388
  34.2 18.3 %copy-start.11 = (bf16[8,2,1,128]{3,1,2,0:T(2,128)(2,1)S(1)}, bf16[8,2,1,128]{3,1,2,0:T(2,128)(2,1)}, u32[]{:S(2)}) copy-start(bf16[8,2,1,128]{3,1,2,0:T(2,128)(2,1)} %param.11) | copy-start | bytes 12292
  34.2 18.3 %copy-start.12 = (bf16[8,2,1,128]{3,1,2,0:T(2,128)(2,1)S(1)}, bf16[8,2,1,128]{3,1,2,0:T(2,128)(2,1)}, u32[]{:S(2)}) copy-start(bf16[8,2,1,128]{3,1,2,0:T(2,128)(2,1)} %param.12) | copy-start | bytes 12292
  34.2 18.3 %copy-start.14 = (s32[8]{0:T(128)S(1)}, s32[8]{0:T(128)}, u32[]{:S(2)}) copy-start(s32[8]{0:T(128)} %lengths.3) | copy-start | bytes 100
  40.4 25.0 %all-to-all-start.1 = ((bf16[32,48,128]{2,1,0:T(8,128)(2,1)}), bf16[32,48,128]{2,1,0:T(8,128)(2,1)S(1)}, u32[]{:S(2)}, u32[]{:S(2)}) async-start(bf16[32,48,128]{2,1,0:T(8,128)(2,1)} %shard_map.101), calls=%async_computation.1 | async-start | bytes 786432 | tf_op jit(solution)/shard_map/all_to_all | solution.py:309
  52.5 1.6 %copy-start.4 = (bf16[64,1,128,128]{3,2,1,0:T(8,128)(2,1)S(1)}, bf16[64,1,128,128]{3,2,1,0:T(8,128)(2,1)}, u32[]{:S(2)}) copy-start(bf16[64,1,128,128]{3,2,1,0:T(8,128)(2,1)} %param.14) | copy-start | bytes 6291460
  65.4 3.4 %copy-start = (bf16[1024,4096]{1,0:T(8,128)(2,1)S(1)}, bf16[1024,4096]{1,0:T(8,128)(2,1)}, u32[]{:S(2)}) copy-start(bf16[1024,4096]{1,0:T(8,128)(2,1)} %w.1) | copy-start | bytes 25165828

commit v2 on v1

v2 whole, which is shorter than its diff:
```python
import functools

import jax
import jax.numpy as jnp
from jax import lax
from jax.experimental import pallas as pl
from jax.experimental.pallas import tpu as pltpu
from jax.sharding import PartitionSpec as P

DEAD = -1e30
CAP = 2
GROUP = 8
ROWS = 16
HALF = 8
SLAB = 40
BF = jnp.bfloat16
F32 = jnp.float32
VM = pl.BlockSpec(memory_space=pltpu.VMEM)
HB = pl.BlockSpec(memory_space=pl.ANY)


def lane_iota(rows=ROWS):
    return lax.broadcasted_iota(jnp.int32, (rows, 128), 1)


def fetch_all(pairs, sems):
    copies = [pltpu.make_async_copy(a, b, sems.at[i]) for i, (a, b) in enumerate(pairs)]
    for c in copies:
        c.start()
    return copies


def pack_kernel(
    entry_h, target_h, table_h, lengths_h, q_h, kp_h, vp_h,
    send, kp, vp,
    entry, target, table, lengths, q, tiles, count, slots, lives, sems,
):
    peers = send.shape[0]
    blocks = table.shape[1]
    small = fetch_all(
        [(entry_h, entry), (target_h, target), (table_h, table), (lengths_h, lengths), (q_h, q), (kp_h, kp), (vp_h, vp)],
        sems,
    )

    def clear(i, _):
        count[i] = 0
        for c in range(CAP):
            slots[i * CAP + c] = 0
            lives[i * CAP + c] = 0
        return 0

    lax.fori_loop(0, peers, clear, 0, unroll=4)
    for c in small[:5]:
        c.wait()

    def place(j, _):
        e = entry[j]
        t = target[j]
        r = e // blocks
        b = e % blocks
        rank = count[t]
        count[t] = rank + 1
        i = t * CAP + rank
        slots[i] = table[r, b]
        lives[i] = jnp.clip(lengths[r] - b * 128, 0, 128)
        tiles[i] = q[r]
        return 0

    lax.fori_loop(0, entry.shape[0], place, 0, unroll=4)
    lane = lane_iota(HALF)

    def lay(i, _):
        v = jnp.where(lane == 0, slots[i * CAP], 0)
        v = jnp.where(lane == 1, lives[i * CAP], v)
        v = jnp.where(lane == 2, slots[i * CAP + 1], v)
        v = jnp.where(lane == 3, lives[i * CAP + 1], v)
        send[i] = jnp.concatenate(
            [tiles[i * CAP], tiles[i * CAP + 1], v.astype(F32).astype(BF)], axis=0
        )
        return 0

    lax.fori_loop(0, peers, lay, 0, unroll=4)
    for c in small[5:]:
        c.wait()


def attend(n, query, slot_of, live_of, store, kp, vp, scores):
    scale = 128**-0.5
    groups = (n + GROUP - 1) // GROUP
    lane = lane_iota()

    def score(g):
        out = []
        for i in range(GROUP):
            item = jnp.minimum(g * GROUP + i, n - 1)
            out.append(
                lax.dot_general(
                    query(item),
                    kp[slot_of(item)],
                    (((1,), (1,)), ((), ())),
                    preferred_element_type=F32,
                )
            )
        return out

    @pl.when(n > 0)
    def _():
        for i, s in enumerate(score(0)):
            scores[0, i] = s

    def work(g, _):
        now = lax.rem(g, 2)
        held = [scores[now, i] for i in range(GROUP)]
        later = score(jnp.minimum(g + 1, groups - 1))
        done = []
        for i in range(GROUP):
            item = jnp.minimum(g * GROUP + i, n - 1)
            s = jnp.where(lane < live_of(item), held[i] * scale, DEAD)
            m = jnp.max(s, axis=1, keepdims=True)
            p = jnp.exp(s - m)
            l = jnp.sum(p, axis=1, keepdims=True)
            o = jnp.dot(p.astype(BF), vp[slot_of(item)], preferred_element_type=F32) / l
            done.append((item, o, jnp.broadcast_to(m + jnp.log(l), (ROWS, 128))))
        for item, o, z in done:
            store(item, o, z)
        for i, s in enumerate(later):
            scores[1 - now, i] = s
        return 0

    lax.fori_loop(0, groups, work, 0)


def serve_kernel(recv, kp, vp, back, side_f, side_i, side_s, ids, att, lse, scores, sem):
    peers = recv.shape[0]
    side = recv[...][:, CAP * ROWS :, :].astype(F32)
    side_f[...] = side.reshape(peers * HALF, 128)
    side_i[...] = side_f[pl.ds(0, peers, stride=HALF), :].astype(jnp.int32)
    copy = pltpu.make_async_copy(side_i, side_s, sem)
    copy.start()
    att[...] = jnp.zeros(att.shape, F32)
    lse[...] = jnp.full(lse.shape, DEAD, F32)
    copy.wait()

    def listing(i, n):
        for c in range(CAP):
            ids[n] = i * CAP + c
            n = n + jnp.where(side_s[i, 2 * c + 1] > 0, 1, 0)
        return n

    n = lax.fori_loop(0, peers, listing, 0, unroll=4)

    def query(item):
        i = ids[item]
        return recv[i // CAP, pl.ds(pl.multiple_of((i % CAP) * ROWS, ROWS), ROWS), :]

    def slot_of(item):
        i = ids[item]
        return side_s[i // CAP, 2 * (i % CAP)]

    def live_of(item):
        i = ids[item]
        return side_s[i // CAP, 2 * (i % CAP) + 1]

    def store(item, o, z):
        att[ids[item]] = o
        lse[ids[item]] = z

    attend(n, query, slot_of, live_of, store, kp, vp, scores)
    lane = lane_iota(HALF)

    def lay(i, _):
        side = jnp.zeros((HALF, 128), F32)
        for c in range(CAP):
            for h in range(2):
                rest = lse[i * CAP + c, h * HALF : (h + 1) * HALF, :]
                for piece in range(3):
                    part = rest.astype(BF).astype(F32)
                    rest = rest - part
                    side = jnp.where(lane == (h * CAP + c) * 4 + piece, part, side)
        rows = jnp.concatenate([att[i * CAP], att[i * CAP + 1], side], axis=0)
        back[i] = rows.astype(BF)
        return 0

    lax.fori_loop(0, peers, lay, 0, unroll=4)


def home_kernel(
    entry_h, table_h, lengths_h, w_h, q, nk, nv, kp, vp,
    o_out, z_out, w,
    entry, table, lengths, lent, ids, scores, sems,
):
    requests, blocks = table.shape
    entries = requests * blocks
    copies = fetch_all(
        [(entry_h, entry), (table_h, table), (lengths_h, lengths), (w_h, w)], sems
    )
    z_out[...] = jnp.full(z_out.shape, DEAD, F32)
    o_out[...] = jnp.zeros(o_out.shape, F32)

    def clear(i, _):
        lent[i] = 0
        return 0

    lax.fori_loop(0, entries, clear, 0, unroll=8)
    for c in copies[:3]:
        c.wait()

    def mark(j, _):
        lent[entry[j]] = 1
        return 0

    lax.fori_loop(0, entry.shape[0], mark, 0, unroll=8)

    def listing(e, n):
        ids[n] = e
        alive = lengths[e // blocks] > (e % blocks) * 128
        return n + jnp.where(jnp.logical_and(alive, lent[e] == 0), 1, 0)

    n = lax.fori_loop(0, entries, listing, 0, unroll=4)

    def query(item):
        return q[ids[item] // blocks]

    def slot_of(item):
        e = ids[item]
        return table[e // blocks, e % blocks]

    def live_of(item):
        e = ids[item]
        return lengths[e // blocks] - (e % blocks) * 128

    def store(item, o, z):
        o_out[ids[item]] = o
        z_out[ids[item]] = z

    attend(n, query, slot_of, live_of, store, kp, vp, scores)
    scale = 128**-0.5
    second = lax.broadcasted_iota(jnp.int32, (ROWS, 1), 0) >= HALF
    for r in range(requests):
        qr = q[r].astype(F32)
        k = nk[r].astype(F32)
        v = nv[r].astype(F32)
        s0 = jnp.sum(qr * k[0:1], axis=1, keepdims=True) * scale
        s1 = jnp.sum(qr * k[1:2], axis=1, keepdims=True) * scale
        s1 = jnp.where(second, s1, DEAD)
        m = jnp.maximum(s0, s1)
        p0 = jnp.exp(s0 - m)
        p1 = jnp.where(second, jnp.exp(s1 - m), 0.0)
        l = p0 + p1
        o_out[entries + r] = (p0 * v[0:1] + p1 * v[1:2]) / l
        z_out[entries + r] = jnp.broadcast_to(m + jnp.log(l), (ROWS, 128))
    copies[3].wait()


def merge_kernel(
    entry_h, target_h, back, o_home, z_home, w,
    out,
    entry, target, o_all, z_all, z_back, att, count, sems,
):
    requests = o_home.shape[0] // 9
    entries = requests * 8
    peers = back.shape[0]
    copies = fetch_all([(entry_h, entry), (target_h, target)], sems)
    o_all[...] = o_home[...]
    z_all[...] = z_home[...]
    side = back[...][:, CAP * ROWS :, :].reshape(peers * HALF, 128)
    kinds = 2 * CAP
    lane = lax.broadcasted_iota(jnp.int32, (128, kinds * 128), 0)
    block = lax.broadcasted_iota(jnp.int32, (128, kinds * 128), 1) // 128
    pick = jnp.logical_and(lane >= block * 4, lane < block * 4 + 3)
    z_back[...] = jnp.dot(side, pick.astype(F32).astype(BF), preferred_element_type=F32)

    def clear(i, _):
        count[i] = 0
        return 0

    lax.fori_loop(0, peers, clear, 0, unroll=8)
    for c in copies:
        c.wait()

    def fetch(j, _):
        e = entry[j]
        t = target[j]
        rank = count[t]
        count[t] = rank + 1
        o_all[e] = back[t, pl.ds(pl.multiple_of(rank * ROWS, ROWS), ROWS), :].astype(F32)
        rows = pl.ds(pl.multiple_of(t * HALF, HALF), HALF)
        for h in range(2):
            cols = pl.ds(pl.multiple_of((h * CAP + rank) * 128, 128), 128)
            z_all[e, h * HALF : (h + 1) * HALF, :] = z_back[rows, cols]
        return 0

    lax.fori_loop(0, entry.shape[0], fetch, 0, unroll=4)
    for r in range(requests):
        z = [z_all[r * 8 + b] for b in range(8)] + [z_all[entries + r]]
        o = [o_all[r * 8 + b] for b in range(8)] + [o_all[entries + r]]
        m = functools.reduce(jnp.maximum, z)
        f = [jnp.exp(x - m) for x in z]
        top = functools.reduce(jnp.add, [a * b for a, b in zip(f, o)])
        att[r * ROWS : (r + 1) * ROWS, :] = top / functools.reduce(jnp.add, f)
    heads = ROWS // 2
    a = jnp.concatenate(
        [att[pl.ds(g, 2 * requests, stride=heads), :].astype(BF) for g in range(heads)], axis=1
    )
    width = out.shape[2]

    def project(p, _):
        cols = pl.ds(pl.multiple_of(p * width, width), width)
        out[p] = jnp.dot(a, w[:, cols], preferred_element_type=F32).astype(BF)
        return 0

    lax.fori_loop(0, out.shape[0], project, 0)


def sum_kernel(parts, out):
    total = parts[0].astype(F32)
    for i in range(1, parts.shape[0]):
        total = total + parts[i].astype(F32)
    out[...] = total.astype(BF).reshape(out.shape)


def params(limit):
    return pltpu.CompilerParams(vmem_limit_bytes=limit * 1024 * 1024)


def on_device(
    queries,
    new_keys,
    new_values,
    key_pool,
    value_pool,
    block_table,
    lengths,
    lend_entry,
    lend_target,
    out_weight,
):
    requests, steps, heads, size = queries.shape
    peers = lax.axis_size("inst")
    parts = lax.axis_size("tp")
    pool = key_pool.shape[0]
    entries = block_table.size
    lends = lend_entry.shape[0]
    q = queries.reshape(requests, steps * heads, size)
    nk = new_keys.reshape(requests, steps, size)
    nv = new_values.reshape(requests, steps, size)
    kp = key_pool.reshape(pool, 128, size)
    vp = value_pool.reshape(pool, 128, size)
    target = lend_target.reshape(lends)
    held = lambda x: pltpu.with_memory_space_constraint(x, pltpu.HBM)
    smem = lambda *n: pltpu.SMEM(n, jnp.int32)
    sems = lambda n: pltpu.SemaphoreType.DMA((n,))
    like = lambda x: jax.ShapeDtypeStruct(x.shape, x.dtype)
    scores = pltpu.VMEM((2, GROUP, ROWS, 128), F32)

    send, kp, vp = pl.pallas_call(
        pack_kernel,
        out_shape=(jax.ShapeDtypeStruct((peers, SLAB, size), BF), like(kp), like(vp)),
        in_specs=[HB] * 7,
        out_specs=(VM, VM, VM),
        scratch_shapes=[
            smem(lends),
            smem(lends),
            smem(*block_table.shape),
            smem(requests),
            pltpu.VMEM(q.shape, BF),
            pltpu.VMEM((peers * CAP, ROWS, size), BF),
            smem(peers),
            smem(peers * CAP),
            smem(peers * CAP),
            sems(7),
        ],
        compiler_params=params(16),
    )(*map(held, (lend_entry, target, block_table, lengths, q, kp, vp)))

    recv = lax.all_to_all(send, "inst", split_axis=0, concat_axis=0, tiled=True)

    tile_state = jax.ShapeDtypeStruct((entries + requests, ROWS, size), F32)
    o_home, z_home, weight = pl.pallas_call(
        home_kernel,
        out_shape=(tile_state, tile_state, like(out_weight)),
        in_specs=[HB] * 4 + [VM] * 5,
        out_specs=(VM, VM, VM),
        scratch_shapes=[
            smem(lends),
            smem(*block_table.shape),
            smem(requests),
            smem(entries),
            smem(entries + 1),
            scores,
            sems(4),
        ],
        compiler_params=params(24),
        cost_estimate=pl.CostEstimate(flops=10**9, bytes_accessed=16 * 2**20, transcendentals=0),
    )(*map(held, (lend_entry, block_table, lengths, out_weight)), q, nk, nv, kp, vp)

    back = pl.pallas_call(
        serve_kernel,
        out_shape=jax.ShapeDtypeStruct((peers, SLAB, size), BF),
        in_specs=[VM, VM, VM],
        out_specs=VM,
        scratch_shapes=[
            pltpu.VMEM((peers * HALF, 128), F32),
            pltpu.VMEM((peers, 128), jnp.int32),
            smem(peers, 128),
            smem(peers * CAP + 1),
            pltpu.VMEM((peers * CAP, ROWS, 128), F32),
            pltpu.VMEM((peers * CAP, ROWS, 128), F32),
            scores,
            pltpu.SemaphoreType.DMA,
        ],
        compiler_params=params(16),
    )(recv, kp, vp)

    mine = lax.all_to_all(back, "inst", split_axis=0, concat_axis=0, tiled=True)

    partial = pl.pallas_call(
        merge_kernel,
        out_shape=jax.ShapeDtypeStruct((parts, requests * steps, out_weight.shape[1] // parts), BF),
        in_specs=[HB] * 2 + [VM] * 4,
        out_specs=VM,
        scratch_shapes=[
            smem(lends),
            smem(lends),
            pltpu.VMEM(tile_state.shape, F32),
            pltpu.VMEM(tile_state.shape, F32),
            pltpu.VMEM((peers * HALF, 2 * CAP * 128), F32),
            pltpu.VMEM((requests * ROWS, size), F32),
            smem(peers),
            sems(2),
        ],
        compiler_params=params(24),
    )(held(lend_entry), held(target), mine, o_home, z_home, weight)

    shares = lax.all_to_all(partial, "tp", split_axis=0, concat_axis=0, tiled=True)

    return pl.pallas_call(
        sum_kernel,
        out_shape=jax.ShapeDtypeStruct((requests, steps, shares.shape[2]), BF),
        in_specs=[VM],
        out_specs=VM,
    )(shares)


def solution(mesh):
    placed = (
        P("inst", None, "tp", None),
        P("inst", None, "tp", None),
        P("inst", None, "tp", None),
        P("inst", "tp", None, None),
        P("inst", "tp", None, None),
        P("inst", None),
        P("inst"),
        P("inst"),
        P("inst", None),
        P("tp", None),
    )
    return jax.shard_map(
        on_device, mesh=mesh, in_specs=placed, out_specs=P("inst", None, "tp"), check_vma=False
    )
```

time: 88.7 us -> 71.1 us (0.80); the launches traced: 89.4 us -> 70.5 us
  Pallas kernels: 22.1 us -> 13.6 us
  starting transfers between devices: 12.1 us -> 5.73 us
  local copies, waits for them, and re-layouts: 13 us -> 11.4 us
  waiting for transfers between devices: 3.69 us -> 2.1 us
    all_to_all x1, starting transfers between devices: 12.1 us -> 5.73 us  [on_device(): mine = lax.all_to_all(back, 'inst', split_axis=0, concat_axis=0, tiled=True)]
    pallas_call x3, Pallas kernels: 11.1 us -> 7.26 us  [the longest x1 3.42 us: on_device(): pl.pallas_call(home_kernel, out_shape=(tile_state, tile_state, like(out_w...]
    pallas_call x1, Pallas kernels: 6.13 us -> 3.16 us  [on_device(): pl.pallas_call(serve_kernel, out_shape=jax.ShapeDtypeStruct((peers, SLAB,...]
    pallas_call x1, Pallas kernels: 4.82 us -> 3.16 us  [on_device(): pl.pallas_call(merge_kernel, out_shape=jax.ShapeDtypeStruct((parts, reque...]
    all_to_all x1, waiting for transfers between devices: 3.69 us -> 2.1 us  [on_device(): mine = lax.all_to_all(back, 'inst', split_axis=0, concat_axis=0, tiled=True)]
    reshape x1 -> x0, local copies, waits for them, and re-layouts: 1.33 us -> none  [on_device(): return total.reshape(requests, steps, total.shape[1])]
    all_to_all x1, blocking collectives: 25.5 us -> 24.2 us  [on_device(): recv = lax.all_to_all(send, 'inst', split_axis=0, concat_axis=0, tiled=True)]
    unnamed x31 -> x18, local copies, waits for them, and re-layouts: 11.7 us -> 11.4 us
  transfers between devices with their start and end apart: 1 -> 1, of which waited for: 1 -> 1; matrix products, arithmetic and copies ran while one was open for 0% -> 0% of each run, Pallas kernels for 8% -> 5%
where the time goes in v2:
time: 71.1 us; the launch traced here: 70.5 us
  blocking collectives  37.6 us (53%)
  Pallas kernels  13.6 us (19%)
  local copies, waits for them, and re-layouts  11.4 us (16%)
  starting transfers between devices  5.73 us (8%)
  waiting for transfers between devices  2.1 us (3%)
    all_to_all x1, blocking collectives, on_device(): recv = lax.all_to_all(send, 'inst', split_axis=0, concat_axis=0, tiled=True)  24.2 us
    all_to_all x1, blocking collectives, on_device(): lax.all_to_all(partial, 'tp', split_axis=0, concat_axis=0, tiled=True)  13.3 us
    unnamed x18, local copies, waits for them, and re-layouts  11.4 us
    all_to_all x1, starting transfers between devices, on_device(): mine = lax.all_to_all(back, 'inst', split_axis=0, concat_axis=0, tiled=True)  5.73 us
    pallas_call x1, Pallas kernels, on_device(): pl.pallas_call(home_kernel, out_shape=(tile_state, tile_state, like(out_w...  3.42 us
    pallas_call x1, Pallas kernels, on_device(): pl.pallas_call(serve_kernel, out_shape=jax.ShapeDtypeStruct((peers, SLAB,...  3.16 us
    pallas_call x1, Pallas kernels, on_device(): pl.pallas_call(merge_kernel, out_shape=jax.ShapeDtypeStruct((parts, reque...  3.16 us
    pallas_call x1, Pallas kernels, on_device(): pl.pallas_call(pack_kernel, out_shape=(jax.ShapeDtypeStruct((peers, SLAB,...  2.3 us
  transfers between devices with their start and end apart: 1, of which 1 were waited for; matrix products, arithmetic and copies ran while one was open for 0% of the time, Pallas kernels for 5%

profile of v2, /device:TPU:1, one launch (start us, length us, event | category | flops | bytes accessed | tf_op | source)
XLA Modules:
  0.0 70.5 jit_solution(4574850399235343513)
XLA Ops:
  0.0 2.3 %shard_map.100 = (bf16[32,40,128]{2,1,0:T(8,128)(2,1)S(1)}, bf16[64,128,128]{2,1,0:T(8,128)(2,1)S(1)}, bf16[64,128,128]{2,1,0:T(8,128)(2,1)S(1)}) custom-call(s32[32]{0:T(128)} %entry_h.5, s32[32]{0:T(128)} %bitcast.12, s32[8,8]{1,0:T(8,128)} %table_h.3, s32[8]{0:T(128)} %lengths_h.3, bf16[8,16,128]{2,1,0:T(8,128)(2,1)} %bitcast.6, ...), custom_call_target="tpu_custom_call" | custom-call | tf_op jit(solution)/shard_map/pallas_call | solution.py:356
  2.3 24.2 %all_to_all.15.recv = bf16[32,40,128]{2,1,0:T(8,128)(2,1)S(1)} all-to-all(bf16[32,40,128]{2,1,0:T(8,128)(2,1)S(1)} %get-tuple-element.11), channel_id=1, replica_groups=mesh['inst'=32,'tp'=8] {'inst'}, dimensions={0} | all-to-all | bytes 655360 | tf_op jit(solution)/shard_map/all_to_all | solution.py:376
  26.5 0.0 copy-start.6
  26.5 0.0 copy-start.7
  26.5 0.0 copy-start.8
  26.5 3.2 %shard_map.101 = bf16[32,40,128]{2,1,0:T(8,128)(2,1)} custom-call(bf16[32,40,128]{2,1,0:T(8,128)(2,1)S(1)} %all_to_all.15.recv, bf16[64,128,128]{2,1,0:T(8,128)(2,1)S(1)} %get-tuple-element.12.kp, bf16[64,128,128]{2,1,0:T(8,128)(2,1)S(1)} %get-tuple-element.13.vp), custom_call_target="tpu_custom_call" | custom-call | tf_op jit(solution)/shard_map/pallas_call | solution.py:397
  29.7 0.0 copy-start.2
  29.7 1.3 %copy-done.2 = bf16[64,128,128]{2,1,0:T(8,128)(2,1)} copy-done((bf16[64,128,128]{2,1,0:T(8,128)(2,1)}, bf16[64,128,128]{2,1,0:T(8,128)(2,1)S(1)}, u32[]{:S(2)}) %copy-start.2) | copy-done | bytes 2097176
  31.0 5.7 %all-to-all-start.1 = ((bf16[32,40,128]{2,1,0:T(8,128)(2,1)}), bf16[32,40,128]{2,1,0:T(8,128)(2,1)S(1)}, u32[]{:S(2)}, u32[]{:S(2)}) async-start(bf16[32,40,128]{2,1,0:T(8,128)(2,1)} %shard_map.101), calls=%async_computation.1 | async-start | bytes 655360 | tf_op jit(solution)/shard_map/all_to_all | solution.py:415
  36.8 0.0 copy-done.6
  36.8 0.0 copy-done.7
  36.8 0.0 copy-done.8
  36.8 0.0 copy-start.3
  36.8 1.6 %copy-done.3 = bf16[64,128,128]{2,1,0:T(8,128)(2,1)S(1)} copy-done((bf16[64,128,128]{2,1,0:T(8,128)(2,1)S(1)}, bf16[64,128,128]{2,1,0:T(8,128)(2,1)}, u32[]{:S(2)}) %copy-start.3) | copy-done | bytes 2097176
  38.4 3.4 %shard_map.102 = (f32[72,16,128]{2,1,0:T(8,128)S(1)}, f32[72,16,128]{2,1,0:T(8,128)S(1)}, bf16[1024,4096]{1,0:T(8,128)(2,1)S(1)}) custom-call(s32[32]{0:T(128)} %entry_h.5, s32[8,8]{1,0:T(8,128)} %table_h.3, s32[8]{0:T(128)} %lengths_h.3, bf16[1024,4096]{1,0:T(8,128)(2,1)} %w_h.1, bf16[8,16,128]{2,1,0:T(8,128)(2,1)S(1)} %bitcast.7, ...), custom_call_target="tpu_custom_call" | custom-call | flops 1000000000 | bytes 16777216 | tf_op jit(solution)/shard_map/pallas_call | solution.py:379
  41.8 0.0 copy-start
  41.8 3.2 %copy-done = bf16[1024,4096]{1,0:T(8,128)(2,1)} copy-done((bf16[1024,4096]{1,0:T(8,128)(2,1)}, bf16[1024,4096]{1,0:T(8,128)(2,1)S(1)}, u32[]{:S(2)}) %copy-start) | copy-done | bytes 8388632
  45.0 0.0 copy-start.4
  45.1 0.9 %copy-done.4 = f32[72,16,128]{2,1,0:T(8,128)} copy-done((f32[72,16,128]{2,1,0:T(8,128)}, f32[72,16,128]{2,1,0:T(8,128)S(1)}, u32[]{:S(2)}) %copy-start.4) | copy-done | bytes 589848
  45.9 2.1 %all-to-all-done.1.back = bf16[32,40,128]{2,1,0:T(8,128)(2,1)S(1)} async-done(((bf16[32,40,128]{2,1,0:T(8,128)(2,1)}), bf16[32,40,128]{2,1,0:T(8,128)(2,1)S(1)}, u32[]{:S(2)}, u32[]{:S(2)}) %all-to-all-start.1) | async-done | bytes 327712 | tf_op jit(solution)/shard_map/all_to_all | solution.py:415
  48.0 0.0 copy-start.1
  48.0 3.4 %copy-done.1 = bf16[1024,4096]{1,0:T(8,128)(2,1)S(1)} copy-done((bf16[1024,4096]{1,0:T(8,128)(2,1)S(1)}, bf16[1024,4096]{1,0:T(8,128)(2,1)}, u32[]{:S(2)}) %copy-start.1) | copy-done | bytes 8388632
  51.4 0.0 copy-start.5
  51.4 1.1 %copy-done.5 = f32[72,16,128]{2,1,0:T(8,128)S(1)} copy-done((f32[72,16,128]{2,1,0:T(8,128)S(1)}, f32[72,16,128]{2,1,0:T(8,128)}, u32[]{:S(2)}) %copy-start.5) | copy-done | bytes 589848
  52.4 3.2 %shard_map.103 = bf16[8,16,512]{2,1,0:T(8,128)(2,1)S(1)} custom-call(s32[32]{0:T(128)} %entry_h.5, s32[32]{0:T(128)} %bitcast.13, bf16[32,40,128]{2,1,0:T(8,128)(2,1)S(1)} %all-to-all-done.1.back, f32[72,16,128]{2,1,0:T(8,128)S(1)} %get-tuple-element.14.o_home, f32[72,16,128]{2,1,0:T(8,128)S(1)} %copy-done.5, bf16[1024,4096]{1,0:T(8,128)(2,1)S(1)} %copy-done.1), custom_call_target="tpu_custom_call" | custom-call | tf_op jit(solution)/shard_map/pallas_call | solution.py:417
  55.6 13.3 %all_to_all.16.parts = bf16[8,16,512]{2,1,0:T(8,128)(2,1)} all-to-all(bf16[8,16,512]{2,1,0:T(8,128)(2,1)S(1)} %shard_map.103), channel_id=1, replica_groups=mesh['inst'=32,'tp'=8] {'tp'}, dimensions={0} | all-to-all | bytes 262144 | tf_op jit(solution)/shard_map/all_to_all | solution.py:435
  69.0 1.5 %shard_map.104 = bf16[8,2,512]{2,1,0:T(2,128)(2,1)} custom-call(bf16[8,16,512]{2,1,0:T(8,128)(2,1)} %all_to_all.16.parts), custom_call_target="tpu_custom_call" | custom-call | tf_op jit(solution)/shard_map/pallas_call | solution.py:437
Async XLA Ops:
  26.5 10.3 %copy-start.6 = (bf16[8,2,8,128]{3,2,1,0:T(8,128)(2,1)S(1)}, bf16[8,2,8,128]{3,2,1,0:T(8,128)(2,1)}, u32[]{:S(2)}) copy-start(bf16[8,2,8,128]{3,2,1,0:T(8,128)(2,1)} %param.10) | copy-start | bytes 98308
  26.5 10.3 %copy-start.7 = (bf16[8,2,1,128]{3,1,2,0:T(2,128)(2,1)S(1)}, bf16[8,2,1,128]{3,1,2,0:T(2,128)(2,1)}, u32[]{:S(2)}) copy-start(bf16[8,2,1,128]{3,1,2,0:T(2,128)(2,1)} %param.11) | copy-start | bytes 12292
  26.5 10.3 %copy-start.8 = (bf16[8,2,1,128]{3,1,2,0:T(2,128)(2,1)S(1)}, bf16[8,2,1,128]{3,1,2,0:T(2,128)(2,1)}, u32[]{:S(2)}) copy-start(bf16[8,2,1,128]{3,1,2,0:T(2,128)(2,1)} %param.12) | copy-start | bytes 12292
  29.7 1.3 %copy-start.2 = (bf16[64,128,128]{2,1,0:T(8,128)(2,1)}, bf16[64,128,128]{2,1,0:T(8,128)(2,1)S(1)}, u32[]{:S(2)}) copy-start(bf16[64,128,128]{2,1,0:T(8,128)(2,1)S(1)} %get-tuple-element.13.vp) | copy-start | bytes 6291460
  31.0 17.0 %all-to-all-start.1 = ((bf16[32,40,128]{2,1,0:T(8,128)(2,1)}), bf16[32,40,128]{2,1,0:T(8,128)(2,1)S(1)}, u32[]{:S(2)}, u32[]{:S(2)}) async-start(bf16[32,40,128]{2,1,0:T(8,128)(2,1)} %shard_map.101), calls=%async_computation.1 | async-start | bytes 655360 | tf_op jit(solution)/shard_map/all_to_all | solution.py:415
  36.8 1.6 %copy-start.3 = (bf16[64,128,128]{2,1,0:T(8,128)(2,1)S(1)}, bf16[64,128,128]{2,1,0:T(8,128)(2,1)}, u32[]{:S(2)}) copy-start(bf16[64,128,128]{2,1,0:T(8,128)(2,1)} %copy-done.2) | copy-start | bytes 6291460
  41.8 3.2 %copy-start = (bf16[1024,4096]{1,0:T(8,128)(2,1)}, bf16[1024,4096]{1,0:T(8,128)(2,1)S(1)}, u32[]{:S(2)}) copy-start(bf16[1024,4096]{1,0:T(8,128)(2,1)S(1)} %get-tuple-element.16.w) | copy-start | bytes 25165828
  45.0 0.9 %copy-start.4 = (f32[72,16,128]{2,1,0:T(8,128)}, f32[72,16,128]{2,1,0:T(8,128)S(1)}, u32[]{:S(2)}) copy-start(f32[72,16,128]{2,1,0:T(8,128)S(1)} %get-tuple-element.15.z_home) | copy-start | bytes 1769476
  48.0 3.4 %copy-start.1 = (bf16[1024,4096]{1,0:T(8,128)(2,1)S(1)}, bf16[1024,4096]{1,0:T(8,128)(2,1)}, u32[]{:S(2)}) copy-start(bf16[1024,4096]{1,0:T(8,128)(2,1)} %copy-done) | copy-start | bytes 25165828
  51.4 1.1 %copy-start.5 = (f32[72,16,128]{2,1,0:T(8,128)S(1)}, f32[72,16,128]{2,1,0:T(8,128)}, u32[]{:S(2)}) copy-start(f32[72,16,128]{2,1,0:T(8,128)} %copy-done.4) | copy-start | bytes 1769476

commit v3 on v2

--- a/solution.py
+++ b/solution.py
@@ -184,18 +184,26 @@
     lax.fori_loop(0, peers, lay, 0, unroll=4)
 
 
+def weigh(states):
+    top = functools.reduce(jnp.maximum, [z for _, z in states])
+    shares = [jnp.exp(z - top) for _, z in states]
+    total = functools.reduce(jnp.add, shares)
+    o = functools.reduce(jnp.add, [f * o for f, (o, _) in zip(shares, states)])
+    return o / total, top, total
+
+
 def home_kernel(
-    entry_h, table_h, lengths_h, w_h, q, nk, nv, kp, vp,
-    o_out, z_out, w,
-    entry, table, lengths, lent, ids, scores, sems,
+    entry_h, table_h, lengths_h, kp_h, vp_h, q, nk, nv,
+    o_out, z_out,
+    entry, table, lengths, kp, vp, o_part, z_part, lent, ids, scores, sems,
 ):
     requests, blocks = table.shape
     entries = requests * blocks
     copies = fetch_all(
-        [(entry_h, entry), (table_h, table), (lengths_h, lengths), (w_h, w)], sems
+        [(entry_h, entry), (table_h, table), (lengths_h, lengths), (kp_h, kp), (vp_h, vp)], sems
     )
-    z_out[...] = jnp.full(z_out.shape, DEAD, F32)
-    o_out[...] = jnp.zeros(o_out.shape, F32)
+    z_part[...] = jnp.full(z_part.shape, DEAD, F32)
+    o_part[...] = jnp.zeros(o_part.shape, F32)
 
     def clear(i, _):
         lent[i] = 0
@@ -230,9 +238,11 @@
         return lengths[e // blocks] - (e % blocks) * 128
 
     def store(item, o, z):
-        o_out[ids[item]] = o
-        z_out[ids[item]] = z
-
+        o_part[ids[item]] = o
+        z_part[ids[item]] = z
+
+    for c in copies[3:]:
+        c.wait()
     attend(n, query, slot_of, live_of, store, kp, vp, scores)
     scale = 128**-0.5
     second = lax.broadcasted_iota(jnp.int32, (ROWS, 1), 0) >= HALF
@@ -247,22 +257,24 @@
         p0 = jnp.exp(s0 - m)
         p1 = jnp.where(second, jnp.exp(s1 - m), 0.0)
         l = p0 + p1
-        o_out[entries + r] = (p0 * v[0:1] + p1 * v[1:2]) / l
-        z_out[entries + r] = jnp.broadcast_to(m + jnp.log(l), (ROWS, 128))
-    copies[3].wait()
+        fresh = ((p0 * v[0:1] + p1 * v[1:2]) / l, jnp.broadcast_to(m + jnp.log(l), (ROWS, 128)))
+        o, top, total = weigh([fresh] + [(o_part[r * 8 + b], z_part[r * 8 + b]) for b in range(8)])
+        o_out[r] = o
+        z_out[r] = top + jnp.log(total)
 
 
 def merge_kernel(
-    entry_h, target_h, back, o_home, z_home, w,
+    entry_h, target_h, w_h, back, o_home, z_home,
     out,
-    entry, target, o_all, z_all, z_back, att, count, sems,
+    entry, target, w, o_all, z_all, z_back, att, count, sems,
 ):
-    requests = o_home.shape[0] // 9
-    entries = requests * 8
+    requests = o_home.shape[0]
     peers = back.shape[0]
-    copies = fetch_all([(entry_h, entry), (target_h, target)], sems)
-    o_all[...] = o_home[...]
-    z_all[...] = z_home[...]
+    width = out.shape[2]
+    chunks = [(w_h.at[:, pl.ds(i * width, width)], w.at[i]) for i in range(out.shape[0])]
+    copies = fetch_all([(entry_h, entry), (target_h, target)] + chunks, sems)
+    o_all[...] = jnp.zeros(o_all.shape, F32)
+    z_all[...] = jnp.full(z_all.shape, DEAD, F32)
     side = back[...][:, CAP * ROWS :, :].reshape(peers * HALF, 128)
     kinds = 2 * CAP
     lane = lax.broadcasted_iota(jnp.int32, (128, kinds * 128), 0)
@@ -275,7 +287,7 @@
         return 0
 
     lax.fori_loop(0, peers, clear, 0, unroll=8)
-    for c in copies:
+    for c in copies[:2]:
         c.wait()
 
     def fetch(j, _):
@@ -292,24 +304,15 @@
 
     lax.fori_loop(0, entry.shape[0], fetch, 0, unroll=4)
     for r in range(requests):
-        z = [z_all[r * 8 + b] for b in range(8)] + [z_all[entries + r]]
-        o = [o_all[r * 8 + b] for b in range(8)] + [o_all[entries + r]]
-        m = functools.reduce(jnp.maximum, z)
-        f = [jnp.exp(x - m) for x in z]
-        top = functools.reduce(jnp.add, [a * b for a, b in zip(f, o)])
-        att[r * ROWS : (r + 1) * ROWS, :] = top / functools.reduce(jnp.add, f)
+        parts = [(o_home[r], z_home[r])] + [(o_all[r * 8 + b], z_all[r * 8 + b]) for b in range(8)]
+        att[r * ROWS : (r + 1) * ROWS, :] = weigh(parts)[0]
     heads = ROWS // 2
     a = jnp.concatenate(
         [att[pl.ds(g, 2 * requests, stride=heads), :].astype(BF) for g in range(heads)], axis=1
     )
-    width = out.shape[2]
-
-    def project(p, _):
-        cols = pl.ds(pl.multiple_of(p * width, width), width)
-        out[p] = jnp.dot(a, w[:, cols], preferred_element_type=F32).astype(BF)
-        return 0
-
-    lax.fori_loop(0, out.shape[0], project, 0)
+    for i, c in enumerate(copies[2:]):
+        c.wait()
+        out[i] = jnp.dot(a, w[i], preferred_element_type=F32).astype(BF)
 
 
 def sum_kernel(parts, out):
@@ -344,8 +347,8 @@
     q = queries.reshape(requests, steps * heads, size)
     nk = new_keys.reshape(requests, steps, size)
     nv = new_values.reshape(requests, steps, size)
-    kp = key_pool.reshape(pool, 128, size)
-    vp = value_pool.reshape(pool, 128, size)
+    k_hbm = key_pool.reshape(pool, 128, size)
+    v_hbm = value_pool.reshape(pool, 128, size)
     target = lend_target.reshape(lends)
     held = lambda x: pltpu.with_memory_space_constraint(x, pltpu.HBM)
     smem = lambda *n: pltpu.SMEM(n, jnp.int32)
@@ -355,7 +358,7 @@
 
     send, kp, vp = pl.pallas_call(
         pack_kernel,
-        out_shape=(jax.ShapeDtypeStruct((peers, SLAB, size), BF), like(kp), like(vp)),
+        out_shape=(jax.ShapeDtypeStruct((peers, SLAB, size), BF), like(k_hbm), like(v_hbm)),
         in_specs=[HB] * 7,
         out_specs=(VM, VM, VM),
         scratch_shapes=[
@@ -371,28 +374,32 @@
             sems(7),
         ],
         compiler_params=params(16),
-    )(*map(held, (lend_entry, target, block_table, lengths, q, kp, vp)))
+    )(*map(held, (lend_entry, target, block_table, lengths, q, k_hbm, v_hbm)))
 
     recv = lax.all_to_all(send, "inst", split_axis=0, concat_axis=0, tiled=True)
 
-    tile_state = jax.ShapeDtypeStruct((entries + requests, ROWS, size), F32)
-    o_home, z_home, weight = pl.pallas_call(
+    tile_state = jax.ShapeDtypeStruct((requests, ROWS, size), F32)
+    o_home, z_home = pl.pallas_call(
         home_kernel,
-        out_shape=(tile_state, tile_state, like(out_weight)),
-        in_specs=[HB] * 4 + [VM] * 5,
-        out_specs=(VM, VM, VM),
+        out_shape=(tile_state, tile_state),
+        in_specs=[HB] * 5 + [VM] * 3,
+        out_specs=(VM, VM),
         scratch_shapes=[
             smem(lends),
             smem(*block_table.shape),
             smem(requests),
+            pltpu.VMEM(k_hbm.shape, BF),
+            pltpu.VMEM(v_hbm.shape, BF),
+            pltpu.VMEM((entries, ROWS, size), F32),
+            pltpu.VMEM((entries, ROWS, size), F32),
             smem(entries),
             smem(entries + 1),
             scores,
-            sems(4),
+            sems(5),
         ],
         compiler_params=params(24),
         cost_estimate=pl.CostEstimate(flops=10**9, bytes_accessed=16 * 2**20, transcendentals=0),
-    )(*map(held, (lend_entry, block_table, lengths, out_weight)), q, nk, nv, kp, vp)
+    )(*map(held, (lend_entry, block_table, lengths, k_hbm, v_hbm)), q, nk, nv)
 
     back = pl.pallas_call(
         serve_kernel,
@@ -417,20 +424,21 @@
     partial = pl.pallas_call(
         merge_kernel,
         out_shape=jax.ShapeDtypeStruct((parts, requests * steps, out_weight.shape[1] // parts), BF),
-        in_specs=[HB] * 2 + [VM] * 4,
+        in_specs=[HB] * 3 + [VM] * 3,
         out_specs=VM,
         scratch_shapes=[
             smem(lends),
             smem(lends),
-            pltpu.VMEM(tile_state.shape, F32),
-            pltpu.VMEM(tile_state.shape, F32),
+            pltpu.VMEM((parts, out_weight.shape[0], out_weight.shape[1] // parts), BF),
+            pltpu.VMEM((entries, ROWS, size), F32),
+            pltpu.VMEM((entries, ROWS, size), F32),
             pltpu.VMEM((peers * HALF, 2 * CAP * 128), F32),
             pltpu.VMEM((requests * ROWS, size), F32),
             smem(peers),
-            sems(2),
+            sems(2 + parts),
         ],
         compiler_params=params(24),
-    )(held(lend_entry), held(target), mine, o_home, z_home, weight)
+    )(*map(held, (lend_entry, target, out_weight)), mine, o_home, z_home)
 
     shares = lax.all_to_all(partial, "tp", split_axis=0, concat_axis=0, tiled=True)
 
@@ -439,6 +447,7 @@
         out_shape=jax.ShapeDtypeStruct((requests, steps, shares.shape[2]), BF),
         in_specs=[VM],
         out_specs=VM,
+        compiler_params=params(8),
     )(shares)
 
 

time: 71.1 us -> 65 us (0.914)
  local copies, waits for them, and re-layouts: 11.4 us -> 0.01 us
  waiting for transfers between devices: 2.1 us -> 8.44 us
  blocking collectives: 37.6 us -> 36.1 us
    unnamed x18 -> x6, local copies, waits for them, and re-layouts: 11.4 us -> 0.01 us
    all_to_all x1, waiting for transfers between devices: 2.1 us -> 8.44 us  [on_device(): mine = lax.all_to_all(back, 'inst', split_axis=0, concat_axis=0, tiled=True)]
    all_to_all x1, blocking collectives: 13.3 us -> 11.9 us  [on_device(): lax.all_to_all(partial, 'tp', split_axis=0, concat_axis=0, tiled=True)]
    pallas_call x1, Pallas kernels: 1.53 us -> 0.63 us  [on_device(): pl.pallas_call(sum_kernel, out_shape=jax.ShapeDtypeStruct((requests, step...]
  transfers between devices with their start and end apart: 1 -> 1, of which waited for: 1 -> 1; matrix products, arithmetic and copies ran while one was open for 0% -> 0% of each run, Pallas kernels for 5% -> 6%
where the time goes in v3:
time: 65 us; the launch traced here: 64.7 us
  blocking collectives  36.1 us (56%)
  Pallas kernels  13.9 us (21%)
  waiting for transfers between devices  8.44 us (13%)
  starting transfers between devices  6.2 us (10%)
    all_to_all x1, blocking collectives, on_device(): recv = lax.all_to_all(send, 'inst', split_axis=0, concat_axis=0, tiled=True)  24.2 us
    all_to_all x1, blocking collectives, on_device(): lax.all_to_all(partial, 'tp', split_axis=0, concat_axis=0, tiled=True)  11.9 us
    all_to_all x1, waiting for transfers between devices, on_device(): mine = lax.all_to_all(back, 'inst', split_axis=0, concat_axis=0, tiled=True)  8.44 us
    all_to_all x1, starting transfers between devices, on_device(): mine = lax.all_to_all(back, 'inst', split_axis=0, concat_axis=0, tiled=True)  6.2 us
    pallas_call x1, Pallas kernels, on_device(): pl.pallas_call(home_kernel, out_shape=(tile_state, tile_state), in_specs=...  3.99 us
    pallas_call x1, Pallas kernels, on_device(): pl.pallas_call(merge_kernel, out_shape=jax.ShapeDtypeStruct((parts, reque...  3.81 us
    pallas_call x1, Pallas kernels, on_device(): pl.pallas_call(serve_kernel, out_shape=jax.ShapeDtypeStruct((peers, SLAB,...  3.16 us
    pallas_call x1, Pallas kernels, on_device(): pl.pallas_call(pack_kernel, out_shape=(jax.ShapeDtypeStruct((peers, SLAB,...  2.3 us
  transfers between devices with their start and end apart: 1, of which 1 were waited for; matrix products, arithmetic and copies ran while one was open for 0% of the time, Pallas kernels for 6%

profile of v3, /device:TPU:1, one launch (start us, length us, event | category | flops | bytes accessed | tf_op | source)
XLA Modules:
  0.0 64.7 jit_solution(17712281377283483787)
XLA Ops:
  0.0 2.3 %shard_map.100 = (bf16[32,40,128]{2,1,0:T(8,128)(2,1)S(1)}, bf16[64,128,128]{2,1,0:T(8,128)(2,1)S(1)}, bf16[64,128,128]{2,1,0:T(8,128)(2,1)S(1)}) custom-call(s32[32]{0:T(128)} %entry_h.5, s32[32]{0:T(128)} %bitcast.14, s32[8,8]{1,0:T(8,128)} %table_h.3, s32[8]{0:T(128)} %lengths_h.3, bf16[8,16,128]{2,1,0:T(8,128)(2,1)} %bitcast.6, ...), custom_call_target="tpu_custom_call" | custom-call | tf_op jit(solution)/shard_map/pallas_call | solution.py:359
  2.3 24.2 %all_to_all.15.recv = bf16[32,40,128]{2,1,0:T(8,128)(2,1)S(1)} all-to-all(bf16[32,40,128]{2,1,0:T(8,128)(2,1)S(1)} %get-tuple-element.10), channel_id=1, replica_groups=mesh['inst'=32,'tp'=8] {'inst'}, dimensions={0} | all-to-all | bytes 655360 | tf_op jit(solution)/shard_map/all_to_all | solution.py:379
  26.5 0.0 copy-start
  26.5 0.0 copy-start.1
  26.5 0.0 copy-start.2
  26.5 3.2 %shard_map.101 = bf16[32,40,128]{2,1,0:T(8,128)(2,1)} custom-call(bf16[32,40,128]{2,1,0:T(8,128)(2,1)S(1)} %all_to_all.15.recv, bf16[64,128,128]{2,1,0:T(8,128)(2,1)S(1)} %get-tuple-element.11.kp, bf16[64,128,128]{2,1,0:T(8,128)(2,1)S(1)} %get-tuple-element.12.vp), custom_call_target="tpu_custom_call" | custom-call | tf_op jit(solution)/shard_map/pallas_call | solution.py:404
  29.7 6.2 %all-to-all-start.1 = ((bf16[32,40,128]{2,1,0:T(8,128)(2,1)}), bf16[32,40,128]{2,1,0:T(8,128)(2,1)S(1)}, u32[]{:S(2)}, u32[]{:S(2)}) async-start(bf16[32,40,128]{2,1,0:T(8,128)(2,1)} %shard_map.101), calls=%async_computation.1 | async-start | bytes 655360 | tf_op jit(solution)/shard_map/all_to_all | solution.py:422
  35.9 0.0 copy-done
  35.9 0.0 copy-done.1
  35.9 0.0 copy-done.2
  35.9 4.0 %shard_map.102 = (f32[8,16,128]{2,1,0:T(8,128)S(1)}, f32[8,16,128]{2,1,0:T(8,128)S(1)}) custom-call(s32[32]{0:T(128)} %entry_h.5, s32[8,8]{1,0:T(8,128)} %table_h.3, s32[8]{0:T(128)} %lengths_h.3, bf16[64,128,128]{2,1,0:T(8,128)(2,1)} %bitcast.11, bf16[64,128,128]{2,1,0:T(8,128)(2,1)} %bitcast.13, bf16[8,16,128]{2,1,0:T(8,128)(2,1)S(1)} %bitcast.7, ...), custom_call_target="tpu_custom_call" | custom-call | flops 1000000000 | bytes 16777216 | tf_op jit(solution)/shard_map/pallas_call | solution.py:382
  39.9 8.4 %all-to-all-done.1.back = bf16[32,40,128]{2,1,0:T(8,128)(2,1)S(1)} async-done(((bf16[32,40,128]{2,1,0:T(8,128)(2,1)}), bf16[32,40,128]{2,1,0:T(8,128)(2,1)S(1)}, u32[]{:S(2)}, u32[]{:S(2)}) %all-to-all-start.1) | async-done | bytes 327712 | tf_op jit(solution)/shard_map/all_to_all | solution.py:422
  48.4 3.8 %shard_map.103 = bf16[8,16,512]{2,1,0:T(8,128)(2,1)S(1)} custom-call(s32[32]{0:T(128)} %entry_h.5, s32[32]{0:T(128)} %bitcast.15, bf16[1024,4096]{1,0:T(8,128)(2,1)} %w_h.1, bf16[32,40,128]{2,1,0:T(8,128)(2,1)S(1)} %all-to-all-done.1.back, f32[8,16,128]{2,1,0:T(8,128)S(1)} %get-tuple-element.13.o_home, f32[8,16,128]{2,1,0:T(8,128)S(1)} %get-tuple-element.14.z_home), custom_call_target="tpu_custom_call" | custom-call | tf_op jit(solution)/shard_map/pallas_call | solution.py:424
  52.2 11.9 %all_to_all.16.parts = bf16[8,16,512]{2,1,0:T(8,128)(2,1)S(1)} all-to-all(bf16[8,16,512]{2,1,0:T(8,128)(2,1)S(1)} %shard_map.103), channel_id=1, replica_groups=mesh['inst'=32,'tp'=8] {'tp'}, dimensions={0} | all-to-all | bytes 262144 | tf_op jit(solution)/shard_map/all_to_all | solution.py:443
  64.1 0.6 shard_map.104
Async XLA Ops:
  26.5 9.4 %copy-start = (bf16[8,2,8,128]{3,2,1,0:T(8,128)(2,1)S(1)}, bf16[8,2,8,128]{3,2,1,0:T(8,128)(2,1)}, u32[]{:S(2)}) copy-start(bf16[8,2,8,128]{3,2,1,0:T(8,128)(2,1)} %param.10) | copy-start | bytes 98308
  26.5 9.4 %copy-start.1 = (bf16[8,2,1,128]{3,1,2,0:T(2,128)(2,1)S(1)}, bf16[8,2,1,128]{3,1,2,0:T(2,128)(2,1)}, u32[]{:S(2)}) copy-start(bf16[8,2,1,128]{3,1,2,0:T(2,128)(2,1)} %param.11) | copy-start | bytes 12292
  26.5 9.4 %copy-start.2 = (bf16[8,2,1,128]{3,1,2,0:T(2,128)(2,1)S(1)}, bf16[8,2,1,128]{3,1,2,0:T(2,128)(2,1)}, u32[]{:S(2)}) copy-start(bf16[8,2,1,128]{3,1,2,0:T(2,128)(2,1)} %param.12) | copy-start | bytes 12292
  29.7 18.7 %all-to-all-start.1 = ((bf16[32,40,128]{2,1,0:T(8,128)(2,1)}), bf16[32,40,128]{2,1,0:T(8,128)(2,1)S(1)}, u32[]{:S(2)}, u32[]{:S(2)}) async-start(bf16[32,40,128]{2,1,0:T(8,128)(2,1)} %shard_map.101), calls=%async_computation.1 | async-start | bytes 655360 | tf_op jit(solution)/shard_map/all_to_all | solution.py:422

commit v4 on v3

--- a/solution.py
+++ b/solution.py
@@ -31,14 +31,14 @@
 
 
 def pack_kernel(
-    entry_h, target_h, table_h, lengths_h, q_h, kp_h, vp_h,
-    send, kp, vp,
+    entry_h, target_h, table_h, lengths_h, q_h, kp_h,
+    send, kp,
     entry, target, table, lengths, q, tiles, count, slots, lives, sems,
 ):
     peers = send.shape[0]
     blocks = table.shape[1]
     small = fetch_all(
-        [(entry_h, entry), (target_h, target), (table_h, table), (lengths_h, lengths), (q_h, q), (kp_h, kp), (vp_h, vp)],
+        [(entry_h, entry), (target_h, target), (table_h, table), (lengths_h, lengths), (q_h, q), (kp_h, kp)],
         sems,
     )
 
@@ -84,7 +84,7 @@
         c.wait()
 
 
-def attend(n, query, slot_of, live_of, store, kp, vp, scores):
+def attend(n, query, slot_of, live_of, store, kp, vp, scores, ready):
     scale = 128**-0.5
     groups = (n + GROUP - 1) // GROUP
     lane = lane_iota()
@@ -107,6 +107,8 @@
     def _():
         for i, s in enumerate(score(0)):
             scores[0, i] = s
+
+    ready()
 
     def work(g, _):
         now = lax.rem(g, 2)
@@ -130,12 +132,21 @@
     lax.fori_loop(0, groups, work, 0)
 
 
-def serve_kernel(recv, kp, vp, back, side_f, side_i, side_s, ids, att, lse, scores, sem):
+def serve_kernel(
+    vp_h, w_h, recv, kp, after,
+    back, w,
+    vp, side_f, side_i, side_s, ids, att, lse, scores, sems,
+):
     peers = recv.shape[0]
+    values = pltpu.make_async_copy(vp_h, vp, sems.at[1])
+    values.start()
+    width = w.shape[2]
+    chunks = [(w_h.at[:, pl.ds(i * width, width)], w.at[i]) for i in range(w.shape[0])]
+    weights = fetch_all(chunks, sems.at[pl.ds(2, len(chunks))])
     side = recv[...][:, CAP * ROWS :, :].astype(F32)
     side_f[...] = side.reshape(peers * HALF, 128)
     side_i[...] = side_f[pl.ds(0, peers, stride=HALF), :].astype(jnp.int32)
-    copy = pltpu.make_async_copy(side_i, side_s, sem)
+    copy = pltpu.make_async_copy(side_i, side_s, sems.at[0])
     copy.start()
     att[...] = jnp.zeros(att.shape, F32)
     lse[...] = jnp.full(lse.shape, DEAD, F32)
@@ -151,21 +162,21 @@
 
     def query(item):
         i = ids[item]
-        return recv[i // CAP, pl.ds(pl.multiple_of((i % CAP) * ROWS, ROWS), ROWS), :]
+        return recv[lax.shift_right_logical(i, 1), pl.ds(pl.multiple_of((i & 1) * ROWS, ROWS), ROWS), :]
 
     def slot_of(item):
         i = ids[item]
-        return side_s[i // CAP, 2 * (i % CAP)]
+        return side_s[lax.shift_right_logical(i, 1), 2 * (i & 1)]
 
     def live_of(item):
         i = ids[item]
-        return side_s[i // CAP, 2 * (i % CAP) + 1]
+        return side_s[lax.shift_right_logical(i, 1), 2 * (i & 1) + 1]
 
     def store(item, o, z):
         att[ids[item]] = o
         lse[ids[item]] = z
 
-    attend(n, query, slot_of, live_of, store, kp, vp, scores)
+    attend(n, query, slot_of, live_of, store, kp, vp, scores, values.wait)
     lane = lane_iota(HALF)
 
     def lay(i, _):
@@ -182,6 +193,8 @@
         return 0
 
     lax.fori_loop(0, peers, lay, 0, unroll=4)
+    for c in weights:
+        c.wait()
 
 
 def weigh(states):
@@ -241,9 +254,8 @@
         o_part[ids[item]] = o
         z_part[ids[item]] = z
 
-    for c in copies[3:]:
-        c.wait()
-    attend(n, query, slot_of, live_of, store, kp, vp, scores)
+    copies[3].wait()
+    attend(n, query, slot_of, live_of, store, kp, vp, scores, copies[4].wait)
     scale = 128**-0.5
     second = lax.broadcasted_iota(jnp.int32, (ROWS, 1), 0) >= HALF
     for r in range(requests):
@@ -264,14 +276,15 @@
 
 
 def merge_kernel(
-    entry_h, target_h, w_h, back, o_home, z_home,
+    entry_h, target_h, w_h, w_early, back, o_home, z_home,
     out,
     entry, target, w, o_all, z_all, z_back, att, count, sems,
 ):
     requests = o_home.shape[0]
     peers = back.shape[0]
     width = out.shape[2]
-    chunks = [(w_h.at[:, pl.ds(i * width, width)], w.at[i]) for i in range(out.shape[0])]
+    early = w_early.shape[0]
+    chunks = [(w_h.at[:, pl.ds((early + i) * width, width)], w.at[i]) for i in range(w.shape[0])]
     copies = fetch_all([(entry_h, entry), (target_h, target)] + chunks, sems)
     o_all[...] = jnp.zeros(o_all.shape, F32)
     z_all[...] = jnp.full(z_all.shape, DEAD, F32)
@@ -310,9 +323,11 @@
     a = jnp.concatenate(
         [att[pl.ds(g, 2 * requests, stride=heads), :].astype(BF) for g in range(heads)], axis=1
     )
-    for i, c in enumerate(copies[2:]):
-        c.wait()
-        out[i] = jnp.dot(a, w[i], preferred_element_type=F32).astype(BF)
+    for i in range(out.shape[0]):
+        if i >= early:
+            copies[2 + i - early].wait()
+        block = w_early[i] if i < early else w[i - early]
+        out[i] = jnp.dot(a, block, preferred_element_type=F32).astype(BF)
 
 
 def sum_kernel(parts, out):
@@ -356,11 +371,11 @@
     like = lambda x: jax.ShapeDtypeStruct(x.shape, x.dtype)
     scores = pltpu.VMEM((2, GROUP, ROWS, 128), F32)
 
-    send, kp, vp = pl.pallas_call(
+    send, kp = pl.pallas_call(
         pack_kernel,
-        out_shape=(jax.ShapeDtypeStruct((peers, SLAB, size), BF), like(k_hbm), like(v_hbm)),
-        in_specs=[HB] * 7,
-        out_specs=(VM, VM, VM),
+        out_shape=(jax.ShapeDtypeStruct((peers, SLAB, size), BF), like(k_hbm)),
+        in_specs=[HB] * 6,
+        out_specs=(VM, VM),
         scratch_shapes=[
             smem(lends),
             smem(lends),
@@ -371,10 +386,10 @@
             smem(peers),
             smem(peers * CAP),
             smem(peers * CAP),
-            sems(7),
+            sems(6),
         ],
         compiler_params=params(16),
-    )(*map(held, (lend_entry, target, block_table, lengths, q, k_hbm, v_hbm)))
+    )(*map(held, (lend_entry, target, block_table, lengths, q, k_hbm)))
 
     recv = lax.all_to_all(send, "inst", split_axis=0, concat_axis=0, tiled=True)
 
@@ -401,12 +416,18 @@
         cost_estimate=pl.CostEstimate(flops=10**9, bytes_accessed=16 * 2**20, transcendentals=0),
     )(*map(held, (lend_entry, block_table, lengths, k_hbm, v_hbm)), q, nk, nv)
 
-    back = pl.pallas_call(
+    width = out_weight.shape[1] // parts
+    early = parts // 2
+    back, w_early = pl.pallas_call(
         serve_kernel,
-        out_shape=jax.ShapeDtypeStruct((peers, SLAB, size), BF),
-        in_specs=[VM, VM, VM],
-        out_specs=VM,
+        out_shape=(
+            jax.ShapeDtypeStruct((peers, SLAB, size), BF),
+            jax.ShapeDtypeStruct((early, out_weight.shape[0], width), BF),
+        ),
+        in_specs=[HB, HB, VM, VM, VM],
+        out_specs=(VM, VM),
         scratch_shapes=[
+            pltpu.VMEM(v_hbm.shape, BF),
             pltpu.VMEM((peers * HALF, 128), F32),
             pltpu.VMEM((peers, 128), jnp.int32),
             smem(peers, 128),
@@ -414,31 +435,31 @@
             pltpu.VMEM((peers * CAP, ROWS, 128), F32),
             pltpu.VMEM((peers * CAP, ROWS, 128), F32),
             scores,
-            pltpu.SemaphoreType.DMA,
+            sems(2 + early),
         ],
-        compiler_params=params(16),
-    )(recv, kp, vp)
+        compiler_params=params(24),
+    )(held(v_hbm), held(out_weight), recv, kp, z_home)
 
     mine = lax.all_to_all(back, "inst", split_axis=0, concat_axis=0, tiled=True)
 
     partial = pl.pallas_call(
         merge_kernel,
         out_shape=jax.ShapeDtypeStruct((parts, requests * steps, out_weight.shape[1] // parts), BF),
-        in_specs=[HB] * 3 + [VM] * 3,
+        in_specs=[HB] * 3 + [VM] * 4,
         out_specs=VM,
         scratch_shapes=[
             smem(lends),
             smem(lends),
-            pltpu.VMEM((parts, out_weight.shape[0], out_weight.shape[1] // parts), BF),
+            pltpu.VMEM((parts - early, out_weight.shape[0], width), BF),
             pltpu.VMEM((entries, ROWS, size), F32),
             pltpu.VMEM((entries, ROWS, size), F32),
             pltpu.VMEM((peers * HALF, 2 * CAP * 128), F32),
             pltpu.VMEM((requests * ROWS, size), F32),
             smem(peers),
-            sems(2 + parts),
+            sems(2 + parts - early),
         ],
         compiler_params=params(24),
-    )(*map(held, (lend_entry, target, out_weight)), mine, o_home, z_home)
+    )(*map(held, (lend_entry, target, out_weight)), w_early, mine, o_home, z_home)
 
     shares = lax.all_to_all(partial, "tp", split_axis=0, concat_axis=0, tiled=True)
 

time: 65 us -> 63.2 us (0.972)
  blocking collectives: 36.1 us -> 29.7 us
  starting transfers between devices: 6.2 us -> 11.9 us
  Pallas kernels: 13.9 us -> 12.6 us
    all_to_all x1, blocking collectives: 24.2 us -> 15.4 us  [on_device(): mine = lax.all_to_all(back, 'inst', split_axis=0, concat_axis=0, tiled=True)]
    all_to_all x1, starting transfers between devices: 6.2 us -> 11.9 us  [on_device(): recv = lax.all_to_all(send, 'inst', split_axis=0, concat_axis=0, tiled=True)]
    all_to_all x1, blocking collectives: 11.9 us -> 14.3 us  [on_device(): lax.all_to_all(partial, 'tp', split_axis=0, concat_axis=0, tiled=True)]
    pallas_call x1, Pallas kernels: 3.81 us -> 2.81 us  [on_device(): pl.pallas_call(merge_kernel, out_shape=jax.ShapeDtypeStruct((parts, reque...]
where the time goes in v4:
time: 63.2 us; the launch traced here: 63 us
  blocking collectives  29.7 us (47%)
  Pallas kernels  12.6 us (20%)
  starting transfers between devices  11.9 us (19%)
  waiting for transfers between devices  8.78 us (14%)
    all_to_all x1, blocking collectives, on_device(): mine = lax.all_to_all(back, 'inst', split_axis=0, concat_axis=0, tiled=True)  15.4 us
    all_to_all x1, blocking collectives, on_device(): lax.all_to_all(partial, 'tp', split_axis=0, concat_axis=0, tiled=True)  14.3 us
    all_to_all x1, starting transfers between devices, on_device(): recv = lax.all_to_all(send, 'inst', split_axis=0, concat_axis=0, tiled=True)  11.9 us
    all_to_all x1, waiting for transfers between devices, on_device(): recv = lax.all_to_all(send, 'inst', split_axis=0, concat_axis=0, tiled=True)  8.78 us
    pallas_call x1, Pallas kernels, on_device(): pl.pallas_call(home_kernel, out_shape=(tile_state, tile_state), in_specs=...  3.73 us
    pallas_call x1, Pallas kernels, on_device(): pl.pallas_call(serve_kernel, out_shape=(jax.ShapeDtypeStruct((peers, SLAB...  3 us
    pallas_call x1, Pallas kernels, on_device(): pl.pallas_call(merge_kernel, out_shape=jax.ShapeDtypeStruct((parts, reque...  2.81 us
    pallas_call x1, Pallas kernels, on_device(): pl.pallas_call(pack_kernel, out_shape=(jax.ShapeDtypeStruct((peers, SLAB,...  2.43 us
  transfers between devices with their start and end apart: 1, of which 1 were waited for; matrix products, arithmetic and copies ran while one was open for 0% of the time, Pallas kernels for 6%

profile of v4, /device:TPU:1, one launch (start us, length us, event | category | flops | bytes accessed | tf_op | source)
XLA Modules:
  0.0 63.0 jit_solution(7369174006336488073)
XLA Ops:
  0.0 0.0 copy-start
  0.0 0.0 copy-start.2
  0.0 0.0 copy-start.1
  0.0 2.4 %shard_map.100 = (bf16[32,40,128]{2,1,0:T(8,128)(2,1)}, bf16[64,128,128]{2,1,0:T(8,128)(2,1)S(1)}) custom-call(s32[32]{0:T(128)} %entry_h.5, s32[32]{0:T(128)} %bitcast.14, s32[8,8]{1,0:T(8,128)} %table_h.3, s32[8]{0:T(128)} %lengths_h.3, bf16[8,16,128]{2,1,0:T(8,128)(2,1)} %bitcast.6, bf16[64,128,128]{2,1,0:T(8,128)(2,1)} %bitcast.12), custom_call_target="tpu_custom_call" | custom-call | tf_op jit(solution)/shard_map/pallas_call | solution.py:374
  2.4 11.9 %all-to-all-start = ((bf16[32,40,128]{2,1,0:T(8,128)(2,1)}), bf16[32,40,128]{2,1,0:T(8,128)(2,1)S(1)}, u32[]{:S(2)}, u32[]{:S(2)}) async-start(bf16[32,40,128]{2,1,0:T(8,128)(2,1)} %get-tuple-element.11), calls=%async_computation | async-start | bytes 655360 | tf_op jit(solution)/shard_map/all_to_all | solution.py:394
  14.3 0.0 copy-done
  14.3 0.0 copy-done.2
  14.3 0.0 copy-done.1
  14.4 3.7 %shard_map.101 = (f32[8,16,128]{2,1,0:T(8,128)S(1)}, f32[8,16,128]{2,1,0:T(8,128)S(1)}) custom-call(s32[32]{0:T(128)} %entry_h.5, s32[8,8]{1,0:T(8,128)} %table_h.3, s32[8]{0:T(128)} %lengths_h.3, bf16[64,128,128]{2,1,0:T(8,128)(2,1)} %bitcast.13, bf16[64,128,128]{2,1,0:T(8,128)(2,1)} %bitcast.10, bf16[8,16,128]{2,1,0:T(8,128)(2,1)S(1)} %bitcast.7, ...), custom_call_target="tpu_custom_call" | custom-call | flops 1000000000 | bytes 16777216 | tf_op jit(solution)/shard_map/pallas_call | solution.py:397
  18.1 8.8 %all-to-all-done.recv = bf16[32,40,128]{2,1,0:T(8,128)(2,1)S(1)} async-done(((bf16[32,40,128]{2,1,0:T(8,128)(2,1)}), bf16[32,40,128]{2,1,0:T(8,128)(2,1)S(1)}, u32[]{:S(2)}, u32[]{:S(2)}) %all-to-all-start) | async-done | bytes 327712 | tf_op jit(solution)/shard_map/all_to_all | solution.py:394
  26.9 3.0 %shard_map.102 = (bf16[32,40,128]{2,1,0:T(8,128)(2,1)S(1)}, bf16[4,1024,512]{2,1,0:T(8,128)(2,1)S(1)}) custom-call(bf16[64,128,128]{2,1,0:T(8,128)(2,1)} %bitcast.11, bf16[1024,4096]{1,0:T(8,128)(2,1)} %w_h.3, bf16[32,40,128]{2,1,0:T(8,128)(2,1)S(1)} %all-to-all-done.recv, bf16[64,128,128]{2,1,0:T(8,128)(2,1)S(1)} %get-tuple-element.12.kp, ...), custom_call_target="tpu_custom_call" | custom-call | tf_op jit(solution)/shard_map/pallas_call | solution.py:421
  29.9 15.4 %all_to_all.15.back = bf16[32,40,128]{2,1,0:T(8,128)(2,1)S(1)} all-to-all(bf16[32,40,128]{2,1,0:T(8,128)(2,1)S(1)} %get-tuple-element.15), channel_id=1, replica_groups=mesh['inst'=32,'tp'=8] {'inst'}, dimensions={0} | all-to-all | bytes 655360 | tf_op jit(solution)/shard_map/all_to_all | solution.py:443
  45.3 2.8 %shard_map.103 = bf16[8,16,512]{2,1,0:T(8,128)(2,1)S(1)} custom-call(s32[32]{0:T(128)} %entry_h.5, s32[32]{0:T(128)} %bitcast.15, bf16[1024,4096]{1,0:T(8,128)(2,1)} %w_h.3, bf16[4,1024,512]{2,1,0:T(8,128)(2,1)S(1)} %get-tuple-element.14.w_early, bf16[32,40,128]{2,1,0:T(8,128)(2,1)S(1)} %all_to_all.15.back, f32[8,16,128]{2,1,0:T(8,128)S(1)} %get-tuple-element.16.o_home, ...), custom_call_target="tpu_custom_call" | custom-call | tf_op jit(solution)/shard_map/pallas_call | solution.py:445
  48.1 14.3 %all_to_all.16.parts = bf16[8,16,512]{2,1,0:T(8,128)(2,1)S(1)} all-to-all(bf16[8,16,512]{2,1,0:T(8,128)(2,1)S(1)} %shard_map.103), channel_id=1, replica_groups=mesh['inst'=32,'tp'=8] {'tp'}, dimensions={0} | all-to-all | bytes 262144 | tf_op jit(solution)/shard_map/all_to_all | solution.py:464
  62.4 0.6 %shard_map.104 = bf16[8,2,512]{2,1,0:T(2,128)(2,1)} custom-call(bf16[8,16,512]{2,1,0:T(8,128)(2,1)S(1)} %all_to_all.16.parts), custom_call_target="tpu_custom_call" | custom-call | tf_op jit(solution)/shard_map/pallas_call | solution.py:466
Async XLA Ops:
  0.0 14.3 %copy-start = (bf16[8,2,8,128]{3,2,1,0:T(8,128)(2,1)S(1)}, bf16[8,2,8,128]{3,2,1,0:T(8,128)(2,1)}, u32[]{:S(2)}) copy-start(bf16[8,2,8,128]{3,2,1,0:T(8,128)(2,1)} %param.10) | copy-start | bytes 98308
  0.0 14.3 %copy-start.2 = (bf16[8,2,1,128]{3,1,2,0:T(2,128)(2,1)S(1)}, bf16[8,2,1,128]{3,1,2,0:T(2,128)(2,1)}, u32[]{:S(2)}) copy-start(bf16[8,2,1,128]{3,1,2,0:T(2,128)(2,1)} %param.12) | copy-start | bytes 12292
  0.0 14.3 %copy-start.1 = (bf16[8,2,1,128]{3,1,2,0:T(2,128)(2,1)S(1)}, bf16[8,2,1,128]{3,1,2,0:T(2,128)(2,1)}, u32[]{:S(2)}) copy-start(bf16[8,2,1,128]{3,1,2,0:T(2,128)(2,1)} %param.11) | copy-start | bytes 12292
  2.4 24.4 %all-to-all-start = ((bf16[32,40,128]{2,1,0:T(8,128)(2,1)}), bf16[32,40,128]{2,1,0:T(8,128)(2,1)S(1)}, u32[]{:S(2)}, u32[]{:S(2)}) async-start(bf16[32,40,128]{2,1,0:T(8,128)(2,1)} %get-tuple-element.11), calls=%async_computation | async-start | bytes 655360 | tf_op jit(solution)/shard_map/all_to_all | solution.py:394

commit v5 on v4

--- a/solution.py
+++ b/solution.py
@@ -31,14 +31,14 @@
 
 
 def pack_kernel(
-    entry_h, target_h, table_h, lengths_h, q_h, kp_h,
-    send, kp,
+    entry_h, target_h, table_h, lengths_h, q_h,
+    send,
     entry, target, table, lengths, q, tiles, count, slots, lives, sems,
 ):
     peers = send.shape[0]
     blocks = table.shape[1]
     small = fetch_all(
-        [(entry_h, entry), (target_h, target), (table_h, table), (lengths_h, lengths), (q_h, q), (kp_h, kp)],
+        [(entry_h, entry), (target_h, target), (table_h, table), (lengths_h, lengths), (q_h, q)],
         sems,
     )
 
@@ -50,7 +50,7 @@
         return 0
 
     lax.fori_loop(0, peers, clear, 0, unroll=4)
-    for c in small[:5]:
+    for c in small:
         c.wait()
 
     def place(j, _):
@@ -80,8 +80,6 @@
         return 0
 
     lax.fori_loop(0, peers, lay, 0, unroll=4)
-    for c in small[5:]:
-        c.wait()
 
 
 def attend(n, query, slot_of, live_of, store, kp, vp, scores, ready):
@@ -133,7 +131,7 @@
 
 
 def serve_kernel(
-    vp_h, w_h, recv, kp, after,
+    vp_h, w_h, recv, kp,
     back, w,
     vp, side_f, side_i, side_s, ids, att, lse, scores, sems,
 ):
@@ -206,14 +204,15 @@
 
 
 def home_kernel(
-    entry_h, table_h, lengths_h, kp_h, vp_h, q, nk, nv,
-    o_out, z_out,
-    entry, table, lengths, kp, vp, o_part, z_part, lent, ids, scores, sems,
+    entry_h, table_h, lengths_h, q_h, nk_h, nv_h, kp_h, vp_h,
+    o_out, z_out, kp,
+    entry, table, lengths, q, nk, nv, vp, o_part, z_part, lent, ids, scores, sems,
 ):
     requests, blocks = table.shape
     entries = requests * blocks
     copies = fetch_all(
-        [(entry_h, entry), (table_h, table), (lengths_h, lengths), (kp_h, kp), (vp_h, vp)], sems
+        [(entry_h, entry), (table_h, table), (lengths_h, lengths), (q_h, q), (nk_h, nk), (nv_h, nv), (kp_h, kp), (vp_h, vp)],
+        sems,
     )
     z_part[...] = jnp.full(z_part.shape, DEAD, F32)
     o_part[...] = jnp.zeros(o_part.shape, F32)
@@ -223,7 +222,7 @@
         return 0
 
     lax.fori_loop(0, entries, clear, 0, unroll=8)
-    for c in copies[:3]:
+    for c in copies[:6]:
         c.wait()
 
     def mark(j, _):
@@ -254,8 +253,8 @@
         o_part[ids[item]] = o
         z_part[ids[item]] = z
 
-    copies[3].wait()
-    attend(n, query, slot_of, live_of, store, kp, vp, scores, copies[4].wait)
+    copies[6].wait()
+    attend(n, query, slot_of, live_of, store, kp, vp, scores, copies[7].wait)
     scale = 128**-0.5
     second = lax.broadcasted_iota(jnp.int32, (ROWS, 1), 0) >= HALF
     for r in range(requests):
@@ -371,11 +370,11 @@
     like = lambda x: jax.ShapeDtypeStruct(x.shape, x.dtype)
     scores = pltpu.VMEM((2, GROUP, ROWS, 128), F32)
 
-    send, kp = pl.pallas_call(
+    send = pl.pallas_call(
         pack_kernel,
-        out_shape=(jax.ShapeDtypeStruct((peers, SLAB, size), BF), like(k_hbm)),
-        in_specs=[HB] * 6,
-        out_specs=(VM, VM),
+        out_shape=jax.ShapeDtypeStruct((peers, SLAB, size), BF),
+        in_specs=[HB] * 5,
+        out_specs=VM,
         scratch_shapes=[
             smem(lends),
             smem(lends),
@@ -386,35 +385,37 @@
             smem(peers),
             smem(peers * CAP),
             smem(peers * CAP),
-            sems(6),
+            sems(5),
         ],
         compiler_params=params(16),
-    )(*map(held, (lend_entry, target, block_table, lengths, q, k_hbm)))
+    )(*map(held, (lend_entry, target, block_table, lengths, q)))
 
     recv = lax.all_to_all(send, "inst", split_axis=0, concat_axis=0, tiled=True)
 
     tile_state = jax.ShapeDtypeStruct((requests, ROWS, size), F32)
-    o_home, z_home = pl.pallas_call(
+    o_home, z_home, kp = pl.pallas_call(
         home_kernel,
-        out_shape=(tile_state, tile_state),
-        in_specs=[HB] * 5 + [VM] * 3,
-        out_specs=(VM, VM),
+        out_shape=(tile_state, tile_state, like(k_hbm)),
+        in_specs=[HB] * 8,
+        out_specs=(VM, VM, VM),
         scratch_shapes=[
             smem(lends),
             smem(*block_table.shape),
             smem(requests),
-            pltpu.VMEM(k_hbm.shape, BF),
+            pltpu.VMEM(q.shape, BF),
+            pltpu.VMEM(nk.shape, BF),
+            pltpu.VMEM(nv.shape, BF),
             pltpu.VMEM(v_hbm.shape, BF),
             pltpu.VMEM((entries, ROWS, size), F32),
             pltpu.VMEM((entries, ROWS, size), F32),
             smem(entries),
             smem(entries + 1),
             scores,
-            sems(5),
+            sems(8),
         ],
         compiler_params=params(24),
         cost_estimate=pl.CostEstimate(flops=10**9, bytes_accessed=16 * 2**20, transcendentals=0),
-    )(*map(held, (lend_entry, block_table, lengths, k_hbm, v_hbm)), q, nk, nv)
+    )(*map(held, (lend_entry, block_table, lengths, q, nk, nv, k_hbm, v_hbm)))
 
     width = out_weight.shape[1] // parts
     early = parts // 2
@@ -424,7 +425,7 @@
             jax.ShapeDtypeStruct((peers, SLAB, size), BF),
             jax.ShapeDtypeStruct((early, out_weight.shape[0], width), BF),
         ),
-        in_specs=[HB, HB, VM, VM, VM],
+        in_specs=[HB, HB, VM, VM],
         out_specs=(VM, VM),
         scratch_shapes=[
             pltpu.VMEM(v_hbm.shape, BF),
@@ -438,7 +439,7 @@
             sems(2 + early),
         ],
         compiler_params=params(24),
-    )(held(v_hbm), held(out_weight), recv, kp, z_home)
+    )(held(v_hbm), held(out_weight), recv, kp)
 
     mine = lax.all_to_all(back, "inst", split_axis=0, concat_axis=0, tiled=True)
 

time: 63.2 us -> 62.7 us (level)
    all_to_all x1, blocking collectives: 15.4 us -> 16.1 us  [on_device(): mine = lax.all_to_all(back, 'inst', split_axis=0, concat_axis=0, tiled=True)]
    all_to_all x1, blocking collectives: 14.3 us -> 13.6 us  [on_device(): lax.all_to_all(partial, 'tp', split_axis=0, concat_axis=0, tiled=True)]
where the time goes in v5:
time: 62.7 us; the launch traced here: 62.6 us
  blocking collectives  29.7 us (47%)
  Pallas kernels  12.2 us (19%)
  starting transfers between devices  11.9 us (19%)
  waiting for transfers between devices  8.73 us (14%)
    all_to_all x1, blocking collectives, on_device(): mine = lax.all_to_all(back, 'inst', split_axis=0, concat_axis=0, tiled=True)  16.1 us
    all_to_all x1, blocking collectives, on_device(): lax.all_to_all(partial, 'tp', split_axis=0, concat_axis=0, tiled=True)  13.6 us
    all_to_all x1, starting transfers between devices, on_device(): recv = lax.all_to_all(send, 'inst', split_axis=0, concat_axis=0, tiled=True)  11.9 us
    all_to_all x1, waiting for transfers between devices, on_device(): recv = lax.all_to_all(send, 'inst', split_axis=0, concat_axis=0, tiled=True)  8.73 us
    pallas_call x1, Pallas kernels, on_device(): pl.pallas_call(home_kernel, out_shape=(tile_state, tile_state, like(k_hbm...  3.82 us
    pallas_call x1, Pallas kernels, on_device(): pl.pallas_call(serve_kernel, out_shape=(jax.ShapeDtypeStruct((peers, SLAB...  2.88 us
    pallas_call x1, Pallas kernels, on_device(): pl.pallas_call(merge_kernel, out_shape=jax.ShapeDtypeStruct((parts, reque...  2.81 us
    pallas_call x1, Pallas kernels, on_device(): pl.pallas_call(pack_kernel, out_shape=jax.ShapeDtypeStruct((peers, SLAB,...  2.1 us
  transfers between devices with their start and end apart: 1, of which 1 were waited for; matrix products, arithmetic and copies ran while one was open for 0% of the time, Pallas kernels for 6%

profile of v5, /device:TPU:1, one launch (start us, length us, event | category | flops | bytes accessed | tf_op | source)
XLA Modules:
  0.0 62.6 jit_solution(7366673390894059834)
XLA Ops:
  0.0 2.1 %shard_map.100 = bf16[32,40,128]{2,1,0:T(8,128)(2,1)} custom-call(s32[32]{0:T(128)} %entry_h.5, s32[32]{0:T(128)} %bitcast.13, s32[8,8]{1,0:T(8,128)} %table_h.3, s32[8]{0:T(128)} %lengths_h.3, bf16[8,16,128]{2,1,0:T(8,128)(2,1)} %bitcast.9), custom_call_target="tpu_custom_call" | custom-call | tf_op jit(solution)/shard_map/pallas_call | solution.py:373
  2.1 11.9 %all-to-all-start = ((bf16[32,40,128]{2,1,0:T(8,128)(2,1)}), bf16[32,40,128]{2,1,0:T(8,128)(2,1)S(1)}, u32[]{:S(2)}, u32[]{:S(2)}) async-start(bf16[32,40,128]{2,1,0:T(8,128)(2,1)} %shard_map.100), calls=%async_computation | async-start | bytes 655360 | tf_op jit(solution)/shard_map/all_to_all | solution.py:393
  14.0 3.8 %shard_map.101 = (f32[8,16,128]{2,1,0:T(8,128)S(1)}, f32[8,16,128]{2,1,0:T(8,128)S(1)}, bf16[64,128,128]{2,1,0:T(8,128)(2,1)S(1)}) custom-call(s32[32]{0:T(128)} %entry_h.5, s32[8,8]{1,0:T(8,128)} %table_h.3, s32[8]{0:T(128)} %lengths_h.3, bf16[8,16,128]{2,1,0:T(8,128)(2,1)} %bitcast.10, bf16[8,2,128]{2,1,0:T(2,128)(2,1)} %bitcast.11, ...), custom_call_target="tpu_custom_call" | custom-call | flops 1000000000 | bytes 16777216 | tf_op jit(solution)/shard_map/pallas_call | solution.py:396
  17.8 8.7 %all-to-all-done.recv = bf16[32,40,128]{2,1,0:T(8,128)(2,1)S(1)} async-done(((bf16[32,40,128]{2,1,0:T(8,128)(2,1)}), bf16[32,40,128]{2,1,0:T(8,128)(2,1)S(1)}, u32[]{:S(2)}, u32[]{:S(2)}) %all-to-all-start) | async-done | bytes 327712 | tf_op jit(solution)/shard_map/all_to_all | solution.py:393
  26.5 2.9 %shard_map.102 = (bf16[32,40,128]{2,1,0:T(8,128)(2,1)S(1)}, bf16[4,1024,512]{2,1,0:T(8,128)(2,1)S(1)}) custom-call(bf16[64,128,128]{2,1,0:T(8,128)(2,1)} %bitcast.7, bf16[1024,4096]{1,0:T(8,128)(2,1)} %w_h.3, bf16[32,40,128]{2,1,0:T(8,128)(2,1)S(1)} %all-to-all-done.recv, bf16[64,128,128]{2,1,0:T(8,128)(2,1)S(1)} %get-tuple-element.10.kp), custom_call_target="tpu_custom_call" | custom-call | tf_op jit(solution)/shard_map/pallas_call | solution.py:422
  29.4 16.1 %all_to_all.15.back = bf16[32,40,128]{2,1,0:T(8,128)(2,1)S(1)} all-to-all(bf16[32,40,128]{2,1,0:T(8,128)(2,1)S(1)} %get-tuple-element.12), channel_id=1, replica_groups=mesh['inst'=32,'tp'=8] {'inst'}, dimensions={0} | all-to-all | bytes 655360 | tf_op jit(solution)/shard_map/all_to_all | solution.py:444
  45.5 2.8 %shard_map.103 = bf16[8,16,512]{2,1,0:T(8,128)(2,1)S(1)} custom-call(s32[32]{0:T(128)} %entry_h.5, s32[32]{0:T(128)} %bitcast.14, bf16[1024,4096]{1,0:T(8,128)(2,1)} %w_h.3, bf16[4,1024,512]{2,1,0:T(8,128)(2,1)S(1)} %get-tuple-element.11.w_early, bf16[32,40,128]{2,1,0:T(8,128)(2,1)S(1)} %all_to_all.15.back, f32[8,16,128]{2,1,0:T(8,128)S(1)} %get-tuple-element.13.o_home, ...), custom_call_target="tpu_custom_call" | custom-call | tf_op jit(solution)/shard_map/pallas_call | solution.py:446
  48.4 13.6 %all_to_all.16.parts = bf16[8,16,512]{2,1,0:T(8,128)(2,1)S(1)} all-to-all(bf16[8,16,512]{2,1,0:T(8,128)(2,1)S(1)} %shard_map.103), channel_id=1, replica_groups=mesh['inst'=32,'tp'=8] {'tp'}, dimensions={0} | all-to-all | bytes 262144 | tf_op jit(solution)/shard_map/all_to_all | solution.py:465
  61.9 0.6 %shard_map.104 = bf16[8,2,512]{2,1,0:T(2,128)(2,1)} custom-call(bf16[8,16,512]{2,1,0:T(8,128)(2,1)S(1)} %all_to_all.16.parts), custom_call_target="tpu_custom_call" | custom-call | tf_op jit(solution)/shard_map/pallas_call | solution.py:467
Async XLA Ops:
  2.1 24.4 %all-to-all-start = ((bf16[32,40,128]{2,1,0:T(8,128)(2,1)}), bf16[32,40,128]{2,1,0:T(8,128)(2,1)S(1)}, u32[]{:S(2)}, u32[]{:S(2)}) async-start(bf16[32,40,128]{2,1,0:T(8,128)(2,1)} %shard_map.100), calls=%async_computation | async-start | bytes 655360 | tf_op jit(solution)/shard_map/all_to_all | solution.py:393

commit v6 on v5

--- a/solution.py
+++ b/solution.py
@@ -9,7 +9,7 @@
 
 DEAD = -1e30
 CAP = 2
-GROUP = 8
+GROUP = 16
 ROWS = 16
 HALF = 8
 SLAB = 40
@@ -66,7 +66,7 @@
         tiles[i] = q[r]
         return 0
 
-    lax.fori_loop(0, entry.shape[0], place, 0, unroll=4)
+    lax.fori_loop(0, entry.shape[0], place, 0, unroll=True)
     lane = lane_iota(HALF)
 
     def lay(i, _):
@@ -79,7 +79,7 @@
         )
         return 0
 
-    lax.fori_loop(0, peers, lay, 0, unroll=4)
+    lax.fori_loop(0, peers, lay, 0, unroll=8)
 
 
 def attend(n, query, slot_of, live_of, store, kp, vp, scores, ready):
@@ -418,7 +418,7 @@
     )(*map(held, (lend_entry, block_table, lengths, q, nk, nv, k_hbm, v_hbm)))
 
     width = out_weight.shape[1] // parts
-    early = parts // 2
+    early = 5
     back, w_early = pl.pallas_call(
         serve_kernel,
         out_shape=(

time: 62.7 us -> 62.5 us (level)
  transfers between devices with their start and end apart: 1 -> 1, of which waited for: 1 -> 1; matrix products, arithmetic and copies ran while one was open for 0% -> 0% of each run, Pallas kernels for 6% -> 5%
where the time goes in v6:
time: 62.5 us; the launch traced here: 62.2 us
  blocking collectives  29.2 us (47%)
  starting transfers between devices  11.9 us (19%)
  Pallas kernels  11.8 us (19%)
  waiting for transfers between devices  9.31 us (15%)
    all_to_all x1, blocking collectives, on_device(): mine = lax.all_to_all(back, 'inst', split_axis=0, concat_axis=0, tiled=True)  16 us
    all_to_all x1, blocking collectives, on_device(): lax.all_to_all(partial, 'tp', split_axis=0, concat_axis=0, tiled=True)  13.2 us
    all_to_all x1, starting transfers between devices, on_device(): recv = lax.all_to_all(send, 'inst', split_axis=0, concat_axis=0, tiled=True)  11.9 us
    all_to_all x1, waiting for transfers between devices, on_device(): recv = lax.all_to_all(send, 'inst', split_axis=0, concat_axis=0, tiled=True)  9.31 us
    pallas_call x1, Pallas kernels, on_device(): pl.pallas_call(home_kernel, out_shape=(tile_state, tile_state, like(k_hbm...  3.23 us
    pallas_call x1, Pallas kernels, on_device(): pl.pallas_call(serve_kernel, out_shape=(jax.ShapeDtypeStruct((peers, SLAB...  3.2 us
    pallas_call x1, Pallas kernels, on_device(): pl.pallas_call(merge_kernel, out_shape=jax.ShapeDtypeStruct((parts, reque...  2.69 us
    pallas_call x1, Pallas kernels, on_device(): pl.pallas_call(pack_kernel, out_shape=jax.ShapeDtypeStruct((peers, SLAB,...  2.04 us
  transfers between devices with their start and end apart: 1, of which 1 were waited for; matrix products, arithmetic and copies ran while one was open for 0% of the time, Pallas kernels for 5%

profile of v6, /device:TPU:1, one launch (start us, length us, event | category | flops | bytes accessed | tf_op | source)
XLA Modules:
  0.0 62.2 jit_solution(2994815262993083581)
XLA Ops:
  0.0 2.0 %shard_map.100 = bf16[32,40,128]{2,1,0:T(8,128)(2,1)} custom-call(s32[32]{0:T(128)} %entry_h.5, s32[32]{0:T(128)} %bitcast.13, s32[8,8]{1,0:T(8,128)} %table_h.3, s32[8]{0:T(128)} %lengths_h.3, bf16[8,16,128]{2,1,0:T(8,128)(2,1)} %bitcast.9), custom_call_target="tpu_custom_call" | custom-call | tf_op jit(solution)/shard_map/pallas_call | solution.py:373
  2.0 11.9 %all-to-all-start = ((bf16[32,40,128]{2,1,0:T(8,128)(2,1)}), bf16[32,40,128]{2,1,0:T(8,128)(2,1)S(1)}, u32[]{:S(2)}, u32[]{:S(2)}) async-start(bf16[32,40,128]{2,1,0:T(8,128)(2,1)} %shard_map.100), calls=%async_computation | async-start | bytes 655360 | tf_op jit(solution)/shard_map/all_to_all | solution.py:393
  13.9 3.2 %shard_map.101 = (f32[8,16,128]{2,1,0:T(8,128)S(1)}, f32[8,16,128]{2,1,0:T(8,128)S(1)}, bf16[64,128,128]{2,1,0:T(8,128)(2,1)S(1)}) custom-call(s32[32]{0:T(128)} %entry_h.5, s32[8,8]{1,0:T(8,128)} %table_h.3, s32[8]{0:T(128)} %lengths_h.3, bf16[8,16,128]{2,1,0:T(8,128)(2,1)} %bitcast.10, bf16[8,2,128]{2,1,0:T(2,128)(2,1)} %bitcast.11, ...), custom_call_target="tpu_custom_call" | custom-call | flops 1000000000 | bytes 16777216 | tf_op jit(solution)/shard_map/pallas_call | solution.py:396
  17.2 9.3 %all-to-all-done.recv = bf16[32,40,128]{2,1,0:T(8,128)(2,1)S(1)} async-done(((bf16[32,40,128]{2,1,0:T(8,128)(2,1)}), bf16[32,40,128]{2,1,0:T(8,128)(2,1)S(1)}, u32[]{:S(2)}, u32[]{:S(2)}) %all-to-all-start) | async-done | bytes 327712 | tf_op jit(solution)/shard_map/all_to_all | solution.py:393
  26.5 3.2 %shard_map.102 = (bf16[32,40,128]{2,1,0:T(8,128)(2,1)S(1)}, bf16[5,1024,512]{2,1,0:T(8,128)(2,1)S(1)}) custom-call(bf16[64,128,128]{2,1,0:T(8,128)(2,1)} %bitcast.7, bf16[1024,4096]{1,0:T(8,128)(2,1)} %w_h.3, bf16[32,40,128]{2,1,0:T(8,128)(2,1)S(1)} %all-to-all-done.recv, bf16[64,128,128]{2,1,0:T(8,128)(2,1)S(1)} %get-tuple-element.10.kp), custom_call_target="tpu_custom_call" | custom-call | tf_op jit(solution)/shard_map/pallas_call | solution.py:422
  29.7 16.0 %all_to_all.15.back = bf16[32,40,128]{2,1,0:T(8,128)(2,1)S(1)} all-to-all(bf16[32,40,128]{2,1,0:T(8,128)(2,1)S(1)} %get-tuple-element.12), channel_id=1, replica_groups=mesh['inst'=32,'tp'=8] {'inst'}, dimensions={0} | all-to-all | bytes 655360 | tf_op jit(solution)/shard_map/all_to_all | solution.py:444
  45.7 2.7 %shard_map.103 = bf16[8,16,512]{2,1,0:T(8,128)(2,1)S(1)} custom-call(s32[32]{0:T(128)} %entry_h.5, s32[32]{0:T(128)} %bitcast.14, bf16[1024,4096]{1,0:T(8,128)(2,1)} %w_h.3, bf16[5,1024,512]{2,1,0:T(8,128)(2,1)S(1)} %get-tuple-element.11.w_early, bf16[32,40,128]{2,1,0:T(8,128)(2,1)S(1)} %all_to_all.15.back, f32[8,16,128]{2,1,0:T(8,128)S(1)} %get-tuple-element.13.o_home, ...), custom_call_target="tpu_custom_call" | custom-call | tf_op jit(solution)/shard_map/pallas_call | solution.py:446
  48.4 13.2 %all_to_all.16.parts = bf16[8,16,512]{2,1,0:T(8,128)(2,1)S(1)} all-to-all(bf16[8,16,512]{2,1,0:T(8,128)(2,1)S(1)} %shard_map.103), channel_id=1, replica_groups=mesh['inst'=32,'tp'=8] {'tp'}, dimensions={0} | all-to-all | bytes 262144 | tf_op jit(solution)/shard_map/all_to_all | solution.py:465
  61.6 0.6 %shard_map.104 = bf16[8,2,512]{2,1,0:T(2,128)(2,1)} custom-call(bf16[8,16,512]{2,1,0:T(8,128)(2,1)S(1)} %all_to_all.16.parts), custom_call_target="tpu_custom_call" | custom-call | tf_op jit(solution)/shard_map/pallas_call | solution.py:467
Async XLA Ops:
  2.0 24.4 %all-to-all-start = ((bf16[32,40,128]{2,1,0:T(8,128)(2,1)}), bf16[32,40,128]{2,1,0:T(8,128)(2,1)S(1)}, u32[]{:S(2)}, u32[]{:S(2)}) async-start(bf16[32,40,128]{2,1,0:T(8,128)(2,1)} %shard_map.100), calls=%async_computation | async-start | bytes 655360 | tf_op jit(solution)/shard_map/all_to_all | solution.py:393

commit v7 on v6

--- a/solution.py
+++ b/solution.py
@@ -12,7 +12,7 @@
 GROUP = 16
 ROWS = 16
 HALF = 8
-SLAB = 40
+SLAB = CAP * ROWS + 2
 BF = jnp.bfloat16
 F32 = jnp.float32
 VM = pl.BlockSpec(memory_space=pltpu.VMEM)
@@ -30,12 +30,20 @@
     return copies
 
 
+def tile_rows(peer, rank):
+    return pl.ds(peer * SLAB + rank * ROWS, ROWS)
+
+
+def side_rows(peers):
+    return pl.ds(CAP * ROWS, peers, stride=SLAB)
+
+
 def pack_kernel(
     entry_h, target_h, table_h, lengths_h, q_h,
     send,
-    entry, target, table, lengths, q, tiles, count, slots, lives, sems,
+    entry, target, table, lengths, q, wide, count, slots, lives, sems,
 ):
-    peers = send.shape[0]
+    peers = count.shape[0]
     blocks = table.shape[1]
     small = fetch_all(
         [(entry_h, entry), (target_h, target), (table_h, table), (lengths_h, lengths), (q_h, q)],
@@ -63,23 +71,22 @@
         i = t * CAP + rank
         slots[i] = table[r, b]
         lives[i] = jnp.clip(lengths[r] - b * 128, 0, 128)
-        tiles[i] = q[r]
+        wide[tile_rows(t, rank), :] = q[r].astype(F32)
         return 0
 
     lax.fori_loop(0, entry.shape[0], place, 0, unroll=True)
-    lane = lane_iota(HALF)
+    lane = lane_iota(2)
 
     def lay(i, _):
         v = jnp.where(lane == 0, slots[i * CAP], 0)
         v = jnp.where(lane == 1, lives[i * CAP], v)
         v = jnp.where(lane == 2, slots[i * CAP + 1], v)
         v = jnp.where(lane == 3, lives[i * CAP + 1], v)
-        send[i] = jnp.concatenate(
-            [tiles[i * CAP], tiles[i * CAP + 1], v.astype(F32).astype(BF)], axis=0
-        )
+        wide[pl.ds(i * SLAB + CAP * ROWS, 2), :] = v.astype(F32)
         return 0
 
     lax.fori_loop(0, peers, lay, 0, unroll=8)
+    send[...] = wide[...].astype(BF)
 
 
 def attend(n, query, slot_of, live_of, store, kp, vp, scores, ready):
@@ -133,20 +140,19 @@
 def serve_kernel(
     vp_h, w_h, recv, kp,
     back, w,
-    vp, side_f, side_i, side_s, ids, att, lse, scores, sems,
+    vp, wide, side_i, side_s, ids, answer, lse, scores, sems,
 ):
-    peers = recv.shape[0]
+    peers = side_i.shape[0]
     values = pltpu.make_async_copy(vp_h, vp, sems.at[1])
     values.start()
     width = w.shape[2]
     chunks = [(w_h.at[:, pl.ds(i * width, width)], w.at[i]) for i in range(w.shape[0])]
     weights = fetch_all(chunks, sems.at[pl.ds(2, len(chunks))])
-    side = recv[...][:, CAP * ROWS :, :].astype(F32)
-    side_f[...] = side.reshape(peers * HALF, 128)
-    side_i[...] = side_f[pl.ds(0, peers, stride=HALF), :].astype(jnp.int32)
+    wide[...] = recv[...].astype(F32)
+    side_i[...] = wide[side_rows(peers), :].astype(jnp.int32)
     copy = pltpu.make_async_copy(side_i, side_s, sems.at[0])
     copy.start()
-    att[...] = jnp.zeros(att.shape, F32)
+    answer[...] = jnp.zeros(answer.shape, F32)
     lse[...] = jnp.full(lse.shape, DEAD, F32)
     copy.wait()
 
@@ -160,7 +166,7 @@
 
     def query(item):
         i = ids[item]
-        return recv[lax.shift_right_logical(i, 1), pl.ds(pl.multiple_of((i & 1) * ROWS, ROWS), ROWS), :]
+        return wide[tile_rows(lax.shift_right_logical(i, 1), i & 1), :].astype(BF)
 
     def slot_of(item):
         i = ids[item]
@@ -171,26 +177,23 @@
         return side_s[lax.shift_right_logical(i, 1), 2 * (i & 1) + 1]
 
     def store(item, o, z):
-        att[ids[item]] = o
-        lse[ids[item]] = z
-
+        i = ids[item]
+        answer[tile_rows(lax.shift_right_logical(i, 1), i & 1), :] = o
+        lse[pl.ds(i, 1), :] = jnp.sum(jnp.where(own, z, 0.0), axis=0, keepdims=True)
+
+    own = lane_iota() % ROWS == lax.broadcasted_iota(jnp.int32, (ROWS, 128), 0)
     attend(n, query, slot_of, live_of, store, kp, vp, scores, values.wait)
-    lane = lane_iota(HALF)
-
-    def lay(i, _):
-        side = jnp.zeros((HALF, 128), F32)
-        for c in range(CAP):
-            for h in range(2):
-                rest = lse[i * CAP + c, h * HALF : (h + 1) * HALF, :]
-                for piece in range(3):
-                    part = rest.astype(BF).astype(F32)
-                    rest = rest - part
-                    side = jnp.where(lane == (h * CAP + c) * 4 + piece, part, side)
-        rows = jnp.concatenate([att[i * CAP], att[i * CAP + 1], side], axis=0)
-        back[i] = rows.astype(BF)
-        return 0
-
-    lax.fori_loop(0, peers, lay, 0, unroll=4)
+    group = lane_iota(peers) // ROWS
+    rest = jnp.where(
+        group < 3, lse[pl.ds(0, peers, stride=CAP), :], lse[pl.ds(1, peers, stride=CAP), :]
+    )
+    side = jnp.zeros((peers, 128), F32)
+    for piece in range(3):
+        part = rest.astype(BF).astype(F32)
+        rest = rest - part
+        side = jnp.where(group % 3 == piece, part, side)
+    answer[side_rows(peers), :] = side
+    back[...] = answer[...].astype(BF)
     for c in weights:
         c.wait()
 
@@ -277,22 +280,26 @@
 def merge_kernel(
     entry_h, target_h, w_h, w_early, back, o_home, z_home,
     out,
-    entry, target, w, o_all, z_all, z_back, att, count, sems,
+    entry, target, w, wide, o_all, z_all, z_back, att, count, sems,
 ):
     requests = o_home.shape[0]
-    peers = back.shape[0]
+    peers = count.shape[0]
     width = out.shape[2]
     early = w_early.shape[0]
     chunks = [(w_h.at[:, pl.ds((early + i) * width, width)], w.at[i]) for i in range(w.shape[0])]
     copies = fetch_all([(entry_h, entry), (target_h, target)] + chunks, sems)
     o_all[...] = jnp.zeros(o_all.shape, F32)
     z_all[...] = jnp.full(z_all.shape, DEAD, F32)
-    side = back[...][:, CAP * ROWS :, :].reshape(peers * HALF, 128)
-    kinds = 2 * CAP
-    lane = lax.broadcasted_iota(jnp.int32, (128, kinds * 128), 0)
-    block = lax.broadcasted_iota(jnp.int32, (128, kinds * 128), 1) // 128
-    pick = jnp.logical_and(lane >= block * 4, lane < block * 4 + 3)
-    z_back[...] = jnp.dot(side, pick.astype(F32).astype(BF), preferred_element_type=F32)
+    wide[...] = back[...].astype(F32)
+    side = wide[side_rows(peers), :].reshape(peers, 1, 128)
+    lane = lax.broadcasted_iota(jnp.int32, (peers, ROWS, 128), 2)
+    own = lane % ROWS == lax.broadcasted_iota(jnp.int32, (peers, ROWS, 128), 1)
+    ones = jnp.ones((128, 128), BF)
+    for c in range(CAP):
+        mine = jnp.logical_and(own, lane // (3 * ROWS) == c)
+        pieces = jnp.where(mine, side, 0.0).astype(BF).reshape(peers * ROWS, 128)
+        z = jnp.dot(pieces, ones, preferred_element_type=F32)
+        z_back[c * peers : (c + 1) * peers] = z.reshape(peers, ROWS, 128)
 
     def clear(i, _):
         count[i] = 0
@@ -307,11 +314,8 @@
         t = target[j]
         rank = count[t]
         count[t] = rank + 1
-        o_all[e] = back[t, pl.ds(pl.multiple_of(rank * ROWS, ROWS), ROWS), :].astype(F32)
-        rows = pl.ds(pl.multiple_of(t * HALF, HALF), HALF)
-        for h in range(2):
-            cols = pl.ds(pl.multiple_of((h * CAP + rank) * 128, 128), 128)
-            z_all[e, h * HALF : (h + 1) * HALF, :] = z_back[rows, cols]
+        o_all[e] = wide[tile_rows(t, rank), :]
+        z_all[e] = z_back[rank * peers + t]
         return 0
 
     lax.fori_loop(0, entry.shape[0], fetch, 0, unroll=4)
@@ -368,11 +372,12 @@
     smem = lambda *n: pltpu.SMEM(n, jnp.int32)
     sems = lambda n: pltpu.SemaphoreType.DMA((n,))
     like = lambda x: jax.ShapeDtypeStruct(x.shape, x.dtype)
+    wide = pltpu.VMEM((peers * SLAB, size), F32)
     scores = pltpu.VMEM((2, GROUP, ROWS, 128), F32)
 
     send = pl.pallas_call(
         pack_kernel,
-        out_shape=jax.ShapeDtypeStruct((peers, SLAB, size), BF),
+        out_shape=jax.ShapeDtypeStruct((peers * SLAB, size), BF),
         in_specs=[HB] * 5,
         out_specs=VM,
         scratch_shapes=[
@@ -381,7 +386,7 @@
             smem(*block_table.shape),
             smem(requests),
             pltpu.VMEM(q.shape, BF),
-            pltpu.VMEM((peers * CAP, ROWS, size), BF),
+            wide,
             smem(peers),
             smem(peers * CAP),
             smem(peers * CAP),
@@ -390,7 +395,12 @@
         compiler_params=params(16),
     )(*map(held, (lend_entry, target, block_table, lengths, q)))
 
-    recv = lax.all_to_all(send, "inst", split_axis=0, concat_axis=0, tiled=True)
+    def exchange(x):
+        y = x.reshape(peers, SLAB // 2, 2, size)
+        y = lax.all_to_all(y, "inst", split_axis=0, concat_axis=0, tiled=True)
+        return y.reshape(x.shape)
+
+    recv = exchange(send)
 
     tile_state = jax.ShapeDtypeStruct((requests, ROWS, size), F32)
     o_home, z_home, kp = pl.pallas_call(
@@ -422,26 +432,26 @@
     back, w_early = pl.pallas_call(
         serve_kernel,
         out_shape=(
-            jax.ShapeDtypeStruct((peers, SLAB, size), BF),
+            jax.ShapeDtypeStruct((peers * SLAB, size), BF),
             jax.ShapeDtypeStruct((early, out_weight.shape[0], width), BF),
         ),
         in_specs=[HB, HB, VM, VM],
         out_specs=(VM, VM),
         scratch_shapes=[
             pltpu.VMEM(v_hbm.shape, BF),
-            pltpu.VMEM((peers * HALF, 128), F32),
+            wide,
             pltpu.VMEM((peers, 128), jnp.int32),
             smem(peers, 128),
             smem(peers * CAP + 1),
-            pltpu.VMEM((peers * CAP, ROWS, 128), F32),
-            pltpu.VMEM((peers * CAP, ROWS, 128), F32),
+            wide,
+            pltpu.VMEM((peers * CAP, 128), F32),
             scores,
             sems(2 + early),
         ],
         compiler_params=params(24),
     )(held(v_hbm), held(out_weight), recv, kp)
 
-    mine = lax.all_to_all(back, "inst", split_axis=0, concat_axis=0, tiled=True)
+    mine = exchange(back)
 
     partial = pl.pallas_call(
         merge_kernel,
@@ -452,9 +462,10 @@
             smem(lends),
             smem(lends),
             pltpu.VMEM((parts - early, out_weight.shape[0], width), BF),
+            wide,
             pltpu.VMEM((entries, ROWS, size), F32),
             pltpu.VMEM((entries, ROWS, size), F32),
-            pltpu.VMEM((peers * HALF, 2 * CAP * 128), F32),
+            pltpu.VMEM((CAP * peers, ROWS, 128), F32),
             pltpu.VMEM((requests * ROWS, size), F32),
             smem(peers),
             sems(2 + parts - early),

time: 62.5 us -> 60.9 us (0.974)
  waiting for transfers between devices: 9.31 us -> 7.97 us
  blocking collectives: 29.2 us -> 28.3 us
    all_to_all x1, waiting for transfers between devices: 9.31 us -> 7.97 us  [exchange(): y = lax.all_to_all(y, 'inst', split_axis=0, concat_axis=0, tiled=True)]
    all_to_all x1, blocking collectives: 16 us -> 14.8 us  [exchange(): y = lax.all_to_all(y, 'inst', split_axis=0, concat_axis=0, tiled=True)]
  transfers between devices with their start and end apart: 1 -> 1, of which waited for: 1 -> 1; matrix products, arithmetic and copies ran while one was open for 0% -> 0% of each run, Pallas kernels for 5% -> 6%
where the time goes in v7:
time: 60.9 us; the launch traced here: 60.6 us
  blocking collectives  28.3 us (46%)
  Pallas kernels  12.4 us (20%)
  starting transfers between devices  11.9 us (20%)
  waiting for transfers between devices  7.97 us (13%)
    all_to_all x1, blocking collectives, exchange(): y = lax.all_to_all(y, 'inst', split_axis=0, concat_axis=0, tiled=True)  14.8 us
    all_to_all x1, blocking collectives, on_device(): lax.all_to_all(partial, 'tp', split_axis=0, concat_axis=0, tiled=True)  13.4 us
    all_to_all x1, starting transfers between devices, exchange(): y = lax.all_to_all(y, 'inst', split_axis=0, concat_axis=0, tiled=True)  11.9 us
    all_to_all x1, waiting for transfers between devices, exchange(): y = lax.all_to_all(y, 'inst', split_axis=0, concat_axis=0, tiled=True)  7.97 us
    pallas_call x1, Pallas kernels, on_device(): pl.pallas_call(home_kernel, out_shape=(tile_state, tile_state, like(k_hbm...  3.84 us
    pallas_call x1, Pallas kernels, on_device(): pl.pallas_call(serve_kernel, out_shape=(jax.ShapeDtypeStruct((peers * SLA...  3.2 us
    pallas_call x1, Pallas kernels, on_device(): pl.pallas_call(merge_kernel, out_shape=jax.ShapeDtypeStruct((parts, reque...  2.72 us
    pallas_call x1, Pallas kernels, on_device(): pl.pallas_call(pack_kernel, out_shape=jax.ShapeDtypeStruct((peers * SLAB,...  2.07 us
  transfers between devices with their start and end apart: 1, of which 1 were waited for; matrix products, arithmetic and copies ran while one was open for 0% of the time, Pallas kernels for 6%

profile of v7, /device:TPU:1, one launch (start us, length us, event | category | flops | bytes accessed | tf_op | source)
XLA Modules:
  0.0 60.6 jit_solution(13364442994855356605)
XLA Ops:
  0.0 2.1 %shard_map.100 = bf16[1088,128]{1,0:T(8,128)(2,1)} custom-call(s32[32]{0:T(128)} %entry_h.5, s32[32]{0:T(128)} %bitcast.20, s32[8,8]{1,0:T(8,128)} %table_h.3, s32[8]{0:T(128)} %lengths_h.3, bf16[8,16,128]{2,1,0:T(8,128)(2,1)} %bitcast.16), custom_call_target="tpu_custom_call" | custom-call | tf_op jit(solution)/shard_map/pallas_call | solution.py:378
  2.1 11.9 %all-to-all-start = ((bf16[32,17,2,128]{3,2,1,0:T(2,128)(2,1)}), bf16[32,17,2,128]{3,2,1,0:T(2,128)(2,1)S(1)}, u32[]{:S(2)}, u32[]{:S(2)}) async-start(bf16[32,17,2,128]{3,2,1,0:T(2,128)(2,1)} %bitcast.3), calls=%async_computation | async-start | bytes 557056 | tf_op jit(solution)/shard_map/all_to_all | solution.py:400
  14.0 3.8 %shard_map.101 = (f32[8,16,128]{2,1,0:T(8,128)S(1)}, f32[8,16,128]{2,1,0:T(8,128)S(1)}, bf16[64,128,128]{2,1,0:T(8,128)(2,1)S(1)}) custom-call(s32[32]{0:T(128)} %entry_h.5, s32[8,8]{1,0:T(8,128)} %table_h.3, s32[8]{0:T(128)} %lengths_h.3, bf16[8,16,128]{2,1,0:T(8,128)(2,1)} %bitcast.17, bf16[8,2,128]{2,1,0:T(2,128)(2,1)} %bitcast.18, ...), custom_call_target="tpu_custom_call" | custom-call | flops 1000000000 | bytes 16777216 | tf_op jit(solution)/shard_map/pallas_call | solution.py:406
  17.8 8.0 %all-to-all-done = bf16[32,17,2,128]{3,2,1,0:T(2,128)(2,1)S(1)} async-done(((bf16[32,17,2,128]{3,2,1,0:T(2,128)(2,1)}), bf16[32,17,2,128]{3,2,1,0:T(2,128)(2,1)S(1)}, u32[]{:S(2)}, u32[]{:S(2)}) %all-to-all-start) | async-done | bytes 278560 | tf_op jit(solution)/shard_map/all_to_all | solution.py:400
  25.8 3.2 %shard_map.102 = (bf16[1088,128]{1,0:T(8,128)(2,1)S(1)}, bf16[5,1024,512]{2,1,0:T(8,128)(2,1)S(1)}) custom-call(bf16[64,128,128]{2,1,0:T(8,128)(2,1)} %bitcast.14, bf16[1024,4096]{1,0:T(8,128)(2,1)} %w_h.3, bf16[1088,128]{1,0:T(8,128)(2,1)S(1)} %bitcast.10, bf16[64,128,128]{2,1,0:T(8,128)(2,1)S(1)} %get-tuple-element.10.kp), custom_call_target="tpu_custom_call" | custom-call | tf_op jit(solution)/shard_map/pallas_call | solution.py:432
  29.0 14.8 %all_to_all.15 = bf16[32,17,2,128]{3,2,1,0:T(2,128)(2,1)S(1)} all-to-all(bf16[32,17,2,128]{3,2,1,0:T(2,128)(2,1)S(1)} %bitcast.12), channel_id=1, replica_groups=mesh['inst'=32,'tp'=8] {'inst'}, dimensions={0} | all-to-all | bytes 557056 | tf_op jit(solution)/shard_map/all_to_all | solution.py:400
  43.8 2.7 %shard_map.103 = bf16[8,16,512]{2,1,0:T(8,128)(2,1)S(1)} custom-call(s32[32]{0:T(128)} %entry_h.5, s32[32]{0:T(128)} %bitcast.21, bf16[1024,4096]{1,0:T(8,128)(2,1)} %w_h.3, bf16[5,1024,512]{2,1,0:T(8,128)(2,1)S(1)} %get-tuple-element.11.w_early, bf16[1088,128]{1,0:T(8,128)(2,1)S(1)} %bitcast.11, f32[8,16,128]{2,1,0:T(8,128)S(1)} %get-tuple-element.13.o_home, ...), custom_call_target="tpu_custom_call" | custom-call | tf_op jit(solution)/shard_map/pallas_call | solution.py:456
  46.6 13.4 %all_to_all.16.parts = bf16[8,16,512]{2,1,0:T(8,128)(2,1)S(1)} all-to-all(bf16[8,16,512]{2,1,0:T(8,128)(2,1)S(1)} %shard_map.103), channel_id=1, replica_groups=mesh['inst'=32,'tp'=8] {'tp'}, dimensions={0} | all-to-all | bytes 262144 | tf_op jit(solution)/shard_map/all_to_all | solution.py:476
  60.0 0.6 %shard_map.104 = bf16[8,2,512]{2,1,0:T(2,128)(2,1)} custom-call(bf16[8,16,512]{2,1,0:T(8,128)(2,1)S(1)} %all_to_all.16.parts), custom_call_target="tpu_custom_call" | custom-call | tf_op jit(solution)/shard_map/pallas_call | solution.py:478
Async XLA Ops:
  2.1 23.7 %all-to-all-start = ((bf16[32,17,2,128]{3,2,1,0:T(2,128)(2,1)}), bf16[32,17,2,128]{3,2,1,0:T(2,128)(2,1)S(1)}, u32[]{:S(2)}, u32[]{:S(2)}) async-start(bf16[32,17,2,128]{3,2,1,0:T(2,128)(2,1)} %bitcast.3), calls=%async_computation | async-start | bytes 557056 | tf_op jit(solution)/shard_map/all_to_all | solution.py:400

commit v8 on v7

--- a/solution.py
+++ b/solution.py
@@ -146,7 +146,7 @@
     values = pltpu.make_async_copy(vp_h, vp, sems.at[1])
     values.start()
     width = w.shape[2]
-    chunks = [(w_h.at[:, pl.ds(i * width, width)], w.at[i]) for i in range(w.shape[0])]
+    chunks = [(w_h.at[:, pl.ds((1 + i) * width, width)], w.at[i]) for i in range(w.shape[0])]
     weights = fetch_all(chunks, sems.at[pl.ds(2, len(chunks))])
     wide[...] = recv[...].astype(F32)
     side_i[...] = wide[side_rows(peers), :].astype(jnp.int32)
@@ -207,37 +207,51 @@
 
 
 def home_kernel(
-    entry_h, table_h, lengths_h, q_h, nk_h, nv_h, kp_h, vp_h,
-    o_out, z_out, kp,
-    entry, table, lengths, q, nk, nv, vp, o_part, z_part, lent, ids, scores, sems,
+    entry_h, target_h, table_h, lengths_h, q_h, nk_h, nv_h, kp_h, vp_h, w_h,
+    o_out, z_out, place_out, kp, w,
+    entry, target, table, lengths, q, nk, nv, vp, o_part, z_part, place, count, ids, scores, sems,
 ):
     requests, blocks = table.shape
     entries = requests * blocks
     copies = fetch_all(
-        [(entry_h, entry), (table_h, table), (lengths_h, lengths), (q_h, q), (nk_h, nk), (nv_h, nv), (kp_h, kp), (vp_h, vp)],
+        [(entry_h, entry), (target_h, target), (table_h, table), (lengths_h, lengths), (q_h, q), (nk_h, nk), (nv_h, nv), (kp_h, kp), (vp_h, vp), (w_h.at[:, pl.ds(0, w.shape[1])], w)],
         sems,
     )
     z_part[...] = jnp.full(z_part.shape, DEAD, F32)
     o_part[...] = jnp.zeros(o_part.shape, F32)
 
+    peers = count.shape[0]
+    none = peers * CAP
+
     def clear(i, _):
-        lent[i] = 0
+        place[0, i] = none
         return 0
 
     lax.fori_loop(0, entries, clear, 0, unroll=8)
-    for c in copies[:6]:
+
+    def clear_count(i, _):
+        count[i] = 0
+        return 0
+
+    lax.fori_loop(0, peers, clear_count, 0, unroll=8)
+    for c in copies[:7]:
         c.wait()
 
     def mark(j, _):
-        lent[entry[j]] = 1
+        t = target[j]
+        rank = count[t]
+        count[t] = rank + 1
+        place[0, entry[j]] = t * CAP + rank
         return 0
 
     lax.fori_loop(0, entry.shape[0], mark, 0, unroll=8)
+    placed = pltpu.make_async_copy(place, place_out, sems.at[10])
+    placed.start()
 
     def listing(e, n):
         ids[n] = e
         alive = lengths[e // blocks] > (e % blocks) * 128
-        return n + jnp.where(jnp.logical_and(alive, lent[e] == 0), 1, 0)
+        return n + jnp.where(jnp.logical_and(alive, place[0, e] == none), 1, 0)
 
     n = lax.fori_loop(0, entries, listing, 0, unroll=4)
 
@@ -256,8 +270,8 @@
         o_part[ids[item]] = o
         z_part[ids[item]] = z
 
-    copies[6].wait()
-    attend(n, query, slot_of, live_of, store, kp, vp, scores, copies[7].wait)
+    copies[7].wait()
+    attend(n, query, slot_of, live_of, store, kp, vp, scores, copies[8].wait)
     scale = 128**-0.5
     second = lax.broadcasted_iota(jnp.int32, (ROWS, 1), 0) >= HALF
     for r in range(requests):
@@ -275,22 +289,24 @@
         o, top, total = weigh([fresh] + [(o_part[r * 8 + b], z_part[r * 8 + b]) for b in range(8)])
         o_out[r] = o
         z_out[r] = top + jnp.log(total)
+    copies[9].wait()
+    placed.wait()
 
 
 def merge_kernel(
-    entry_h, target_h, w_h, w_early, back, o_home, z_home,
+    w_h, w_first, w_early, back, o_home, z_home, place_v,
     out,
-    entry, target, w, wide, o_all, z_all, z_back, att, count, sems,
+    place, w, wide, z_back, att, sems,
 ):
     requests = o_home.shape[0]
-    peers = count.shape[0]
+    peers = z_back.shape[1] - 1
+    rows = peers * SLAB
     width = out.shape[2]
-    early = w_early.shape[0]
+    early = 1 + w_early.shape[0]
     chunks = [(w_h.at[:, pl.ds((early + i) * width, width)], w.at[i]) for i in range(w.shape[0])]
-    copies = fetch_all([(entry_h, entry), (target_h, target)] + chunks, sems)
-    o_all[...] = jnp.zeros(o_all.shape, F32)
-    z_all[...] = jnp.full(z_all.shape, DEAD, F32)
-    wide[...] = back[...].astype(F32)
+    copies = fetch_all([(place_v, place)] + chunks, sems)
+    wide[:rows, :] = back[...].astype(F32)
+    wide[rows:, :] = jnp.zeros((ROWS, 128), F32)
     side = wide[side_rows(peers), :].reshape(peers, 1, 128)
     lane = lax.broadcasted_iota(jnp.int32, (peers, ROWS, 128), 2)
     own = lane % ROWS == lax.broadcasted_iota(jnp.int32, (peers, ROWS, 128), 1)
@@ -299,28 +315,16 @@
         mine = jnp.logical_and(own, lane // (3 * ROWS) == c)
         pieces = jnp.where(mine, side, 0.0).astype(BF).reshape(peers * ROWS, 128)
         z = jnp.dot(pieces, ones, preferred_element_type=F32)
-        z_back[c * peers : (c + 1) * peers] = z.reshape(peers, ROWS, 128)
-
-    def clear(i, _):
-        count[i] = 0
-        return 0
-
-    lax.fori_loop(0, peers, clear, 0, unroll=8)
-    for c in copies[:2]:
-        c.wait()
-
-    def fetch(j, _):
-        e = entry[j]
-        t = target[j]
-        rank = count[t]
-        count[t] = rank + 1
-        o_all[e] = wide[tile_rows(t, rank), :]
-        z_all[e] = z_back[rank * peers + t]
-        return 0
-
-    lax.fori_loop(0, entry.shape[0], fetch, 0, unroll=4)
+        z_back[c, :peers] = z.reshape(peers, ROWS, 128)
+    z_back[0, peers] = jnp.full((ROWS, 128), DEAD, F32)
+    copies[0].wait()
+
     for r in range(requests):
-        parts = [(o_home[r], z_home[r])] + [(o_all[r * 8 + b], z_all[r * 8 + b]) for b in range(8)]
+        parts = [(o_home[r], z_home[r])]
+        for b in range(8):
+            i = place[0, r * 8 + b]
+            peer, c = lax.shift_right_logical(i, 1), i & 1
+            parts.append((wide[tile_rows(peer, c), :], z_back[c, peer]))
         att[r * ROWS : (r + 1) * ROWS, :] = weigh(parts)[0]
     heads = ROWS // 2
     a = jnp.concatenate(
@@ -328,8 +332,8 @@
     )
     for i in range(out.shape[0]):
         if i >= early:
-            copies[2 + i - early].wait()
-        block = w_early[i] if i < early else w[i - early]
+            copies[1 + i - early].wait()
+        block = w_first[...] if i == 0 else w_early[i - 1] if i < early else w[i - early]
         out[i] = jnp.dot(a, block, preferred_element_type=F32).astype(BF)
 
 
@@ -403,12 +407,20 @@
     recv = exchange(send)
 
     tile_state = jax.ShapeDtypeStruct((requests, ROWS, size), F32)
-    o_home, z_home, kp = pl.pallas_call(
+    width = out_weight.shape[1] // parts
+    o_home, z_home, place, kp, w_first = pl.pallas_call(
         home_kernel,
-        out_shape=(tile_state, tile_state, like(k_hbm)),
-        in_specs=[HB] * 8,
-        out_specs=(VM, VM, VM),
+        out_shape=(
+            tile_state,
+            tile_state,
+            jax.ShapeDtypeStruct((1, 128), jnp.int32),
+            like(k_hbm),
+            jax.ShapeDtypeStruct((out_weight.shape[0], width), BF),
+        ),
+        in_specs=[HB] * 10,
+        out_specs=(VM, VM, VM, VM, VM),
         scratch_shapes=[
+            smem(lends),
             smem(lends),
             smem(*block_table.shape),
             smem(requests),
@@ -418,17 +430,17 @@
             pltpu.VMEM(v_hbm.shape, BF),
             pltpu.VMEM((entries, ROWS, size), F32),
             pltpu.VMEM((entries, ROWS, size), F32),
-            smem(entries),
+            smem(1, 128),
+            smem(peers),
             smem(entries + 1),
             scores,
-            sems(8),
+            sems(11),
         ],
         compiler_params=params(24),
         cost_estimate=pl.CostEstimate(flops=10**9, bytes_accessed=16 * 2**20, transcendentals=0),
-    )(*map(held, (lend_entry, block_table, lengths, q, nk, nv, k_hbm, v_hbm)))
-
-    width = out_weight.shape[1] // parts
-    early = 5
+    )(*map(held, (lend_entry, target, block_table, lengths, q, nk, nv, k_hbm, v_hbm, out_weight)))
+
+    early = 4
     back, w_early = pl.pallas_call(
         serve_kernel,
         out_shape=(
@@ -456,22 +468,18 @@
     partial = pl.pallas_call(
         merge_kernel,
         out_shape=jax.ShapeDtypeStruct((parts, requests * steps, out_weight.shape[1] // parts), BF),
-        in_specs=[HB] * 3 + [VM] * 4,
+        in_specs=[HB] + [VM] * 6,
         out_specs=VM,
         scratch_shapes=[
-            smem(lends),
-            smem(lends),
-            pltpu.VMEM((parts - early, out_weight.shape[0], width), BF),
-            wide,
-            pltpu.VMEM((entries, ROWS, size), F32),
-            pltpu.VMEM((entries, ROWS, size), F32),
-            pltpu.VMEM((CAP * peers, ROWS, 128), F32),
+            smem(1, 128),
+            pltpu.VMEM((parts - 1 - early, out_weight.shape[0], width), BF),
+            pltpu.VMEM((peers * SLAB + ROWS, size), F32),
+            pltpu.VMEM((CAP, peers + 1, ROWS, 128), F32),
             pltpu.VMEM((requests * ROWS, size), F32),
-            smem(peers),
-            sems(2 + parts - early),
+            sems(parts - early),
         ],
         compiler_params=params(24),
-    )(*map(held, (lend_entry, target, out_weight)), w_early, mine, o_home, z_home)
+    )(held(out_weight), w_first, w_early, mine, o_home, z_home, place)
 
     shares = lax.all_to_all(partial, "tp", split_axis=0, concat_axis=0, tiled=True)
 

time: 60.9 us -> 60.2 us (0.989)
  Pallas kernels: 12.4 us -> 11.6 us
  transfers between devices with their start and end apart: 1 -> 1, of which waited for: 1 -> 1; matrix products, arithmetic and copies ran while one was open for 0% -> 0% of each run, Pallas kernels for 6% -> 5%
where the time goes in v8:
time: 60.2 us; the launch traced here: 59.9 us
  blocking collectives  27.9 us (46%)
  starting transfers between devices  11.9 us (20%)
  Pallas kernels  11.6 us (19%)
  waiting for transfers between devices  8.02 us (13%)
    all_to_all x1, blocking collectives, exchange(): y = lax.all_to_all(y, 'inst', split_axis=0, concat_axis=0, tiled=True)  14.4 us
    all_to_all x1, blocking collectives, on_device(): lax.all_to_all(partial, 'tp', split_axis=0, concat_axis=0, tiled=True)  13.4 us
    all_to_all x1, starting transfers between devices, exchange(): y = lax.all_to_all(y, 'inst', split_axis=0, concat_axis=0, tiled=True)  11.9 us
    all_to_all x1, waiting for transfers between devices, exchange(): y = lax.all_to_all(y, 'inst', split_axis=0, concat_axis=0, tiled=True)  8.02 us
    pallas_call x1, Pallas kernels, on_device(): pl.pallas_call(serve_kernel, out_shape=(jax.ShapeDtypeStruct((peers * SLA...  3.29 us
    pallas_call x1, Pallas kernels, on_device(): pl.pallas_call(home_kernel, out_shape=(tile_state, tile_state, jax.ShapeD...  3.27 us
    pallas_call x1, Pallas kernels, on_device(): pl.pallas_call(merge_kernel, out_shape=jax.ShapeDtypeStruct((parts, reque...  2.33 us
    pallas_call x1, Pallas kernels, on_device(): pl.pallas_call(pack_kernel, out_shape=jax.ShapeDtypeStruct((peers * SLAB,...  2.08 us
  transfers between devices with their start and end apart: 1, of which 1 were waited for; matrix products, arithmetic and copies ran while one was open for 0% of the time, Pallas kernels for 5%

profile of v8, /device:TPU:1, one launch (start us, length us, event | category | flops | bytes accessed | tf_op | source)
XLA Modules:
  0.0 59.9 jit_solution(6949022695579190022)
XLA Ops:
  0.0 2.1 %shard_map.101 = bf16[1088,128]{1,0:T(8,128)(2,1)} custom-call(s32[32]{0:T(128)} %entry_h.3, s32[32]{0:T(128)} %bitcast.20, s32[8,8]{1,0:T(8,128)} %table_h.3, s32[8]{0:T(128)} %lengths_h.3, bf16[8,16,128]{2,1,0:T(8,128)(2,1)} %bitcast.16), custom_call_target="tpu_custom_call" | custom-call | tf_op jit(solution)/shard_map/pallas_call | solution.py:382
  2.1 11.9 %all-to-all-start = ((bf16[32,17,2,128]{3,2,1,0:T(2,128)(2,1)}), bf16[32,17,2,128]{3,2,1,0:T(2,128)(2,1)S(1)}, u32[]{:S(2)}, u32[]{:S(2)}) async-start(bf16[32,17,2,128]{3,2,1,0:T(2,128)(2,1)} %bitcast.6), calls=%async_computation | async-start | bytes 557056 | tf_op jit(solution)/shard_map/all_to_all | solution.py:404
  14.0 3.3 %shard_map.100 = (f32[8,16,128]{2,1,0:T(8,128)S(1)}, f32[8,16,128]{2,1,0:T(8,128)S(1)}, s32[1,128]{1,0:T(1,128)S(1)}, bf16[64,128,128]{2,1,0:T(8,128)(2,1)S(1)}, bf16[1024,512]{1,0:T(8,128)(2,1)S(1)}) custom-call(s32[32]{0:T(128)} %entry_h.3, s32[32]{0:T(128)} %bitcast.21, s32[8,8]{1,0:T(8,128)} %table_h.3, s32[8]{0:T(128)} %lengths_h.3, ...), custom_call_target="tpu_custom_call" | custom-call | flops 1000000000 | bytes 16777216 | tf_op jit(solution)/shard_map/pallas_call | solution.py:411
  17.2 0.0 copy-start
  17.3 0.5 copy-done
  17.8 8.0 %all-to-all-done = bf16[32,17,2,128]{3,2,1,0:T(2,128)(2,1)S(1)} async-done(((bf16[32,17,2,128]{3,2,1,0:T(2,128)(2,1)}), bf16[32,17,2,128]{3,2,1,0:T(2,128)(2,1)S(1)}, u32[]{:S(2)}, u32[]{:S(2)}) %all-to-all-start) | async-done | bytes 278560 | tf_op jit(solution)/shard_map/all_to_all | solution.py:404
  25.8 0.0 copy-start.1
  25.8 3.3 %shard_map.102 = (bf16[1088,128]{1,0:T(8,128)(2,1)S(1)}, bf16[4,1024,512]{2,1,0:T(8,128)(2,1)S(1)}) custom-call(bf16[64,128,128]{2,1,0:T(8,128)(2,1)} %bitcast.14, bf16[1024,4096]{1,0:T(8,128)(2,1)} %w_h.5, bf16[1088,128]{1,0:T(8,128)(2,1)S(1)} %bitcast.11, bf16[64,128,128]{2,1,0:T(8,128)(2,1)S(1)} %get-tuple-element.13.kp), custom_call_target="tpu_custom_call" | custom-call | tf_op jit(solution)/shard_map/pallas_call | solution.py:444
  29.1 14.4 %all_to_all.15 = bf16[32,17,2,128]{3,2,1,0:T(2,128)(2,1)S(1)} all-to-all(bf16[32,17,2,128]{3,2,1,0:T(2,128)(2,1)S(1)} %bitcast.12), channel_id=1, replica_groups=mesh['inst'=32,'tp'=8] {'inst'}, dimensions={0} | all-to-all | bytes 557056 | tf_op jit(solution)/shard_map/all_to_all | solution.py:404
  43.5 0.0 copy-done.1
  43.5 2.3 %shard_map.103 = bf16[8,16,512]{2,1,0:T(8,128)(2,1)S(1)} custom-call(bf16[1024,4096]{1,0:T(8,128)(2,1)} %w_h.5, bf16[1024,512]{1,0:T(8,128)(2,1)S(1)} %get-tuple-element.12.w_first, bf16[4,1024,512]{2,1,0:T(8,128)(2,1)S(1)} %get-tuple-element.14.w_early, bf16[1088,128]{1,0:T(8,128)(2,1)S(1)} %bitcast.10, f32[8,16,128]{2,1,0:T(8,128)S(1)} %get-tuple-element.16.o_home, ...), custom_call_target="tpu_custom_call" | custom-call | tf_op jit(solution)/shard_map/pallas_call | solution.py:468
  45.9 13.4 %all_to_all.16.parts = bf16[8,16,512]{2,1,0:T(8,128)(2,1)S(1)} all-to-all(bf16[8,16,512]{2,1,0:T(8,128)(2,1)S(1)} %shard_map.103), channel_id=1, replica_groups=mesh['inst'=32,'tp'=8] {'tp'}, dimensions={0} | all-to-all | bytes 262144 | tf_op jit(solution)/shard_map/all_to_all | solution.py:484
  59.3 0.6 %shard_map.104 = bf16[8,2,512]{2,1,0:T(2,128)(2,1)} custom-call(bf16[8,16,512]{2,1,0:T(8,128)(2,1)S(1)} %all_to_all.16.parts), custom_call_target="tpu_custom_call" | custom-call | tf_op jit(solution)/shard_map/pallas_call | solution.py:486
Async XLA Ops:
  2.1 23.7 %all-to-all-start = ((bf16[32,17,2,128]{3,2,1,0:T(2,128)(2,1)}), bf16[32,17,2,128]{3,2,1,0:T(2,128)(2,1)S(1)}, u32[]{:S(2)}, u32[]{:S(2)}) async-start(bf16[32,17,2,128]{3,2,1,0:T(2,128)(2,1)} %bitcast.6), calls=%async_computation | async-start | bytes 557056 | tf_op jit(solution)/shard_map/all_to_all | solution.py:404
  17.2 0.5 copy-start
  25.8 17.7 %copy-start.1 = (s32[1,128]{1,0:T(1,128)S(1)}, s32[1,128]{1,0:T(1,128)}, u32[]{:S(2)}) copy-start(s32[1,128]{1,0:T(1,128)} %copy-done) | copy-start | bytes 1540

commit v9 on v8

--- a/solution.py
+++ b/solution.py
@@ -30,20 +30,32 @@
     return copies
 
 
+MARGIN = 48
+
+
 def tile_rows(peer, rank):
     return pl.ds(peer * SLAB + rank * ROWS, ROWS)
 
 
 def side_rows(peers):
     return pl.ds(CAP * ROWS, peers, stride=SLAB)
+
+
+def note_last(target, latest):
+    for j in range(target.shape[0]):
+        latest[target[j]] = j
+
+
+def rank_of(j, t, latest):
+    return jnp.where(latest[t] == j, 0, 1)
 
 
 def pack_kernel(
     entry_h, target_h, table_h, lengths_h, q_h,
     send,
-    entry, target, table, lengths, q, wide, count, slots, lives, sems,
+    entry, target, table, lengths, q, wide, packed, latest, slots, lives, sems,
 ):
-    peers = count.shape[0]
+    peers = latest.shape[0]
     blocks = table.shape[1]
     small = fetch_all(
         [(entry_h, entry), (target_h, target), (table_h, table), (lengths_h, lengths), (q_h, q)],
@@ -51,23 +63,23 @@
     )
 
     def clear(i, _):
-        count[i] = 0
         for c in range(CAP):
             slots[i * CAP + c] = 0
             lives[i * CAP + c] = 0
         return 0
 
-    lax.fori_loop(0, peers, clear, 0, unroll=4)
+    lax.fori_loop(0, peers, clear, 0, unroll=8)
     for c in small:
         c.wait()
+
+    note_last(target, latest)
 
     def place(j, _):
         e = entry[j]
         t = target[j]
         r = e // blocks
         b = e % blocks
-        rank = count[t]
-        count[t] = rank + 1
+        rank = rank_of(j, t, latest)
         i = t * CAP + rank
         slots[i] = table[r, b]
         lives[i] = jnp.clip(lengths[r] - b * 128, 0, 128)
@@ -85,8 +97,17 @@
         wide[pl.ds(i * SLAB + CAP * ROWS, 2), :] = v.astype(F32)
         return 0
 
-    lax.fori_loop(0, peers, lay, 0, unroll=8)
-    send[...] = wide[...].astype(BF)
+    pieces = 4
+    size = peers * SLAB // pieces
+    copies = []
+    for k in range(pieces):
+        lax.fori_loop(k * peers // pieces, (k + 1) * peers // pieces, lay, 0, unroll=True)
+        rows = pl.ds(k * size, size)
+        packed[rows, :] = wide[rows, :].astype(BF)
+        copies.append(pltpu.make_async_copy(packed.at[rows, :], send.at[rows, :], sems.at[5 + k]))
+        copies[-1].start()
+    for c in copies:
+        c.wait()
 
 
 def attend(n, query, slot_of, live_of, store, kp, vp, scores, ready):
@@ -115,40 +136,44 @@
 
     ready()
 
-    def work(g, _):
+    def finish(g):
         now = lax.rem(g, 2)
-        held = [scores[now, i] for i in range(GROUP)]
-        later = score(jnp.minimum(g + 1, groups - 1))
         done = []
         for i in range(GROUP):
             item = jnp.minimum(g * GROUP + i, n - 1)
-            s = jnp.where(lane < live_of(item), held[i] * scale, DEAD)
+            s = jnp.where(lane < live_of(item), scores[now, i] * scale, DEAD)
             m = jnp.max(s, axis=1, keepdims=True)
             p = jnp.exp(s - m)
             l = jnp.sum(p, axis=1, keepdims=True)
             o = jnp.dot(p.astype(BF), vp[slot_of(item)], preferred_element_type=F32) / l
             done.append((item, o, jnp.broadcast_to(m + jnp.log(l), (ROWS, 128))))
-        for item, o, z in done:
+        return done
+
+    def work(g, _):
+        later = score(g + 1)
+        for item, o, z in finish(g):
             store(item, o, z)
         for i, s in enumerate(later):
-            scores[1 - now, i] = s
+            scores[lax.rem(g + 1, 2), i] = s
         return 0
 
-    lax.fori_loop(0, groups, work, 0)
+    lax.fori_loop(0, groups - 1, work, 0)
+
+    @pl.when(n > 0)
+    def _():
+        for item, o, z in finish(groups - 1):
+            store(item, o, z)
 
 
 def serve_kernel(
-    vp_h, w_h, recv, kp,
-    back, w,
+    vp_h, recv, kp,
+    back,
     vp, wide, side_i, side_s, ids, answer, lse, scores, sems,
 ):
     peers = side_i.shape[0]
     values = pltpu.make_async_copy(vp_h, vp, sems.at[1])
     values.start()
-    width = w.shape[2]
-    chunks = [(w_h.at[:, pl.ds((1 + i) * width, width)], w.at[i]) for i in range(w.shape[0])]
-    weights = fetch_all(chunks, sems.at[pl.ds(2, len(chunks))])
-    wide[...] = recv[...].astype(F32)
+    wide[: recv.shape[0], :] = recv[...].astype(F32)
     side_i[...] = wide[side_rows(peers), :].astype(jnp.int32)
     copy = pltpu.make_async_copy(side_i, side_s, sems.at[0])
     copy.start()
@@ -193,9 +218,7 @@
         rest = rest - part
         side = jnp.where(group % 3 == piece, part, side)
     answer[side_rows(peers), :] = side
-    back[...] = answer[...].astype(BF)
-    for c in weights:
-        c.wait()
+    back[...] = answer[: back.shape[0], :].astype(BF)
 
 
 def weigh(states):
@@ -207,20 +230,20 @@
 
 
 def home_kernel(
-    entry_h, target_h, table_h, lengths_h, q_h, nk_h, nv_h, kp_h, vp_h, w_h,
-    o_out, z_out, place_out, kp, w,
-    entry, target, table, lengths, q, nk, nv, vp, o_part, z_part, place, count, ids, scores, sems,
+    entry_h, target_h, table_h, lengths_h, q_h, nk_h, nv_h, kp_h, vp_h,
+    o_out, z_out, place_out, kp,
+    entry, target, table, lengths, q, nk, nv, vp, o_part, z_part, place, latest, ids, scores, sems,
 ):
     requests, blocks = table.shape
     entries = requests * blocks
     copies = fetch_all(
-        [(entry_h, entry), (target_h, target), (table_h, table), (lengths_h, lengths), (q_h, q), (nk_h, nk), (nv_h, nv), (kp_h, kp), (vp_h, vp), (w_h.at[:, pl.ds(0, w.shape[1])], w)],
+        [(entry_h, entry), (target_h, target), (table_h, table), (lengths_h, lengths), (q_h, q), (nk_h, nk), (nv_h, nv), (kp_h, kp), (vp_h, vp)],
         sems,
     )
     z_part[...] = jnp.full(z_part.shape, DEAD, F32)
     o_part[...] = jnp.zeros(o_part.shape, F32)
 
-    peers = count.shape[0]
+    peers = latest.shape[0]
     none = peers * CAP
 
     def clear(i, _):
@@ -229,23 +252,18 @@
 
     lax.fori_loop(0, entries, clear, 0, unroll=8)
 
-    def clear_count(i, _):
-        count[i] = 0
-        return 0
-
-    lax.fori_loop(0, peers, clear_count, 0, unroll=8)
     for c in copies[:7]:
         c.wait()
 
+    note_last(target, latest)
+
     def mark(j, _):
         t = target[j]
-        rank = count[t]
-        count[t] = rank + 1
-        place[0, entry[j]] = t * CAP + rank
+        place[0, entry[j]] = t * CAP + rank_of(j, t, latest)
         return 0
 
     lax.fori_loop(0, entry.shape[0], mark, 0, unroll=8)
-    placed = pltpu.make_async_copy(place, place_out, sems.at[10])
+    placed = pltpu.make_async_copy(place, place_out, sems.at[9])
     placed.start()
 
     def listing(e, n):
@@ -289,24 +307,22 @@
         o, top, total = weigh([fresh] + [(o_part[r * 8 + b], z_part[r * 8 + b]) for b in range(8)])
         o_out[r] = o
         z_out[r] = top + jnp.log(total)
-    copies[9].wait()
     placed.wait()
 
 
 def merge_kernel(
-    w_h, w_first, w_early, back, o_home, z_home, place_v,
+    w, back, o_home, z_home, place_v,
     out,
-    place, w, wide, z_back, att, sems,
+    place, wide, z_back, att, sems,
 ):
     requests = o_home.shape[0]
     peers = z_back.shape[1] - 1
     rows = peers * SLAB
     width = out.shape[2]
-    early = 1 + w_early.shape[0]
-    chunks = [(w_h.at[:, pl.ds((early + i) * width, width)], w.at[i]) for i in range(w.shape[0])]
-    copies = fetch_all([(place_v, place)] + chunks, sems)
+    copy = pltpu.make_async_copy(place_v, place, sems.at[0])
+    copy.start()
     wide[:rows, :] = back[...].astype(F32)
-    wide[rows:, :] = jnp.zeros((ROWS, 128), F32)
+    wide[rows:, :] = jnp.zeros((MARGIN, 128), F32)
     side = wide[side_rows(peers), :].reshape(peers, 1, 128)
     lane = lax.broadcasted_iota(jnp.int32, (peers, ROWS, 128), 2)
     own = lane % ROWS == lax.broadcasted_iota(jnp.int32, (peers, ROWS, 128), 1)
@@ -317,7 +333,7 @@
         z = jnp.dot(pieces, ones, preferred_element_type=F32)
         z_back[c, :peers] = z.reshape(peers, ROWS, 128)
     z_back[0, peers] = jnp.full((ROWS, 128), DEAD, F32)
-    copies[0].wait()
+    copy.wait()
 
     for r in range(requests):
         parts = [(o_home[r], z_home[r])]
@@ -331,9 +347,7 @@
         [att[pl.ds(g, 2 * requests, stride=heads), :].astype(BF) for g in range(heads)], axis=1
     )
     for i in range(out.shape[0]):
-        if i >= early:
-            copies[1 + i - early].wait()
-        block = w_first[...] if i == 0 else w_early[i - 1] if i < early else w[i - early]
+        block = w[:, i * width : (i + 1) * width]
         out[i] = jnp.dot(a, block, preferred_element_type=F32).astype(BF)
 
 
@@ -376,14 +390,14 @@
     smem = lambda *n: pltpu.SMEM(n, jnp.int32)
     sems = lambda n: pltpu.SemaphoreType.DMA((n,))
     like = lambda x: jax.ShapeDtypeStruct(x.shape, x.dtype)
-    wide = pltpu.VMEM((peers * SLAB, size), F32)
+    wide = pltpu.VMEM((peers * SLAB + MARGIN, size), F32)
     scores = pltpu.VMEM((2, GROUP, ROWS, 128), F32)
 
     send = pl.pallas_call(
         pack_kernel,
         out_shape=jax.ShapeDtypeStruct((peers * SLAB, size), BF),
         in_specs=[HB] * 5,
-        out_specs=VM,
+        out_specs=HB,
         scratch_shapes=[
             smem(lends),
             smem(lends),
@@ -391,10 +405,11 @@
             smem(requests),
             pltpu.VMEM(q.shape, BF),
             wide,
+            pltpu.VMEM((peers * SLAB, size), BF),
             smem(peers),
             smem(peers * CAP),
             smem(peers * CAP),
-            sems(5),
+            sems(9),
         ],
         compiler_params=params(16),
     )(*map(held, (lend_entry, target, block_table, lengths, q)))
@@ -407,18 +422,16 @@
     recv = exchange(send)
 
     tile_state = jax.ShapeDtypeStruct((requests, ROWS, size), F32)
-    width = out_weight.shape[1] // parts
-    o_home, z_home, place, kp, w_first = pl.pallas_call(
+    o_home, z_home, place, kp = pl.pallas_call(
         home_kernel,
         out_shape=(
             tile_state,
             tile_state,
             jax.ShapeDtypeStruct((1, 128), jnp.int32),
             like(k_hbm),
-            jax.ShapeDtypeStruct((out_weight.shape[0], width), BF),
         ),
-        in_specs=[HB] * 10,
-        out_specs=(VM, VM, VM, VM, VM),
+        in_specs=[HB] * 9,
+        out_specs=(VM, VM, VM, VM),
         scratch_shapes=[
             smem(lends),
             smem(lends),
@@ -434,21 +447,17 @@
             smem(peers),
             smem(entries + 1),
             scores,
-            sems(11),
+            sems(10),
         ],
         compiler_params=params(24),
         cost_estimate=pl.CostEstimate(flops=10**9, bytes_accessed=16 * 2**20, transcendentals=0),
-    )(*map(held, (lend_entry, target, block_table, lengths, q, nk, nv, k_hbm, v_hbm, out_weight)))
-
-    early = 4
-    back, w_early = pl.pallas_call(
+    )(*map(held, (lend_entry, target, block_table, lengths, q, nk, nv, k_hbm, v_hbm)))
+
+    back = pl.pallas_call(
         serve_kernel,
-        out_shape=(
-            jax.ShapeDtypeStruct((peers * SLAB, size), BF),
-            jax.ShapeDtypeStruct((early, out_weight.shape[0], width), BF),
-        ),
-        in_specs=[HB, HB, VM, VM],
-        out_specs=(VM, VM),
+        out_shape=jax.ShapeDtypeStruct((peers * SLAB, size), BF),
+        in_specs=[HB, VM, VM],
+        out_specs=VM,
         scratch_shapes=[
             pltpu.VMEM(v_hbm.shape, BF),
             wide,
@@ -456,30 +465,30 @@
             smem(peers, 128),
             smem(peers * CAP + 1),
             wide,
-            pltpu.VMEM((peers * CAP, 128), F32),
+            pltpu.VMEM((peers * CAP + MARGIN, 128), F32),
             scores,
-            sems(2 + early),
+            sems(2),
         ],
-        compiler_params=params(24),
-    )(held(v_hbm), held(out_weight), recv, kp)
+        compiler_params=params(16),
+        cost_estimate=pl.CostEstimate(flops=10000000000, bytes_accessed=16777216, transcendentals=0),
+    )(held(v_hbm), recv, kp)
 
     mine = exchange(back)
 
     partial = pl.pallas_call(
         merge_kernel,
         out_shape=jax.ShapeDtypeStruct((parts, requests * steps, out_weight.shape[1] // parts), BF),
-        in_specs=[HB] + [VM] * 6,
+        in_specs=[VM] * 5,
         out_specs=VM,
         scratch_shapes=[
             smem(1, 128),
-            pltpu.VMEM((parts - 1 - early, out_weight.shape[0], width), BF),
-            pltpu.VMEM((peers * SLAB + ROWS, size), F32),
+            wide,
             pltpu.VMEM((CAP, peers + 1, ROWS, 128), F32),
-            pltpu.VMEM((requests * ROWS, size), F32),
-            sems(parts - early),
+            pltpu.VMEM((requests * ROWS + MARGIN, size), F32),
+            sems(1),
         ],
         compiler_params=params(24),
-    )(held(out_weight), w_first, w_early, mine, o_home, z_home, place)
+    )(out_weight, mine, o_home, z_home, place)
 
     shares = lax.all_to_all(partial, "tp", split_axis=0, concat_axis=0, tiled=True)
 

time: 60.2 us -> 59.7 us (level)
  Pallas kernels: 11.6 us -> 10.4 us
  blocking collectives: 27.9 us -> 28.9 us
    pallas_call x1, Pallas kernels: 3.29 us -> 2.14 us  [on_device(): pl.pallas_call(serve_kernel, out_shape=jax.ShapeDtypeStruct((peers * SLAB...]
    all_to_all x1, blocking collectives: 14.4 us -> 15.4 us  [exchange(): y = lax.all_to_all(y, 'inst', split_axis=0, concat_axis=0, tiled=True)]
  transfers between devices with their start and end apart: 1 -> 1, of which waited for: 1 -> 1; matrix products, arithmetic and copies ran while one was open for 0% -> 0% of each run, Pallas kernels for 5% -> 6%
where the time goes in v9:
time: 59.7 us; the launch traced here: 59.3 us
  blocking collectives  28.9 us (48%)
  starting transfers between devices  11.9 us (20%)
  Pallas kernels  10.4 us (17%)
  waiting for transfers between devices  8.16 us (14%)
    all_to_all x1, blocking collectives, exchange(): y = lax.all_to_all(y, 'inst', split_axis=0, concat_axis=0, tiled=True)  15.4 us
    all_to_all x1, blocking collectives, on_device(): lax.all_to_all(partial, 'tp', split_axis=0, concat_axis=0, tiled=True)  13.5 us
    all_to_all x1, starting transfers between devices, exchange(): y = lax.all_to_all(y, 'inst', split_axis=0, concat_axis=0, tiled=True)  11.9 us
    all_to_all x1, waiting for transfers between devices, exchange(): y = lax.all_to_all(y, 'inst', split_axis=0, concat_axis=0, tiled=True)  8.16 us
    pallas_call x1, Pallas kernels, on_device(): pl.pallas_call(home_kernel, out_shape=(tile_state, tile_state, jax.ShapeD...  3.65 us
    pallas_call x1, Pallas kernels, on_device(): pl.pallas_call(serve_kernel, out_shape=jax.ShapeDtypeStruct((peers * SLAB...  2.14 us
    pallas_call x1, Pallas kernels, on_device(): pl.pallas_call(pack_kernel, out_shape=jax.ShapeDtypeStruct((peers * SLAB,...  2.01 us
    pallas_call x1, Pallas kernels, on_device(): pl.pallas_call(merge_kernel, out_shape=jax.ShapeDtypeStruct((parts, reque...  1.94 us
  transfers between devices with their start and end apart: 1, of which 1 were waited for; matrix products, arithmetic and copies ran while one was open for 0% of the time, Pallas kernels for 6%

profile of v9, /device:TPU:1, one launch (start us, length us, event | category | flops | bytes accessed | tf_op | source)
XLA Modules:
  0.0 59.3 jit_solution(5574736270937498996)
XLA Ops:
  0.0 2.0 %shard_map.100 = bf16[1088,128]{1,0:T(8,128)(2,1)} custom-call(s32[32]{0:T(128)} %entry_h.3, s32[32]{0:T(128)} %bitcast.22, s32[8,8]{1,0:T(8,128)} %table_h.3, s32[8]{0:T(128)} %lengths_h.3, bf16[8,16,128]{2,1,0:T(8,128)(2,1)} %bitcast.18), custom_call_target="tpu_custom_call" | custom-call | tf_op jit(solution)/shard_map/pallas_call | solution.py:396
  2.0 11.9 %all-to-all-start = ((bf16[32,17,2,128]{3,2,1,0:T(2,128)(2,1)}), bf16[32,17,2,128]{3,2,1,0:T(2,128)(2,1)S(1)}, u32[]{:S(2)}, u32[]{:S(2)}) async-start(bf16[32,17,2,128]{3,2,1,0:T(2,128)(2,1)} %bitcast.3), calls=%async_computation | async-start | bytes 557056 | tf_op jit(solution)/shard_map/all_to_all | solution.py:419
  13.9 3.6 %shard_map.101 = (f32[8,16,128]{2,1,0:T(8,128)S(1)}, f32[8,16,128]{2,1,0:T(8,128)S(1)}, s32[1,128]{1,0:T(1,128)S(1)}, bf16[64,128,128]{2,1,0:T(8,128)(2,1)S(1)}) custom-call(s32[32]{0:T(128)} %entry_h.3, s32[32]{0:T(128)} %bitcast.23, s32[8,8]{1,0:T(8,128)} %table_h.3, s32[8]{0:T(128)} %lengths_h.3, bf16[8,16,128]{2,1,0:T(8,128)(2,1)} %bitcast.19, ...), custom_call_target="tpu_custom_call" | custom-call | flops 1000000000 | bytes 16777216 | tf_op jit(solution)/shard_map/pallas_call | solution.py:425
  17.6 8.2 %all-to-all-done = bf16[32,17,2,128]{3,2,1,0:T(2,128)(2,1)S(1)} async-done(((bf16[32,17,2,128]{3,2,1,0:T(2,128)(2,1)}), bf16[32,17,2,128]{3,2,1,0:T(2,128)(2,1)S(1)}, u32[]{:S(2)}, u32[]{:S(2)}) %all-to-all-start) | async-done | bytes 278560 | tf_op jit(solution)/shard_map/all_to_all | solution.py:419
  25.7 0.0 slice-start
  25.7 0.0 slice-start.1
  25.7 2.1 %shard_map.102 = bf16[1088,128]{1,0:T(8,128)(2,1)S(1)} custom-call(bf16[64,128,128]{2,1,0:T(8,128)(2,1)} %bitcast.17, bf16[1088,128]{1,0:T(8,128)(2,1)S(1)} %bitcast.13, bf16[64,128,128]{2,1,0:T(8,128)(2,1)S(1)} %get-tuple-element.9.kp), custom_call_target="tpu_custom_call" | custom-call | flops 10000000000 | bytes 16777216 | tf_op jit(solution)/shard_map/pallas_call | solution.py:456
  27.9 15.4 %all_to_all.15 = bf16[32,17,2,128]{3,2,1,0:T(2,128)(2,1)S(1)} all-to-all(bf16[32,17,2,128]{3,2,1,0:T(2,128)(2,1)S(1)} %bitcast.14), channel_id=1, replica_groups=mesh['inst'=32,'tp'=8] {'inst'}, dimensions={0} | all-to-all | bytes 557056 | tf_op jit(solution)/shard_map/all_to_all | solution.py:419
  43.3 0.0 slice-done
  43.3 0.0 slice-done.1
  43.3 1.9 %shard_map.103 = bf16[8,16,512]{2,1,0:T(8,128)(2,1)S(1)} custom-call(bf16[1024,4096]{1,0:T(8,128)(2,1)S(1)} %bitcast.11, bf16[1088,128]{1,0:T(8,128)(2,1)S(1)} %bitcast.12, f32[8,16,128]{2,1,0:T(8,128)S(1)} %get-tuple-element.10.o_home, f32[8,16,128]{2,1,0:T(8,128)S(1)} %get-tuple-element.11.z_home, s32[1,128]{1,0:T(1,128)S(1)} %get-tuple-element.12.place_v), custom_call_target="tpu_custom_call" | custom-call | tf_op jit(solution)/shard_map/pallas_call | solution.py:478
  45.2 13.5 %all_to_all.16.parts = bf16[8,16,512]{2,1,0:T(8,128)(2,1)S(1)} all-to-all(bf16[8,16,512]{2,1,0:T(8,128)(2,1)S(1)} %shard_map.103), channel_id=1, replica_groups=mesh['inst'=32,'tp'=8] {'tp'}, dimensions={0} | all-to-all | bytes 262144 | tf_op jit(solution)/shard_map/all_to_all | solution.py:493
  58.7 0.6 %shard_map.104 = bf16[8,2,512]{2,1,0:T(2,128)(2,1)} custom-call(bf16[8,16,512]{2,1,0:T(8,128)(2,1)S(1)} %all_to_all.16.parts), custom_call_target="tpu_custom_call" | custom-call | tf_op jit(solution)/shard_map/pallas_call | solution.py:495
  (1 shorter events, 0.0 us)
Async XLA Ops:
  2.0 23.7 %all-to-all-start = ((bf16[32,17,2,128]{3,2,1,0:T(2,128)(2,1)}), bf16[32,17,2,128]{3,2,1,0:T(2,128)(2,1)S(1)}, u32[]{:S(2)}, u32[]{:S(2)}) async-start(bf16[32,17,2,128]{3,2,1,0:T(2,128)(2,1)} %bitcast.3), calls=%async_computation | async-start | bytes 557056 | tf_op jit(solution)/shard_map/all_to_all | solution.py:419
  25.7 17.5 %slice-start = ((s8[8388608]{0:T(1024)(128)(4,1)}), s8[4194304]{0:T(1024)(128)(4,1)S(1)}, s32[]{:S(2)}) async-start(s8[8388608]{0:T(1024)(128)(4,1)} %bitcast.10), calls=%async_computation.3 | async-start | bytes 8388608
  25.7 17.5 %slice-start.1 = ((s8[8388608]{0:T(1024)(128)(4,1)}), s8[4194304]{0:T(1024)(128)(4,1)S(1)}, s32[]{:S(2)}) async-start(s8[8388608]{0:T(1024)(128)(4,1)} %bitcast.10), calls=%async_computation.4 | async-start | bytes 8388608

commit v10 on v9

--- a/solution.py
+++ b/solution.py
@@ -9,7 +9,7 @@
 
 DEAD = -1e30
 CAP = 2
-GROUP = 16
+GROUP = 24
 ROWS = 16
 HALF = 8
 SLAB = CAP * ROWS + 2
@@ -117,16 +117,15 @@
 
     def score(g):
         out = []
-        for i in range(GROUP):
-            item = jnp.minimum(g * GROUP + i, n - 1)
-            out.append(
-                lax.dot_general(
-                    query(item),
-                    kp[slot_of(item)],
-                    (((1,), (1,)), ((), ())),
-                    preferred_element_type=F32,
-                )
+        for i in range(0, GROUP, 2):
+            pair = [jnp.minimum(g * GROUP + i + k, n - 1) for k in range(2)]
+            s = lax.dot_general(
+                jnp.concatenate([query(item) for item in pair], axis=0),
+                jnp.concatenate([kp[slot_of(item)] for item in pair], axis=0),
+                (((1,), (1,)), ((), ())),
+                preferred_element_type=F32,
             )
+            out += [s[:ROWS, :128], s[ROWS:, 128:]]
         return out
 
     @pl.when(n > 0)
@@ -139,14 +138,32 @@
     def finish(g):
         now = lax.rem(g, 2)
         done = []
-        for i in range(GROUP):
-            item = jnp.minimum(g * GROUP + i, n - 1)
-            s = jnp.where(lane < live_of(item), scores[now, i] * scale, DEAD)
-            m = jnp.max(s, axis=1, keepdims=True)
-            p = jnp.exp(s - m)
-            l = jnp.sum(p, axis=1, keepdims=True)
-            o = jnp.dot(p.astype(BF), vp[slot_of(item)], preferred_element_type=F32) / l
-            done.append((item, o, jnp.broadcast_to(m + jnp.log(l), (ROWS, 128))))
+        for i in range(0, GROUP, 2):
+            pair = [jnp.minimum(g * GROUP + i + k, n - 1) for k in range(2)]
+            weights, totals, ends = [], [], []
+            for k, item in enumerate(pair):
+                s = jnp.where(lane < live_of(item), scores[now, i + k] * scale, DEAD)
+                m = jnp.max(s, axis=1, keepdims=True)
+                p = jnp.exp(s - m)
+                l = jnp.sum(p, axis=1, keepdims=True)
+                weights.append(p.astype(BF))
+                totals.append(l)
+                ends.append(jnp.broadcast_to(m + jnp.log(l), (ROWS, 128)))
+            nil = jnp.zeros((ROWS, 128), BF)
+            o = jnp.dot(
+                jnp.concatenate(
+                    [
+                        jnp.concatenate([weights[0], nil], axis=1),
+                        jnp.concatenate([nil, weights[1]], axis=1),
+                    ],
+                    axis=0,
+                ),
+                jnp.concatenate([vp[slot_of(item)] for item in pair], axis=0),
+                preferred_element_type=F32,
+            )
+            parts = [o[:ROWS], o[ROWS:]]
+            for k, item in enumerate(pair):
+                done.append((item, parts[k] / totals[k], ends[k]))
         return done
 
     def work(g, _):

time: 59.7 us -> 59.3 us (level)
  transfers between devices with their start and end apart: 1 -> 1, of which waited for: 1 -> 1; matrix products, arithmetic and copies ran while one was open for 0% -> 0% of each run, Pallas kernels for 6% -> 5%
where the time goes in v10:
time: 59.3 us; the launch traced here: 59.1 us
  blocking collectives  28.5 us (48%)
  starting transfers between devices  11.9 us (20%)
  Pallas kernels  9.89 us (17%)
  waiting for transfers between devices  8.7 us (15%)
    all_to_all x1, blocking collectives, exchange(): y = lax.all_to_all(y, 'inst', split_axis=0, concat_axis=0, tiled=True)  15.1 us
    all_to_all x1, blocking collectives, on_device(): lax.all_to_all(partial, 'tp', split_axis=0, concat_axis=0, tiled=True)  13.4 us
    all_to_all x1, starting transfers between devices, exchange(): y = lax.all_to_all(y, 'inst', split_axis=0, concat_axis=0, tiled=True)  11.9 us
    all_to_all x1, waiting for transfers between devices, exchange(): y = lax.all_to_all(y, 'inst', split_axis=0, concat_axis=0, tiled=True)  8.7 us
    pallas_call x1, Pallas kernels, on_device(): pl.pallas_call(home_kernel, out_shape=(tile_state, tile_state, jax.ShapeD...  3.11 us
    pallas_call x1, Pallas kernels, on_device(): pl.pallas_call(serve_kernel, out_shape=jax.ShapeDtypeStruct((peers * SLAB...  2.19 us
    pallas_call x1, Pallas kernels, on_device(): pl.pallas_call(pack_kernel, out_shape=jax.ShapeDtypeStruct((peers * SLAB,...  2.01 us
    pallas_call x1, Pallas kernels, on_device(): pl.pallas_call(merge_kernel, out_shape=jax.ShapeDtypeStruct((parts, reque...  1.94 us
  transfers between devices with their start and end apart: 1, of which 1 were waited for; matrix products, arithmetic and copies ran while one was open for 0% of the time, Pallas kernels for 5%

profile of v10, /device:TPU:1, one launch (start us, length us, event | category | flops | bytes accessed | tf_op | source)
XLA Modules:
  0.0 59.1 jit_solution(14597739003544309077)
XLA Ops:
  0.0 2.0 %shard_map.100 = bf16[1088,128]{1,0:T(8,128)(2,1)} custom-call(s32[32]{0:T(128)} %entry_h.3, s32[32]{0:T(128)} %bitcast.22, s32[8,8]{1,0:T(8,128)} %table_h.3, s32[8]{0:T(128)} %lengths_h.3, bf16[8,16,128]{2,1,0:T(8,128)(2,1)} %bitcast.18), custom_call_target="tpu_custom_call" | custom-call | tf_op jit(solution)/shard_map/pallas_call | solution.py:413
  2.0 11.9 %all-to-all-start = ((bf16[32,17,2,128]{3,2,1,0:T(2,128)(2,1)}), bf16[32,17,2,128]{3,2,1,0:T(2,128)(2,1)S(1)}, u32[]{:S(2)}, u32[]{:S(2)}) async-start(bf16[32,17,2,128]{3,2,1,0:T(2,128)(2,1)} %bitcast.3), calls=%async_computation | async-start | bytes 557056 | tf_op jit(solution)/shard_map/all_to_all | solution.py:436
  13.9 3.1 %shard_map.101 = (f32[8,16,128]{2,1,0:T(8,128)S(1)}, f32[8,16,128]{2,1,0:T(8,128)S(1)}, s32[1,128]{1,0:T(1,128)S(1)}, bf16[64,128,128]{2,1,0:T(8,128)(2,1)S(1)}) custom-call(s32[32]{0:T(128)} %entry_h.3, s32[32]{0:T(128)} %bitcast.23, s32[8,8]{1,0:T(8,128)} %table_h.3, s32[8]{0:T(128)} %lengths_h.3, bf16[8,16,128]{2,1,0:T(8,128)(2,1)} %bitcast.19, ...), custom_call_target="tpu_custom_call" | custom-call | flops 1000000000 | bytes 16777216 | tf_op jit(solution)/shard_map/pallas_call | solution.py:442
  17.0 8.7 %all-to-all-done = bf16[32,17,2,128]{3,2,1,0:T(2,128)(2,1)S(1)} async-done(((bf16[32,17,2,128]{3,2,1,0:T(2,128)(2,1)}), bf16[32,17,2,128]{3,2,1,0:T(2,128)(2,1)S(1)}, u32[]{:S(2)}, u32[]{:S(2)}) %all-to-all-start) | async-done | bytes 278560 | tf_op jit(solution)/shard_map/all_to_all | solution.py:436
  25.7 0.0 slice-start
  25.7 0.0 slice-start.1
  25.7 2.2 %shard_map.102 = bf16[1088,128]{1,0:T(8,128)(2,1)S(1)} custom-call(bf16[64,128,128]{2,1,0:T(8,128)(2,1)} %bitcast.17, bf16[1088,128]{1,0:T(8,128)(2,1)S(1)} %bitcast.13, bf16[64,128,128]{2,1,0:T(8,128)(2,1)S(1)} %get-tuple-element.9.kp), custom_call_target="tpu_custom_call" | custom-call | flops 10000000000 | bytes 16777216 | tf_op jit(solution)/shard_map/pallas_call | solution.py:473
  27.9 15.1 %all_to_all.15 = bf16[32,17,2,128]{3,2,1,0:T(2,128)(2,1)S(1)} all-to-all(bf16[32,17,2,128]{3,2,1,0:T(2,128)(2,1)S(1)} %bitcast.14), channel_id=1, replica_groups=mesh['inst'=32,'tp'=8] {'inst'}, dimensions={0} | all-to-all | bytes 557056 | tf_op jit(solution)/shard_map/all_to_all | solution.py:436
  43.0 0.0 slice-done
  43.0 0.0 slice-done.1
  43.0 1.9 %shard_map.103 = bf16[8,16,512]{2,1,0:T(8,128)(2,1)S(1)} custom-call(bf16[1024,4096]{1,0:T(8,128)(2,1)S(1)} %bitcast.11, bf16[1088,128]{1,0:T(8,128)(2,1)S(1)} %bitcast.12, f32[8,16,128]{2,1,0:T(8,128)S(1)} %get-tuple-element.10.o_home, f32[8,16,128]{2,1,0:T(8,128)S(1)} %get-tuple-element.11.z_home, s32[1,128]{1,0:T(1,128)S(1)} %get-tuple-element.12.place_v), custom_call_target="tpu_custom_call" | custom-call | tf_op jit(solution)/shard_map/pallas_call | solution.py:495
  45.0 13.4 %all_to_all.16.parts = bf16[8,16,512]{2,1,0:T(8,128)(2,1)S(1)} all-to-all(bf16[8,16,512]{2,1,0:T(8,128)(2,1)S(1)} %shard_map.103), channel_id=1, replica_groups=mesh['inst'=32,'tp'=8] {'tp'}, dimensions={0} | all-to-all | bytes 262144 | tf_op jit(solution)/shard_map/all_to_all | solution.py:510
  58.4 0.6 %shard_map.104 = bf16[8,2,512]{2,1,0:T(2,128)(2,1)} custom-call(bf16[8,16,512]{2,1,0:T(8,128)(2,1)S(1)} %all_to_all.16.parts), custom_call_target="tpu_custom_call" | custom-call | tf_op jit(solution)/shard_map/pallas_call | solution.py:512
  (1 shorter events, 0.0 us)
Async XLA Ops:
  2.0 23.7 %all-to-all-start = ((bf16[32,17,2,128]{3,2,1,0:T(2,128)(2,1)}), bf16[32,17,2,128]{3,2,1,0:T(2,128)(2,1)S(1)}, u32[]{:S(2)}, u32[]{:S(2)}) async-start(bf16[32,17,2,128]{3,2,1,0:T(2,128)(2,1)} %bitcast.3), calls=%async_computation | async-start | bytes 557056 | tf_op jit(solution)/shard_map/all_to_all | solution.py:436
  25.7 17.3 %slice-start = ((s8[8388608]{0:T(1024)(128)(4,1)}), s8[4194304]{0:T(1024)(128)(4,1)S(1)}, s32[]{:S(2)}) async-start(s8[8388608]{0:T(1024)(128)(4,1)} %bitcast.10), calls=%async_computation.3 | async-start | bytes 8388608
  25.7 17.3 %slice-start.1 = ((s8[8388608]{0:T(1024)(128)(4,1)}), s8[4194304]{0:T(1024)(128)(4,1)S(1)}, s32[]{:S(2)}) async-start(s8[8388608]{0:T(1024)(128)(4,1)} %bitcast.10), calls=%async_computation.4 | async-start | bytes 8388608

commit v11 on v10

--- a/solution.py
+++ b/solution.py
@@ -41,6 +41,10 @@
     return pl.ds(CAP * ROWS, peers, stride=SLAB)
 
 
+def split(entry):
+    return lax.shift_right_logical(entry, 3), entry & 7
+
+
 def note_last(target, latest):
     for j in range(target.shape[0]):
         latest[target[j]] = j
@@ -56,7 +60,6 @@
     entry, target, table, lengths, q, wide, packed, latest, slots, lives, sems,
 ):
     peers = latest.shape[0]
-    blocks = table.shape[1]
     small = fetch_all(
         [(entry_h, entry), (target_h, target), (table_h, table), (lengths_h, lengths), (q_h, q)],
         sems,
@@ -77,8 +80,7 @@
     def place(j, _):
         e = entry[j]
         t = target[j]
-        r = e // blocks
-        b = e % blocks
+        r, b = split(e)
         rank = rank_of(j, t, latest)
         i = t * CAP + rank
         slots[i] = table[r, b]
@@ -285,21 +287,22 @@
 
     def listing(e, n):
         ids[n] = e
-        alive = lengths[e // blocks] > (e % blocks) * 128
+        r, b = split(e)
+        alive = lengths[r] > b * 128
         return n + jnp.where(jnp.logical_and(alive, place[0, e] == none), 1, 0)
 
     n = lax.fori_loop(0, entries, listing, 0, unroll=4)
 
     def query(item):
-        return q[ids[item] // blocks]
+        return q[split(ids[item])[0]]
 
     def slot_of(item):
-        e = ids[item]
-        return table[e // blocks, e % blocks]
+        r, b = split(ids[item])
+        return table[r, b]
 
     def live_of(item):
-        e = ids[item]
-        return lengths[e // blocks] - (e % blocks) * 128
+        r, b = split(ids[item])
+        return lengths[r] - b * 128
 
     def store(item, o, z):
         o_part[ids[item]] = o

time: 59.3 us -> 59.4 us (level)
  no operation moved by 1% of the time
where the time goes in v11:
time: 59.4 us
  blocking collectives  29 us (49%)
  starting transfers between devices  11.9 us (20%)
  Pallas kernels  9.65 us (16%)
  waiting for transfers between devices  8.8 us (15%)
    all_to_all x1, blocking collectives, exchange(): y = lax.all_to_all(y, 'inst', split_axis=0, concat_axis=0, tiled=True)  15.6 us
    all_to_all x1, blocking collectives, on_device(): lax.all_to_all(partial, 'tp', split_axis=0, concat_axis=0, tiled=True)  13.4 us
    all_to_all x1, starting transfers between devices, exchange(): y = lax.all_to_all(y, 'inst', split_axis=0, concat_axis=0, tiled=True)  11.9 us
    all_to_all x1, waiting for transfers between devices, exchange(): y = lax.all_to_all(y, 'inst', split_axis=0, concat_axis=0, tiled=True)  8.8 us
    pallas_call x1, Pallas kernels, on_device(): pl.pallas_call(home_kernel, out_shape=(tile_state, tile_state, jax.ShapeD...  3.01 us
    pallas_call x1, Pallas kernels, on_device(): pl.pallas_call(serve_kernel, out_shape=jax.ShapeDtypeStruct((peers * SLAB...  2.19 us
    pallas_call x1, Pallas kernels, on_device(): pl.pallas_call(merge_kernel, out_shape=jax.ShapeDtypeStruct((parts, reque...  1.94 us
    pallas_call x1, Pallas kernels, on_device(): pl.pallas_call(pack_kernel, out_shape=jax.ShapeDtypeStruct((peers * SLAB,...  1.87 us
  transfers between devices with their start and end apart: 1, of which 1 were waited for; matrix products, arithmetic and copies ran while one was open for 0% of the time, Pallas kernels for 5%

profile of v11, /device:TPU:1, one launch (start us, length us, event | category | flops | bytes accessed | tf_op | source)
XLA Modules:
  0.0 59.4 jit_solution(2654040621967518575)
XLA Ops:
  0.0 1.9 %shard_map.100 = bf16[1088,128]{1,0:T(8,128)(2,1)} custom-call(s32[32]{0:T(128)} %entry_h.3, s32[32]{0:T(128)} %bitcast.22, s32[8,8]{1,0:T(8,128)} %table_h.3, s32[8]{0:T(128)} %lengths_h.3, bf16[8,16,128]{2,1,0:T(8,128)(2,1)} %bitcast.18), custom_call_target="tpu_custom_call" | custom-call | tf_op jit(solution)/shard_map/pallas_call | solution.py:416
  1.9 11.9 %all-to-all-start = ((bf16[32,17,2,128]{3,2,1,0:T(2,128)(2,1)}), bf16[32,17,2,128]{3,2,1,0:T(2,128)(2,1)S(1)}, u32[]{:S(2)}, u32[]{:S(2)}) async-start(bf16[32,17,2,128]{3,2,1,0:T(2,128)(2,1)} %bitcast.3), calls=%async_computation | async-start | bytes 557056 | tf_op jit(solution)/shard_map/all_to_all | solution.py:439
  13.8 3.0 %shard_map.101 = (f32[8,16,128]{2,1,0:T(8,128)S(1)}, f32[8,16,128]{2,1,0:T(8,128)S(1)}, s32[1,128]{1,0:T(1,128)S(1)}, bf16[64,128,128]{2,1,0:T(8,128)(2,1)S(1)}) custom-call(s32[32]{0:T(128)} %entry_h.3, s32[32]{0:T(128)} %bitcast.23, s32[8,8]{1,0:T(8,128)} %table_h.3, s32[8]{0:T(128)} %lengths_h.3, bf16[8,16,128]{2,1,0:T(8,128)(2,1)} %bitcast.19, ...), custom_call_target="tpu_custom_call" | custom-call | flops 1000000000 | bytes 16777216 | tf_op jit(solution)/shard_map/pallas_call | solution.py:445
  16.8 8.8 %all-to-all-done = bf16[32,17,2,128]{3,2,1,0:T(2,128)(2,1)S(1)} async-done(((bf16[32,17,2,128]{3,2,1,0:T(2,128)(2,1)}), bf16[32,17,2,128]{3,2,1,0:T(2,128)(2,1)S(1)}, u32[]{:S(2)}, u32[]{:S(2)}) %all-to-all-start) | async-done | bytes 278560 | tf_op jit(solution)/shard_map/all_to_all | solution.py:439
  25.6 0.0 slice-start
  25.6 0.0 slice-start.1
  25.6 2.2 %shard_map.102 = bf16[1088,128]{1,0:T(8,128)(2,1)S(1)} custom-call(bf16[64,128,128]{2,1,0:T(8,128)(2,1)} %bitcast.17, bf16[1088,128]{1,0:T(8,128)(2,1)S(1)} %bitcast.13, bf16[64,128,128]{2,1,0:T(8,128)(2,1)S(1)} %get-tuple-element.9.kp), custom_call_target="tpu_custom_call" | custom-call | flops 10000000000 | bytes 16777216 | tf_op jit(solution)/shard_map/pallas_call | solution.py:476
  27.8 15.6 %all_to_all.15 = bf16[32,17,2,128]{3,2,1,0:T(2,128)(2,1)S(1)} all-to-all(bf16[32,17,2,128]{3,2,1,0:T(2,128)(2,1)S(1)} %bitcast.14), channel_id=1, replica_groups=mesh['inst'=32,'tp'=8] {'inst'}, dimensions={0} | all-to-all | bytes 557056 | tf_op jit(solution)/shard_map/all_to_all | solution.py:439
  43.4 0.0 slice-done
  43.4 0.0 slice-done.1
  43.4 1.9 %shard_map.103 = bf16[8,16,512]{2,1,0:T(8,128)(2,1)S(1)} custom-call(bf16[1024,4096]{1,0:T(8,128)(2,1)S(1)} %bitcast.11, bf16[1088,128]{1,0:T(8,128)(2,1)S(1)} %bitcast.12, f32[8,16,128]{2,1,0:T(8,128)S(1)} %get-tuple-element.10.o_home, f32[8,16,128]{2,1,0:T(8,128)S(1)} %get-tuple-element.11.z_home, s32[1,128]{1,0:T(1,128)S(1)} %get-tuple-element.12.place_v), custom_call_target="tpu_custom_call" | custom-call | tf_op jit(solution)/shard_map/pallas_call | solution.py:498
  45.3 13.4 %all_to_all.16.parts = bf16[8,16,512]{2,1,0:T(8,128)(2,1)S(1)} all-to-all(bf16[8,16,512]{2,1,0:T(8,128)(2,1)S(1)} %shard_map.103), channel_id=1, replica_groups=mesh['inst'=32,'tp'=8] {'tp'}, dimensions={0} | all-to-all | bytes 262144 | tf_op jit(solution)/shard_map/all_to_all | solution.py:513
  58.7 0.6 %shard_map.104 = bf16[8,2,512]{2,1,0:T(2,128)(2,1)} custom-call(bf16[8,16,512]{2,1,0:T(8,128)(2,1)S(1)} %all_to_all.16.parts), custom_call_target="tpu_custom_call" | custom-call | tf_op jit(solution)/shard_map/pallas_call | solution.py:515
  (1 shorter events, 0.0 us)
Async XLA Ops:
  1.9 23.7 %all-to-all-start = ((bf16[32,17,2,128]{3,2,1,0:T(2,128)(2,1)}), bf16[32,17,2,128]{3,2,1,0:T(2,128)(2,1)S(1)}, u32[]{:S(2)}, u32[]{:S(2)}) async-start(bf16[32,17,2,128]{3,2,1,0:T(2,128)(2,1)} %bitcast.3), calls=%async_computation | async-start | bytes 557056 | tf_op jit(solution)/shard_map/all_to_all | solution.py:439
  25.6 17.8 %slice-start = ((s8[8388608]{0:T(1024)(128)(4,1)}), s8[4194304]{0:T(1024)(128)(4,1)S(1)}, s32[]{:S(2)}) async-start(s8[8388608]{0:T(1024)(128)(4,1)} %bitcast.10), calls=%async_computation.3 | async-start | bytes 8388608
  25.6 17.8 %slice-start.1 = ((s8[8388608]{0:T(1024)(128)(4,1)}), s8[4194304]{0:T(1024)(128)(4,1)S(1)}, s32[]{:S(2)}) async-start(s8[8388608]{0:T(1024)(128)(4,1)} %bitcast.10), calls=%async_computation.4 | async-start | bytes 8388608
